TPU v7x, 256 devices: a whole 4x4x8 slice. The times are simulated.
256 devices in a mesh: band: 8 (over y, core), sector: 32 (over x, z).
Axes of the slice: x: 4, y: 4, z: 8, core: 2. Of those that a mesh axis runs over, the one named last changes fastest.
Arguments:
- blocks: float32 [8, 32, 12, 24, 1024], P('band', 'sector'), may hold values from -64 to 64, as said below
- connectivity: int32 [8, 32, 8, 1024], P('band', 'sector'), may hold values from 0 to 2047, as said below
- send_lists: int32 [8, 32, 4, 256], P('band', 'sector'), may hold values from 0 to 1023, as said below
- nodal_loads: float32 [8, 32, 3, 1024], P('band', 'sector'), may hold values from -48 to 48
- step_scale: float32 [1], replicated, may hold values from 0.5 to 0.9
Outputs:
- velocities: float32 [8, 32, 3, 1024], P('band', 'sector')
- multipliers: float32 [8, 32, 12, 1024], P('band', 'sector')
Inputs may be any that keep to these rules, and one draw needn't show every extreme that they name: `connectivity`: indices into the device's extended list of 2048 nodes. Row 0 is a permutation of the 1024 owned nodes; rows 1 and 2 together are a permutation of the whole extended list. `send_lists`: the four lists of a device together are a permutation of its 1024 owned nodes. `blocks`: every entry has magnitude 0.2 or more.
All inputs are finite; a program needn't handle non-finite values.
Results may differ from a plain program's by a relative error of at most 0.0003.
Values sent between devices are 32-bit elements; how exact they have to be, the bound alone decides.
No kernel may reach another device: no remote copies, remote signals or barrier semaphores. Data moves between devices by JAX's collectives and lax.ppermute only.
A program may use at most 128 MiB of HBM per device.

v0:
```python
import functools

import jax
import jax.numpy as jnp
from jax import lax
from jax.experimental import pallas as pl
from jax.experimental.pallas import tpu as pltpu
from jax.sharding import PartitionSpec as P

LANES = 128
CHUNKS = 8
STRAINS = 12
NODE_ROWS = 16
ITEM_ROWS = 64
SIDES = 4
AXES = ("band", "sector")
epsilon = 1e-06
F32 = jnp.float32
I32 = jnp.int32


def tile_iota(axis):
    return lax.broadcasted_iota(I32, (8, LANES), axis)


def pick(rows, index, axis):
    dims = lax.GatherDimensionNumbers(
        offset_dims=(),
        collapsed_slice_dims=(axis,),
        start_index_map=(axis,),
        operand_batching_dims=(1 - axis,),
        start_indices_batching_dims=(1 - axis,),
    )
    return lax.gather(
        rows,
        index[..., None],
        dims,
        slice_sizes=(1, 1),
        mode=lax.GatherScatterMode.PROMISE_IN_BOUNDS,
    )


def table_picks(row_getters, count, flat):
    lanes = flat & (LANES - 1)
    levels = count.bit_length() - 1
    bits = [(flat & (LANES << level)) != 0 for level in range(levels)]

    def descend(row_at, level, base):
        if level < 0:
            return pick(jnp.broadcast_to(row_at(base), (8, LANES)), lanes, 1)
        low = descend(row_at, level - 1, base)
        high = descend(row_at, level - 1, base + (1 << level))
        return jnp.where(bits[level], high, low)

    return [descend(row_at, levels - 1, 0) for row_at in row_getters]


def rows_of(ref, offset):
    return lambda row: ref[offset + row : offset + row + 1, :]


def chunk_at(chunk):
    return pl.ds(pl.multiple_of(chunk * LANES, LANES), LANES)


def eight_at(chunk, offset=0):
    return pl.ds(pl.multiple_of(offset + chunk * 8, 8), 8)


def group_shift(values, distance):
    if distance >= 8:
        return pltpu.roll(values, distance // 8, 1)
    turned = pltpu.roll(values, distance, 0)
    return jnp.where(tile_iota(0) < distance, pltpu.roll(turned, 1, 1), turned)


SCAN_STEPS = tuple(1 << step for step in range(10))


def sort_items(keys):
    sub, lane = tile_iota(0), tile_iota(1)
    size = 2
    while size <= 8192:
        half = size // 2
        while half >= 1:
            new = list(keys)

            def rising(register):
                if size < 8:
                    return (register & size) == 0
                if size < 64:
                    return (sub & (size // 8)) == 0
                if size < 8192:
                    return (lane & (size // 64)) == 0
                return True

            for register in range(8):
                up = rising(register)
                if half < 8:
                    other = register ^ half
                    if other < register:
                        continue
                    low = jnp.minimum(keys[register], keys[other])
                    high = jnp.maximum(keys[register], keys[other])
                    if isinstance(up, bool):
                        new[register], new[other] = (low, high) if up else (high, low)
                    else:
                        new[register] = jnp.where(up, low, high)
                        new[other] = jnp.where(up, high, low)
                    continue
                if half < 64:
                    step = half // 8
                    partner = pick(keys[register], sub ^ step, 0)
                    first = (sub & step) == 0
                else:
                    step = half // 64
                    partner = pick(keys[register], lane ^ step, 1)
                    first = (lane & step) == 0
                low = jnp.minimum(keys[register], partner)
                high = jnp.maximum(keys[register], partner)
                if isinstance(up, bool):
                    keep_low = first if up else jnp.logical_not(first)
                else:
                    keep_low = first == up
                new[register] = jnp.where(keep_low, low, high)
            keys = new
            half //= 2
        size *= 2
    return keys


def make_plan(conn_ref, send_ref, conn_out, key_out, scan_out, end_out, inverse_out, send_scratch):
    for half in range(8):
        start = (half % 2) * LANES
        send_scratch[half : half + 1, :] = send_ref[0, 0, half // 2 : half // 2 + 1, start : start + LANES]
    send_line = jnp.concatenate([send_scratch[row : row + 1, :] for row in range(8)], axis=1)
    place = lax.broadcasted_iota(I32, (8, 8 * LANES), 1)
    in_row = (send_line >> 7) == lax.broadcasted_iota(I32, (8, 8 * LANES), 0)
    left = jnp.concatenate(
        [
            jnp.where(in_row, (place >> 5).astype(F32), 0.0),
            jnp.where(in_row, (place & 31).astype(F32), 0.0),
        ],
        axis=0,
    ).astype(jnp.bfloat16)
    in_lane = (send_line & (LANES - 1)) == lax.broadcasted_iota(I32, (LANES, 8 * LANES), 0)
    right = jnp.where(in_lane, 1.0, 0.0).astype(jnp.bfloat16)
    found = lax.dot_general(left, right, (((1,), (1,)), ((), ())), preferred_element_type=F32)
    inverse_out[...] = (found[0:8] * 32.0 + found[8:16]).astype(I32)
    sub, lane = tile_iota(0), tile_iota(1)
    keys = []
    for chunk in range(CHUNKS):
        ids = conn_ref[0, 0, :, chunk * LANES : (chunk + 1) * LANES]
        (label,) = table_picks([rows_of(inverse_out, 0)], 8, ids & 1023)
        ids = jnp.where(ids < 1024, label, ids)
        conn_out[8 * chunk : 8 * chunk + 8, :] = ids
        keys.append(ids * 8192 + (chunk * 1024 + sub * LANES + lane))
    keys = sort_items(keys)
    for register in range(8):
        key_out[8 * register : 8 * register + 8, :] = keys[register]
    first, last = keys[0] >> 13, keys[7] >> 13
    group = lane * 8 + sub
    scan = jnp.zeros((8, LANES), I32)
    for step, distance in enumerate(SCAN_STEPS):
        same = (group >= distance) & (group_shift(last, distance) == last)
        scan = jnp.where(same, scan | (1 << step), scan)
    same = (group >= 1) & (group_shift(last, 1) == first)
    scan_out[...] = jnp.where(same, scan | (1 << len(SCAN_STEPS)), scan)
    lane_last = jnp.broadcast_to(key_out[63:64, :] >> 13, (8, LANES))
    for half in range(2):
        node = (half * 8 + sub) * LANES + lane
        column = jnp.zeros((8, LANES), I32)
        for step in (64, 32, 16, 8, 4, 2, 1):
            seen = pick(lane_last, column + (step - 1), 1)
            column = jnp.where(seen <= node, column + step, column)
        count = column * 64
        for row in range(ITEM_ROWS):
            seen = pick(jnp.broadcast_to(key_out[row : row + 1, :], (8, LANES)), column, 1)
            count = count + jnp.where((seen >> 13) <= node, 1, 0)
        place = count - 1
        row = (place & 7) * 8 + ((place >> 3) & 7)
        end_out[8 * half : 8 * half + 8, :] = row * LANES + (place >> 6)


def scatter_items(term_ref, channels, plan, sorted_ref, out_ref, merge):
    key_ref, scan_ref, end_ref = plan

    def bring(register, _):
        item = key_ref[eight_at(register), :] & 8191
        tables = [rows_of(term_ref, ITEM_ROWS * channel) for channel in range(channels)]
        for channel, values in enumerate(table_picks(tables, ITEM_ROWS, item)):
            sorted_ref[eight_at(register, ITEM_ROWS * channel), :] = values
        return 0

    lax.fori_loop(0, 8, bring, 0)
    nodes = [key_ref[8 * register : 8 * register + 8, :] >> 13 for register in range(8)]
    scan = scan_ref[...]
    follows = [(scan & (1 << step)) != 0 for step in range(len(SCAN_STEPS) + 1)]
    for channel in range(channels):
        base = ITEM_ROWS * channel
        runs = [sorted_ref[base : base + 8, :]]
        for register in range(1, 8):
            same = nodes[register] == nodes[register - 1]
            here = sorted_ref[base + 8 * register : base + 8 * register + 8, :]
            runs.append(merge(here, jnp.where(same, runs[-1], 0.0)))
        total = runs[7]
        for step, distance in enumerate(SCAN_STEPS):
            total = merge(total, jnp.where(follows[step], group_shift(total, distance), 0.0))
        carry = jnp.where(follows[-1], group_shift(total, 1), 0.0)
        for register in range(8):
            open_run = nodes[register] == nodes[0]
            sorted_ref[base + 8 * register : base + 8 * register + 8, :] = merge(
                runs[register], jnp.where(open_run, carry, 0.0)
            )

    def deliver(half, _):
        index = end_ref[eight_at(half), :]
        tables = [rows_of(sorted_ref, ITEM_ROWS * channel) for channel in range(channels)]
        for channel, values in enumerate(table_picks(tables, ITEM_ROWS, index)):
            out_ref[eight_at(half, NODE_ROWS * channel), :] = values
        return 0

    lax.fori_loop(0, 2, deliver, 0)


def node_picks(table_ref, channels, conn_ref, chunk):
    tables = [rows_of(table_ref, NODE_ROWS * channel) for channel in range(channels)]
    return table_picks(tables, NODE_ROWS, conn_ref[eight_at(chunk), :])


def measure_blocks(blocks_ref, row_ref, scale_ref, conn_ref, term_ref, max_ref):
    def one(chunk, _):
        scales = node_picks(scale_ref, 3, conn_ref, chunk)
        best = [jnp.zeros((8, LANES), F32)] * 3
        at = chunk_at(chunk)
        for r in range(STRAINS):
            sized = [
                jnp.abs(blocks_ref[0, 0, r, 8 * c : 8 * c + 8, at]) * scales[c] for c in range(3)
            ]
            whole = jnp.maximum(jnp.maximum(sized[0], sized[1]), sized[2])
            max_ref[r : r + 1, at] = jnp.max(whole, axis=0, keepdims=True)
            row = row_ref[r : r + 1, at]
            best = [jnp.maximum(best[c], sized[c] * row) for c in range(3)]
        for c in range(3):
            term_ref[eight_at(chunk, ITEM_ROWS * c), :] = best[c]
        return 0

    lax.fori_loop(0, CHUNKS, one, 0)


def apply_blocks(blocks_ref, table_ref, sets, conn_ref, strain_ref):
    def one(chunk, _):
        values = node_picks(table_ref, 3 * sets, conn_ref, chunk)
        at = chunk_at(chunk)
        for r in range(STRAINS):
            parts = [blocks_ref[0, 0, r, 8 * c : 8 * c + 8, at] for c in range(3)]
            for k in range(sets):
                mine = values[3 * k : 3 * k + 3]
                total = parts[0] * mine[0] + parts[1] * mine[1] + parts[2] * mine[2]
                strain_ref[STRAINS * k + r : STRAINS * k + r + 1, at] = jnp.sum(
                    total, axis=0, keepdims=True
                )
        return 0

    lax.fori_loop(0, CHUNKS, one, 0)


def apply_transpose(blocks_ref, strain_ref, sets, term_ref):
    def one(chunk, _):
        at = chunk_at(chunk)
        totals = [jnp.zeros((8, LANES), F32)] * (3 * sets)
        for r in range(STRAINS):
            parts = [blocks_ref[0, 0, r, 8 * c : 8 * c + 8, at] for c in range(3)]
            for k in range(sets):
                strain = strain_ref[STRAINS * k + r : STRAINS * k + r + 1, at]
                for c in range(3):
                    totals[3 * k + c] = totals[3 * k + c] + parts[c] * strain
        for channel in range(3 * sets):
            term_ref[eight_at(chunk, ITEM_ROWS * channel), :] = totals[channel]
        return 0

    lax.fori_loop(0, CHUNKS, one, 0)


def pack(part_ref, channels, packet_refs):
    for side in range(SIDES):
        for channel in range(channels):
            base = NODE_ROWS * channel + 2 * side
            packet_refs[side][4 * channel : 4 * channel + 2, :] = part_ref[base : base + 2, :]
            packet_refs[side][4 * channel + 2 : 4 * channel + 4, :] = part_ref[base + 8 : base + 10, :]


def live_sides():
    band = lax.axis_index("band")
    return [None, None, band > 0, band < lax.axis_size("band") - 1]


def unpack(part_ref, channels, arrived_refs, merge, out_ref, groups=True):
    live = live_sides()
    for side in range(SIDES):
        for channel in range(channels):
            base = NODE_ROWS * channel + 2 * side
            theirs = arrived_refs[side][4 * channel + 2 : 4 * channel + 4, :]
            if live[side] is not None:
                theirs = jnp.where(live[side], theirs, 0.0)
            out_ref[base : base + 2, :] = merge(part_ref[base : base + 2, :], theirs)
            if groups:
                theirs = arrived_refs[side][4 * channel : 4 * channel + 2, :]
                if live[side] is not None:
                    theirs = jnp.where(live[side], theirs, 0.0)
                out_ref[base + 8 : base + 10, :] = merge(part_ref[base + 8 : base + 10, :], theirs)


def rescale(scale, peak):
    seen = peak > 0.0
    return jnp.where(seen, scale / jnp.sqrt(jnp.where(seen, peak, 1.0)), 0.0)


def project_rows(ref):
    def every_third(start):
        return jnp.concatenate([ref[r : r + 1, :] for r in range(start, STRAINS, 3)], axis=0)

    top, first, second = [every_third(start) for start in range(3)]
    norm = jnp.sqrt(first * first + second * second)
    inside = norm <= top
    middle = norm > jnp.abs(top)
    factor = 0.5 * (1.0 + top / jnp.where(middle, norm, 1.0))
    gain = jnp.where(inside, 1.0, jnp.where(middle, factor, 0.0))
    top = jnp.where(inside, top, jnp.where(middle, factor * norm, 0.0))
    for start, values in enumerate((top, gain * first, gain * second)):
        for cone in range(4):
            ref[3 * cone + start : 3 * cone + start + 1, :] = values[cone : cone + 1, :]


def start_kernel(
    blocks_ref,
    conn_ref,
    send_ref,
    loads_ref,
    conn_out,
    key_out,
    scan_out,
    end_out,
    inverse_out,
    row_out,
    scale_out,
    part_out,
    own_loads_out,
    *rest,
):
    packets, (send_ids, term, items, peaks, ones) = rest[:4], rest[4:]
    make_plan(conn_ref, send_ref, conn_out, key_out, scan_out, end_out, inverse_out, send_ids)
    row = lax.broadcasted_iota(I32, (NODE_ROWS, LANES), 0)
    below, above = live_sides()[2:]
    first = jnp.where(row < 12, 1.0, jnp.where(row < 14, below.astype(F32), above.astype(F32)))
    for c in range(3):
        scale_out[NODE_ROWS * c : NODE_ROWS * (c + 1), :] = first
    ones[...] = jnp.ones_like(ones)
    measure_blocks(blocks_ref, ones, scale_out, conn_out, term, peaks)
    row_out[...] = 1.0 / jnp.sqrt(peaks[...])
    scatter_items(term, 3, (key_out, scan_out, end_out), items, part_out, jnp.maximum)
    pack(part_out, 3, packets)
    tables = [
        lambda r, c=c: loads_ref[0, 0, c : c + 1, r * LANES : (r + 1) * LANES] for c in range(3)
    ]
    for c, values in enumerate(table_picks(tables, 8, send_ids[...])):
        own_loads_out[8 * c : 8 * c + 8, :] = values
        for side in range(SIDES):
            packets[side][12 + 2 * c : 14 + 2 * c, :] = own_loads_out[
                8 * c + 2 * side : 8 * c + 2 * side + 2, :
            ]


def sweep_kernel(
    with_loads,
    blocks_ref,
    conn_ref,
    key_ref,
    scan_ref,
    end_ref,
    row_ref,
    scale_ref,
    part_ref,
    *rest,
):
    arrived, rest = rest[:4], rest[4:]
    if with_loads:
        own_loads, rest = rest[0], rest[1:]
    row_out, scale_out, part_out, rest = rest[0], rest[1], rest[2], rest[3:]
    if with_loads:
        loads_out, rest = rest[0], rest[1:]
    packets, (term, items, peaks, merged) = rest[:4], rest[4:]
    unpack(part_ref, 3, arrived, jnp.maximum, merged)
    scale_out[...] = rescale(scale_ref[...], merged[...])
    if with_loads:
        for c in range(3):
            loads_out[NODE_ROWS * c : NODE_ROWS * c + 8, :] = own_loads[8 * c : 8 * c + 8, :]
            for side in range(SIDES):
                base = NODE_ROWS * c + 8 + 2 * side
                loads_out[base : base + 2, :] = arrived[side][12 + 2 * c : 14 + 2 * c, :]
    measure_blocks(blocks_ref, row_ref, scale_out, conn_ref, term, peaks)
    row_out[...] = row_ref[...] / jnp.sqrt(row_ref[...] * peaks[...])
    scatter_items(term, 3, (key_ref, scan_ref, end_ref), items, part_out, jnp.maximum)
    pack(part_out, 3, packets)


def target_kernel(
    blocks_ref,
    conn_ref,
    key_ref,
    scan_ref,
    end_ref,
    row_ref,
    scale_ref,
    part_ref,
    loads_ref,
    *rest,
):
    arrived, rest = rest[:4], rest[4:]
    scale_out, strain_out, part_out, rest = rest[0], rest[1], rest[2], rest[3:]
    packets, (term, items, table, strain, cones) = rest[:4], rest[4:]
    unpack(part_ref, 3, arrived, jnp.maximum, table)
    scale = rescale(scale_ref[...], table[...])
    scale_out[...] = scale
    table[...] = scale * (scale * loads_ref[...])
    apply_blocks(blocks_ref, table, 1, conn_ref, strain)
    row = row_ref[...]
    image = row * strain[0:STRAINS, :]
    cones[...] = image
    project_rows(cones)
    strain[0:STRAINS, :] = row * image
    strain[STRAINS : 2 * STRAINS, :] = row * cones[...]
    strain_out[...] = 3.0 * image + 2.0 * cones[...]
    apply_transpose(blocks_ref, strain, 2, term)
    scatter_items(term, 6, (key_ref, scan_ref, end_ref), items, part_out, jnp.add)
    part_out[0:48, :] = part_out[0:48, :] * scale
    part_out[48:96, :] = part_out[48:96, :] * scale
    pack(part_out, 6, packets)


def second_kernel(
    blocks_ref, conn_ref, key_ref, scan_ref, end_ref, row_ref, scale_ref, part_ref, *rest
):
    arrived, rest = rest[:4], rest[4:]
    joint_out, strain_out, part_out, rest = rest[0], rest[1], rest[2], rest[3:]
    packets, (term, items, table, strain) = rest[:4], rest[4:]
    unpack(part_ref, 6, arrived, jnp.add, table)
    joint_out[...] = table[48:96, :]
    scale = scale_ref[...]
    table[0:48, :] = scale * table[0:48, :]
    table[48:96, :] = scale * table[48:96, :]
    apply_blocks(blocks_ref, table, 2, conn_ref, strain)
    row = row_ref[...]
    strain_out[...] = row * strain[STRAINS : 2 * STRAINS, :]
    strain[0:STRAINS, :] = row * (row * strain[0:STRAINS, :])
    apply_transpose(blocks_ref, strain, 1, term)
    scatter_items(term, 3, (key_ref, scan_ref, end_ref), items, part_out, jnp.add)
    part_out[...] = part_out[...] * scale
    pack(part_out, 3, packets)


def own_square(ref):
    total = jnp.zeros((8, LANES), F32)
    for c in range(3):
        mine = ref[NODE_ROWS * c : NODE_ROWS * c + 8, :]
        total = total + mine * mine
    return jnp.sum(total, axis=0, keepdims=True)


def third_kernel(
    blocks_ref, conn_ref, key_ref, scan_ref, end_ref, row_ref, scale_ref, part_ref, *rest
):
    arrived, rest = rest[:4], rest[4:]
    norm_out, part_out, rest = rest[0], rest[1], rest[2:]
    packets, (term, items, table, strain) = rest[:4], rest[4:]
    unpack(part_ref, 3, arrived, jnp.add, table)
    norm_out[...] = own_square(table)
    scale = scale_ref[...]
    table[...] = scale * table[...]
    apply_blocks(blocks_ref, table, 1, conn_ref, strain)
    row = row_ref[...]
    strain[...] = row * (row * strain[...])
    apply_transpose(blocks_ref, strain, 1, term)
    scatter_items(term, 3, (key_ref, scan_ref, end_ref), items, part_out, jnp.add)
    part_out[...] = part_out[...] * scale
    pack(part_out, 3, packets)


def norm_kernel(
    part_ref, norm_ref, scale_ref, loads_ref, joint_ref, inverse_ref, *rest
):
    arrived, (sums_out, velocity_out, table, lines) = rest[:4], rest[4:]
    unpack(part_ref, 3, arrived, jnp.add, table, groups=False)
    first = jnp.sum(norm_ref[...], axis=1, keepdims=True)
    last = jnp.sum(own_square(table), axis=1, keepdims=True)
    lane = lax.broadcasted_iota(I32, (1, LANES), 1)
    line = jnp.where(lane == 0, first, jnp.where(lane == 1, last, 0.0))
    sums_out[...] = jnp.broadcast_to(line, sums_out.shape)
    for c in range(3):
        base = NODE_ROWS * c
        scale = scale_ref[base : base + 8, :]
        lines[8 * c : 8 * c + 8, :] = scale * (scale * loads_ref[base : base + 8, :])
        lines[24 + 8 * c : 32 + 8 * c, :] = scale * joint_ref[base : base + 8, :]
    tables = [rows_of(lines, 8 * channel) for channel in range(6)]
    for channel, values in enumerate(table_picks(tables, 8, inverse_ref[...])):
        for r in range(8):
            velocity_out[channel : channel + 1, r * LANES : (r + 1) * LANES] = values[r : r + 1, :]


def final_kernel(
    sums_ref, step_ref, velocity_ref, base_ref, joint_ref, row_ref, velocity_out, multiplier_out, cones
):
    sums = jnp.sum(sums_ref[...], axis=0, keepdims=True)
    lane = lax.broadcasted_iota(I32, (1, LANES), 1)
    before = jnp.sum(jnp.where(lane == 0, sums, 0.0), axis=1, keepdims=True)
    after = jnp.sum(jnp.where(lane == 1, sums, 0.0), axis=1, keepdims=True)
    largest = jnp.sqrt(after + epsilon) / jnp.sqrt(before + epsilon)
    step = step_ref[0] / jnp.sqrt(largest)
    square = step * step
    target = velocity_ref[0:3, :]
    joint = velocity_ref[3:6, :]
    velocity_out[0, 0] = (2.0 * step) * (square * joint - target)
    cones[...] = square * (base_ref[...] - (4.0 * square) * joint_ref[...])
    project_rows(cones)
    multiplier_out[0, 0] = row_ref[...] * cones[...]


def call(body, out_shapes, scratch, *arrays, smem=()):
    specs = [
        pl.BlockSpec(memory_space=pltpu.SMEM if i in smem else pltpu.VMEM) for i in range(len(arrays))
    ]
    return pl.pallas_call(
        body,
        out_shape=[jax.ShapeDtypeStruct(shape, kind) for shape, kind in out_shapes],
        in_specs=specs,
        out_specs=[pl.BlockSpec(memory_space=pltpu.VMEM) for _ in out_shapes],
        scratch_shapes=[pltpu.VMEM(shape, kind) for shape, kind in scratch],
        compiler_params=pltpu.CompilerParams(vmem_limit_bytes=24 * 1024 * 1024),
    )(*arrays)


def exchange(packets):
    arrived = []
    for side, packet in enumerate(packets):
        axis = "sector" if side < 2 else "band"
        count = lax.axis_size(axis)
        toward = 1 if side % 2 == 0 else -1
        arrived.append(lax.ppermute(packets[side ^ 1], axis, [(i, (i + toward) % count) for i in range(count)]))
    return arrived


def per_device(blocks, connectivity, send_lists, nodal_loads, step_scale):
    packet = [((12, LANES), F32)] * 4
    nodes = ((48, LANES), F32)
    rows = ((STRAINS, 1024), F32)
    items = ((3 * ITEM_ROWS, LANES), F32)
    (conn, key, scan, end, inverse, row, scale, part, own_loads, *packets) = call(
        start_kernel,
        [
            ((64, LANES), I32),
            ((64, LANES), I32),
            ((8, LANES), I32),
            ((16, LANES), I32),
            ((8, LANES), I32),
            rows,
            nodes,
            nodes,
            ((24, LANES), F32),
        ]
        + [((18, LANES), F32)] * 4,
        [((8, LANES), I32), items, items, rows, rows],
        blocks,
        connectivity,
        send_lists,
        nodal_loads,
    )
    plan = (blocks, conn, key, scan, end)
    row, scale, part, loads, *packets = call(
        functools.partial(sweep_kernel, True),
        [rows, nodes, nodes, nodes] + packet,
        [items, items, rows, nodes],
        *plan,
        row,
        scale,
        part,
        *exchange(packets),
        own_loads,
    )
    row, scale, part, *packets = call(
        functools.partial(sweep_kernel, False),
        [rows, nodes, nodes] + packet,
        [items, items, rows, nodes],
        *plan,
        row,
        scale,
        part,
        *exchange(packets),
    )
    twice = ((6 * ITEM_ROWS, LANES), F32)
    scale, base, part, *packets = call(
        target_kernel,
        [nodes, rows, ((96, LANES), F32)] + [((24, LANES), F32)] * 4,
        [twice, twice, nodes, ((2 * STRAINS, 1024), F32), rows],
        *plan,
        row,
        scale,
        part,
        loads,
        *exchange(packets),
    )
    joint, image, part, *packets = call(
        second_kernel,
        [nodes, rows, nodes] + packet,
        [items, items, ((96, LANES), F32), ((2 * STRAINS, 1024), F32)],
        *plan,
        row,
        scale,
        part,
        *exchange(packets),
    )
    norm, part, *packets = call(
        third_kernel,
        [((1, LANES), F32), nodes] + packet,
        [items, items, nodes, rows],
        *plan,
        row,
        scale,
        part,
        *exchange(packets),
    )
    count = lax.axis_size("band") * lax.axis_size("sector")
    sums, lines = call(
        norm_kernel,
        [((count, LANES), F32), ((6, 1024), F32)],
        [nodes, nodes],
        part,
        norm,
        scale,
        loads,
        joint,
        inverse,
        *exchange(packets),
    )
    sums = lax.all_to_all(sums, AXES, 0, 0, tiled=True)
    return tuple(
        call(
            final_kernel,
            [((1, 1, 3, 1024), F32), ((1, 1, STRAINS, 1024), F32)],
            [rows],
            sums,
            step_scale,
            lines,
            base,
            image,
            row,
            smem=(1,),
        )
    )


def solution(mesh):
    in_specs = (
        P("band", "sector", None, None, None),
        P("band", "sector", None, None),
        P("band", "sector", None, None),
        P("band", "sector", None, None),
        P(),
    )
    out_specs = (P("band", "sector", None, None), P("band", "sector", None, None))
    return jax.shard_map(
        per_device, mesh=mesh, in_specs=in_specs, out_specs=out_specs, check_vma=False
    )
```

profile of v0, /device:TPU:1, one launch (start us, length us, event | category | flops | bytes accessed | tf_op | source)
XLA Modules:
  0.0 123.8 jit_solution(7035543499033854407)
XLA Ops:
  0.6 0.7 copy.10.loads_ref
  1.3 1.3 %copy-done = f32[1,1,12,24,1024]{4,3,2,1,0:T(8,128)S(1)} copy-done((f32[1,1,12,24,1024]{4,3,2,1,0:T(8,128)S(1)}, f32[1,1,12,24,1024]{4,3,2,1,0:T(8,128)}, u32[]{:S(2)}) %copy-start) | copy-done | bytes 1179672
  2.6 0.8 copy-done.1
  3.4 0.7 copy-done.2
  4.1 8.2 %shard_map.68 = (s32[64,128]{1,0:T(8,128)S(1)}, s32[64,128]{1,0:T(8,128)S(1)}, s32[8,128]{1,0:T(8,128)S(1)}, s32[16,128]{1,0:T(8,128)S(1)}, s32[8,128]{1,0:T(8,1...) custom-call(f32[1,1,12,24,1024]{4,3,2,1,0:T(8,128)S(1)} %copy-done, ...), custom_call_target="tpu_custom_call" | custom-call | tf_op jit(solution)/shard_map/pallas_call | solution.py:532
  12.2 2.5 %collective-permute-start = (f32[18,128]{1,0:T(8,128)S(1)}, f32[18,128]{1,0:T(8,128)S(1)}, u32[]{:S(2)}, u32[]{:S(2)}) collective-permute-start(f32[18,128]{1,0:T(8,128)S(1)} %get-tuple-element.59), channel_id=1, source_target_pairs={{0,1},{1,2},{2,3},{3,4},{4,5},{5,6},{6,7},{7,8},{8,9},{9,10},{10,1... | collective-permute-start | bytes 27656 | tf_op jit(solution)/shard_map/ppermute | solution.py:548
  14.8 6.2 %collective-permute-start.1 = (f32[18,128]{1,0:T(8,128)S(1)}, f32[18,128]{1,0:T(8,128)S(1)}, u32[]{:S(2)}, u32[]{:S(2)}) collective-permute-start(f32[18,128]{1,0:T(8,128)S(1)} %get-tuple-element.60), channel_id=1, source_target_pairs={{0,31},{1,0},{2,1},{3,2},{4,3},{5,4},{6,5},{7,6},{8,7},{9,8},{10,9... | collective-permute-start | bytes 27656 | tf_op jit(solution)/shard_map/ppermute | solution.py:548
  21.0 2.1 %collective-permute-start.2 = (f32[18,128]{1,0:T(8,128)S(1)}, f32[18,128]{1,0:T(8,128)S(1)}, u32[]{:S(2)}, u32[]{:S(2)}) collective-permute-start(f32[18,128]{1,0:T(8,128)S(1)} %get-tuple-element.61), channel_id=1, source_target_pairs={{0,32},{32,64},{64,96},{96,128},{128,160},{160,192},{192,224},{224... | collective-permute-start | bytes 27656 | tf_op jit(solution)/shard_map/ppermute | solution.py:548
  23.2 0.8 collective-permute-done.2.rest_2_
  24.0 2.3 %collective-permute-done.3.rest_3_ = f32[18,128]{1,0:T(8,128)S(1)} collective-permute-done((f32[18,128]{1,0:T(8,128)S(1)}, f32[18,128]{1,0:T(8,128)S(1)}, u32[]{:S(2)}, u32[]{:S(2)}) %collective-permute-start.3) | collective-permute-done | bytes 9248 | tf_op jit(solution)/shard_map/ppermute | solution.py:548
  26.3 4.9 %shard_map.69 = (f32[12,1024]{1,0:T(8,128)S(1)}, f32[48,128]{1,0:T(8,128)S(1)}, f32[48,128]{1,0:T(8,128)S(1)}, f32[48,128]{1,0:T(8,128)S(1)}, f32[12,128]{1,0:T(...) custom-call(f32[1,1,12,24,1024]{4,3,2,1,0:T(8,128)S(1)} %copy-done, ...), custom_call_target="tpu_custom_call" | custom-call | tf_op jit(solution)/shard_map/pallas_call | solution.py:532
  31.2 0.1 collective-permute-start.4
  31.2 4.8 %collective-permute-start.5 = (f32[12,128]{1,0:T(8,128)S(1)}, f32[12,128]{1,0:T(8,128)S(1)}, u32[]{:S(2)}, u32[]{:S(2)}) collective-permute-start(f32[12,128]{1,0:T(8,128)S(1)} %get-tuple-element.68), channel_id=1, source_target_pairs={{0,31},{1,0},{2,1},{3,2},{4,3},{5,4},{6,5},{7,6},{8,7},{9,8},{10,9... | collective-permute-start | bytes 18440 | tf_op jit(solution)/shard_map/ppermute | solution.py:548
  36.0 0.6 collective-permute-start.6
  36.6 0.0 collective-permute-start.7
  36.6 0.4 collective-permute-done.4.rest_0_
  37.1 0.3 collective-permute-done.6.rest_2_
  37.4 2.6 %collective-permute-done.7.rest_3_ = f32[12,128]{1,0:T(8,128)S(1)} collective-permute-done((f32[12,128]{1,0:T(8,128)S(1)}, f32[12,128]{1,0:T(8,128)S(1)}, u32[]{:S(2)}, u32[]{:S(2)}) %collective-permute-start.7) | collective-permute-done | bytes 6176 | tf_op jit(solution)/shard_map/ppermute | solution.py:548
  40.0 4.9 %shard_map.70 = (f32[12,1024]{1,0:T(8,128)S(1)}, f32[48,128]{1,0:T(8,128)S(1)}, f32[48,128]{1,0:T(8,128)S(1)}, f32[12,128]{1,0:T(8,128)S(1)}, f32[12,128]{1,0:T(...) custom-call(f32[1,1,12,24,1024]{4,3,2,1,0:T(8,128)S(1)} %copy-done, s32[64,128]{1,0:T(8,128)S(1)} %get-tuple-element.52.conn_ref, ...), custom_call_target="tpu_custom_call" | custom-call | tf_op jit(solution)/shard_map/pallas_call | solution.py:532
  44.9 1.0 collective-permute-start.11
  45.9 4.8 %collective-permute-start.9 = (f32[12,128]{1,0:T(8,128)S(1)}, f32[12,128]{1,0:T(8,128)S(1)}, u32[]{:S(2)}, u32[]{:S(2)}) collective-permute-start(f32[12,128]{1,0:T(8,128)S(1)} %get-tuple-element.76), channel_id=1, source_target_pairs={{0,31},{1,0},{2,1},{3,2},{4,3},{5,4},{6,5},{7,6},{8,7},{9,8},{10,9... | collective-permute-start | bytes 18440 | tf_op jit(solution)/shard_map/ppermute | solution.py:548
  50.7 1.0 collective-permute-done.8.rest_0_
  51.7 7.3 %shard_map.71 = (f32[48,128]{1,0:T(8,128)S(1)}, f32[12,1024]{1,0:T(8,128)S(1)}, f32[96,128]{1,0:T(8,128)S(1)}, f32[24,128]{1,0:T(8,128)S(1)}, f32[24,128]{1,0:T(...) custom-call(f32[1,1,12,24,1024]{4,3,2,1,0:T(8,128)S(1)} %copy-done, s32[64,128]{1,0:T(8,128)S(1)} %get-tuple-element.52.conn_ref, ...), custom_call_target="tpu_custom_call" | custom-call | tf_op jit(solution)/shard_map/pallas_call | solution.py:532
  59.0 0.1 collective-permute-start.12
  59.1 4.9 %collective-permute-start.13 = (f32[24,128]{1,0:T(8,128)S(1)}, f32[24,128]{1,0:T(8,128)S(1)}, u32[]{:S(2)}, u32[]{:S(2)}) collective-permute-start(f32[24,128]{1,0:T(8,128)S(1)} %get-tuple-element.82), channel_id=1, source_target_pairs={{0,31},{1,0},{2,1},{3,2},{4,3},{5,4},{6,5},{7,6},{8,7},{9,8},{10,9... | collective-permute-start | bytes 36872 | tf_op jit(solution)/shard_map/ppermute | solution.py:548
  64.0 2.5 %collective-permute-start.14 = (f32[24,128]{1,0:T(8,128)S(1)}, f32[24,128]{1,0:T(8,128)S(1)}, u32[]{:S(2)}, u32[]{:S(2)}) collective-permute-start(f32[24,128]{1,0:T(8,128)S(1)} %get-tuple-element.83), channel_id=1, source_target_pairs={{0,32},{32,64},{64,96},{96,128},{128,160},{160,192},{192,224},{224... | collective-permute-start | bytes 36872 | tf_op jit(solution)/shard_map/ppermute | solution.py:548
  66.4 2.2 %collective-permute-start.15 = (f32[24,128]{1,0:T(8,128)S(1)}, f32[24,128]{1,0:T(8,128)S(1)}, u32[]{:S(2)}, u32[]{:S(2)}) collective-permute-start(f32[24,128]{1,0:T(8,128)S(1)} %get-tuple-element.84), channel_id=1, source_target_pairs={{0,224},{32,0},{64,32},{96,64},{128,96},{160,128},{192,160},{224,1... | collective-permute-start | bytes 36872 | tf_op jit(solution)/shard_map/ppermute | solution.py:548
  68.6 0.7 collective-permute-done.14.rest_2_
  69.3 0.5 collective-permute-done.15.rest_3_
  69.8 5.5 %shard_map.72 = (f32[48,128]{1,0:T(8,128)S(1)}, f32[12,1024]{1,0:T(8,128)S(1)}, f32[48,128]{1,0:T(8,128)S(1)}, f32[12,128]{1,0:T(8,128)S(1)}, f32[12,128]{1,0:T(...) custom-call(f32[1,1,12,24,1024]{4,3,2,1,0:T(8,128)S(1)} %copy-done, s32[64,128]{1,0:T(8,128)S(1)} %get-tuple-element.52.conn_ref, ...), custom_call_target="tpu_custom_call" | custom-call | tf_op jit(solution)/shard_map/pallas_call | solution.py:532
  75.3 0.1 collective-permute-start.16
  75.3 4.8 %collective-permute-start.17 = (f32[12,128]{1,0:T(8,128)S(1)}, f32[12,128]{1,0:T(8,128)S(1)}, u32[]{:S(2)}, u32[]{:S(2)}) collective-permute-start(f32[12,128]{1,0:T(8,128)S(1)} %get-tuple-element.87), channel_id=1, source_target_pairs={{0,31},{1,0},{2,1},{3,2},{4,3},{5,4},{6,5},{7,6},{8,7},{9,8},{10,9... | collective-permute-start | bytes 18440 | tf_op jit(solution)/shard_map/ppermute | solution.py:548
  80.1 0.4 collective-permute-start.18
  80.5 3.4 %collective-permute-start.19 = (f32[12,128]{1,0:T(8,128)S(1)}, f32[12,128]{1,0:T(8,128)S(1)}, u32[]{:S(2)}, u32[]{:S(2)}) collective-permute-start(f32[12,128]{1,0:T(8,128)S(1)} %get-tuple-element.89), channel_id=1, source_target_pairs={{0,224},{32,0},{64,32},{96,64},{128,96},{160,128},{192,160},{224,1... | collective-permute-start | bytes 18440 | tf_op jit(solution)/shard_map/ppermute | solution.py:548
  83.9 0.7 collective-permute-done.18.rest_2_
  84.5 0.2 collective-permute-done.19.rest_3_
  84.7 5.0 %shard_map.73 = (f32[1,128]{1,0:T(1,128)S(1)}, f32[48,128]{1,0:T(8,128)S(1)}, f32[12,128]{1,0:T(8,128)S(1)}, f32[12,128]{1,0:T(8,128)S(1)}, f32[12,128]{1,0:T(8,128)S(1)}, /*index=5*/f32[12,128]{1,0:T(8,128)S(1)}) custom-call(f32[1,1,12,24,1024]{4,3,2,1,0:T(8,128)S(1)} %copy-done, s32[64,128]{1,0:T(8,128)S(1)} %get-tuple-element.52.conn_ref, ...), custom_call_target="tpu_custom_call" | custom-call | tf_op jit(solution)/shard_map/pallas_call | solution.py:532
  89.7 0.1 collective-permute-start.20
  89.8 4.8 %collective-permute-start.21 = (f32[12,128]{1,0:T(8,128)S(1)}, f32[12,128]{1,0:T(8,128)S(1)}, u32[]{:S(2)}, u32[]{:S(2)}) collective-permute-start(f32[12,128]{1,0:T(8,128)S(1)} %get-tuple-element.95), channel_id=1, source_target_pairs={{0,31},{1,0},{2,1},{3,2},{4,3},{5,4},{6,5},{7,6},{8,7},{9,8},{10,9... | collective-permute-start | bytes 18440 | tf_op jit(solution)/shard_map/ppermute | solution.py:548
  94.6 4.1 %collective-permute-start.23 = (f32[12,128]{1,0:T(8,128)S(1)}, f32[12,128]{1,0:T(8,128)S(1)}, u32[]{:S(2)}, u32[]{:S(2)}) collective-permute-start(f32[12,128]{1,0:T(8,128)S(1)} %get-tuple-element.97), channel_id=1, source_target_pairs={{0,224},{32,0},{64,32},{96,64},{128,96},{160,128},{192,160},{224,1... | collective-permute-start | bytes 18440 | tf_op jit(solution)/shard_map/ppermute | solution.py:548
  98.6 0.7 collective-permute-done.22.rest_2_
  99.3 0.2 collective-permute-done.23.rest_3_
  99.5 0.8 shard_map.74
  100.2 8.9 %all-to-all-start = ((f32[256,1,128]{2,1,0:T(1,128)}), f32[256,1,128]{2,1,0:T(1,128)S(1)}, u32[]{:S(2)}, u32[]{:S(2)}) async-start(f32[256,1,128]{2,1,0:T(1,128)} %bitcast.1), calls=%async_computation | async-start | bytes 262144 | tf_op jit(solution)/shard_map/all_to_all | solution.py:644
  109.8 12.4 %all-to-all-done = f32[256,1,128]{2,1,0:T(1,128)S(1)} async-done(((f32[256,1,128]{2,1,0:T(1,128)}), f32[256,1,128]{2,1,0:T(1,128)S(1)}, u32[]{:S(2)}, u32[]{:S(2)}) %all-to-all-start) | async-done | bytes 131104 | tf_op jit(solution)/shard_map/all_to_all | solution.py:644
  122.2 0.2 shard_map.75
  122.5 0.7 copy.13
  123.2 0.6 copy.12
  (19 shorter events, 0.1 us)
Async XLA Ops:
  1.3 1.3 %copy-start = (f32[1,1,12,24,1024]{4,3,2,1,0:T(8,128)S(1)}, f32[1,1,12,24,1024]{4,3,2,1,0:T(8,128)}, u32[]{:S(2)}) copy-start(f32[1,1,12,24,1024]{4,3,2,1,0:T(8,128)} %blocks_ref.11) | copy-start | bytes 3538948
  2.6 0.8 copy-start.1
  3.4 0.7 copy-start.2
  12.2 10.9 %collective-permute-start = (f32[18,128]{1,0:T(8,128)S(1)}, f32[18,128]{1,0:T(8,128)S(1)}, u32[]{:S(2)}, u32[]{:S(2)}) collective-permute-start(f32[18,128]{1,0:T(8,128)S(1)} %get-tuple-element.59), channel_id=1, source_target_pairs={{0,1},{1,2},{2,3},{3,4},{4,5},{5,6},{6,7},{7,8},{8,9},{9,10},{10,1... | collective-permute-start | bytes 27656 | tf_op jit(solution)/shard_map/ppermute | solution.py:548
  14.8 8.4 %collective-permute-start.1 = (f32[18,128]{1,0:T(8,128)S(1)}, f32[18,128]{1,0:T(8,128)S(1)}, u32[]{:S(2)}, u32[]{:S(2)}) collective-permute-start(f32[18,128]{1,0:T(8,128)S(1)} %get-tuple-element.60), channel_id=1, source_target_pairs={{0,31},{1,0},{2,1},{3,2},{4,3},{5,4},{6,5},{7,6},{8,7},{9,8},{10,9... | collective-permute-start | bytes 27656 | tf_op jit(solution)/shard_map/ppermute | solution.py:548
  21.0 3.0 %collective-permute-start.2 = (f32[18,128]{1,0:T(8,128)S(1)}, f32[18,128]{1,0:T(8,128)S(1)}, u32[]{:S(2)}, u32[]{:S(2)}) collective-permute-start(f32[18,128]{1,0:T(8,128)S(1)} %get-tuple-element.61), channel_id=1, source_target_pairs={{0,32},{32,64},{64,96},{96,128},{128,160},{160,192},{192,224},{224... | collective-permute-start | bytes 27656 | tf_op jit(solution)/shard_map/ppermute | solution.py:548
  23.2 3.1 %collective-permute-start.3 = (f32[18,128]{1,0:T(8,128)S(1)}, f32[18,128]{1,0:T(8,128)S(1)}, u32[]{:S(2)}, u32[]{:S(2)}) collective-permute-start(f32[18,128]{1,0:T(8,128)S(1)} %get-tuple-element.62), channel_id=1, source_target_pairs={{0,224},{32,0},{64,32},{96,64},{128,96},{160,128},{192,160},{224,1... | collective-permute-start | bytes 27656 | tf_op jit(solution)/shard_map/ppermute | solution.py:548
  31.2 5.9 %collective-permute-start.4 = (f32[12,128]{1,0:T(8,128)S(1)}, f32[12,128]{1,0:T(8,128)S(1)}, u32[]{:S(2)}, u32[]{:S(2)}) collective-permute-start(f32[12,128]{1,0:T(8,128)S(1)} %get-tuple-element.67), channel_id=1, source_target_pairs={{0,1},{1,2},{2,3},{3,4},{4,5},{5,6},{6,7},{7,8},{8,9},{9,10},{10,1... | collective-permute-start | bytes 18440 | tf_op jit(solution)/shard_map/ppermute | solution.py:548
  31.2 5.8 %collective-permute-start.5 = (f32[12,128]{1,0:T(8,128)S(1)}, f32[12,128]{1,0:T(8,128)S(1)}, u32[]{:S(2)}, u32[]{:S(2)}) collective-permute-start(f32[12,128]{1,0:T(8,128)S(1)} %get-tuple-element.68), channel_id=1, source_target_pairs={{0,31},{1,0},{2,1},{3,2},{4,3},{5,4},{6,5},{7,6},{8,7},{9,8},{10,9... | collective-permute-start | bytes 18440 | tf_op jit(solution)/shard_map/ppermute | solution.py:548
  36.0 1.4 %collective-permute-start.6 = (f32[12,128]{1,0:T(8,128)S(1)}, f32[12,128]{1,0:T(8,128)S(1)}, u32[]{:S(2)}, u32[]{:S(2)}) collective-permute-start(f32[12,128]{1,0:T(8,128)S(1)} %get-tuple-element.69), channel_id=1, source_target_pairs={{0,32},{32,64},{64,96},{96,128},{128,160},{160,192},{192,224},{224... | collective-permute-start | bytes 18440 | tf_op jit(solution)/shard_map/ppermute | solution.py:548
  36.6 3.4 %collective-permute-start.7 = (f32[12,128]{1,0:T(8,128)S(1)}, f32[12,128]{1,0:T(8,128)S(1)}, u32[]{:S(2)}, u32[]{:S(2)}) collective-permute-start(f32[12,128]{1,0:T(8,128)S(1)} %get-tuple-element.70), channel_id=1, source_target_pairs={{0,224},{32,0},{64,32},{96,64},{128,96},{160,128},{192,160},{224,1... | collective-permute-start | bytes 18440 | tf_op jit(solution)/shard_map/ppermute | solution.py:548
  44.9 5.8 %collective-permute-start.10 = (f32[12,128]{1,0:T(8,128)S(1)}, f32[12,128]{1,0:T(8,128)S(1)}, u32[]{:S(2)}, u32[]{:S(2)}) collective-permute-start(f32[12,128]{1,0:T(8,128)S(1)} %get-tuple-element.77), channel_id=1, source_target_pairs={{0,32},{32,64},{64,96},{96,128},{128,160},{160,192},{192,224},{224... | collective-permute-start | bytes 18440 | tf_op jit(solution)/shard_map/ppermute | solution.py:548
  44.9 5.8 %collective-permute-start.11 = (f32[12,128]{1,0:T(8,128)S(1)}, f32[12,128]{1,0:T(8,128)S(1)}, u32[]{:S(2)}, u32[]{:S(2)}) collective-permute-start(f32[12,128]{1,0:T(8,128)S(1)} %get-tuple-element.78), channel_id=1, source_target_pairs={{0,224},{32,0},{64,32},{96,64},{128,96},{160,128},{192,160},{224,1... | collective-permute-start | bytes 18440 | tf_op jit(solution)/shard_map/ppermute | solution.py:548
  45.9 5.8 %collective-permute-start.8 = (f32[12,128]{1,0:T(8,128)S(1)}, f32[12,128]{1,0:T(8,128)S(1)}, u32[]{:S(2)}, u32[]{:S(2)}) collective-permute-start(f32[12,128]{1,0:T(8,128)S(1)} %get-tuple-element.75), channel_id=1, source_target_pairs={{0,1},{1,2},{2,3},{3,4},{4,5},{5,6},{6,7},{7,8},{8,9},{9,10},{10,1... | collective-permute-start | bytes 18440 | tf_op jit(solution)/shard_map/ppermute | solution.py:548
  45.9 5.8 %collective-permute-start.9 = (f32[12,128]{1,0:T(8,128)S(1)}, f32[12,128]{1,0:T(8,128)S(1)}, u32[]{:S(2)}, u32[]{:S(2)}) collective-permute-start(f32[12,128]{1,0:T(8,128)S(1)} %get-tuple-element.76), channel_id=1, source_target_pairs={{0,31},{1,0},{2,1},{3,2},{4,3},{5,4},{6,5},{7,6},{8,7},{9,8},{10,9... | collective-permute-start | bytes 18440 | tf_op jit(solution)/shard_map/ppermute | solution.py:548
  59.0 9.6 %collective-permute-start.12 = (f32[24,128]{1,0:T(8,128)S(1)}, f32[24,128]{1,0:T(8,128)S(1)}, u32[]{:S(2)}, u32[]{:S(2)}) collective-permute-start(f32[24,128]{1,0:T(8,128)S(1)} %get-tuple-element.81), channel_id=1, source_target_pairs={{0,1},{1,2},{2,3},{3,4},{4,5},{5,6},{6,7},{7,8},{8,9},{9,10},{10,1... | collective-permute-start | bytes 36872 | tf_op jit(solution)/shard_map/ppermute | solution.py:548
  59.1 9.5 %collective-permute-start.13 = (f32[24,128]{1,0:T(8,128)S(1)}, f32[24,128]{1,0:T(8,128)S(1)}, u32[]{:S(2)}, u32[]{:S(2)}) collective-permute-start(f32[24,128]{1,0:T(8,128)S(1)} %get-tuple-element.82), channel_id=1, source_target_pairs={{0,31},{1,0},{2,1},{3,2},{4,3},{5,4},{6,5},{7,6},{8,7},{9,8},{10,9... | collective-permute-start | bytes 36872 | tf_op jit(solution)/shard_map/ppermute | solution.py:548
  64.0 5.3 %collective-permute-start.14 = (f32[24,128]{1,0:T(8,128)S(1)}, f32[24,128]{1,0:T(8,128)S(1)}, u32[]{:S(2)}, u32[]{:S(2)}) collective-permute-start(f32[24,128]{1,0:T(8,128)S(1)} %get-tuple-element.83), channel_id=1, source_target_pairs={{0,32},{32,64},{64,96},{96,128},{128,160},{160,192},{192,224},{224... | collective-permute-start | bytes 36872 | tf_op jit(solution)/shard_map/ppermute | solution.py:548
  66.4 3.4 %collective-permute-start.15 = (f32[24,128]{1,0:T(8,128)S(1)}, f32[24,128]{1,0:T(8,128)S(1)}, u32[]{:S(2)}, u32[]{:S(2)}) collective-permute-start(f32[24,128]{1,0:T(8,128)S(1)} %get-tuple-element.84), channel_id=1, source_target_pairs={{0,224},{32,0},{64,32},{96,64},{128,96},{160,128},{192,160},{224,1... | collective-permute-start | bytes 36872 | tf_op jit(solution)/shard_map/ppermute | solution.py:548
  75.3 8.6 %collective-permute-start.16 = (f32[12,128]{1,0:T(8,128)S(1)}, f32[12,128]{1,0:T(8,128)S(1)}, u32[]{:S(2)}, u32[]{:S(2)}) collective-permute-start(f32[12,128]{1,0:T(8,128)S(1)} %get-tuple-element.86), channel_id=1, source_target_pairs={{0,1},{1,2},{2,3},{3,4},{4,5},{5,6},{6,7},{7,8},{8,9},{9,10},{10,1... | collective-permute-start | bytes 18440 | tf_op jit(solution)/shard_map/ppermute | solution.py:548
  75.3 8.5 %collective-permute-start.17 = (f32[12,128]{1,0:T(8,128)S(1)}, f32[12,128]{1,0:T(8,128)S(1)}, u32[]{:S(2)}, u32[]{:S(2)}) collective-permute-start(f32[12,128]{1,0:T(8,128)S(1)} %get-tuple-element.87), channel_id=1, source_target_pairs={{0,31},{1,0},{2,1},{3,2},{4,3},{5,4},{6,5},{7,6},{8,7},{9,8},{10,9... | collective-permute-start | bytes 18440 | tf_op jit(solution)/shard_map/ppermute | solution.py:548
  80.1 4.4 %collective-permute-start.18 = (f32[12,128]{1,0:T(8,128)S(1)}, f32[12,128]{1,0:T(8,128)S(1)}, u32[]{:S(2)}, u32[]{:S(2)}) collective-permute-start(f32[12,128]{1,0:T(8,128)S(1)} %get-tuple-element.88), channel_id=1, source_target_pairs={{0,32},{32,64},{64,96},{96,128},{128,160},{160,192},{192,224},{224... | collective-permute-start | bytes 18440 | tf_op jit(solution)/shard_map/ppermute | solution.py:548
  80.5 4.2 %collective-permute-start.19 = (f32[12,128]{1,0:T(8,128)S(1)}, f32[12,128]{1,0:T(8,128)S(1)}, u32[]{:S(2)}, u32[]{:S(2)}) collective-permute-start(f32[12,128]{1,0:T(8,128)S(1)} %get-tuple-element.89), channel_id=1, source_target_pairs={{0,224},{32,0},{64,32},{96,64},{128,96},{160,128},{192,160},{224,1... | collective-permute-start | bytes 18440 | tf_op jit(solution)/shard_map/ppermute | solution.py:548
  89.7 8.9 %collective-permute-start.20 = (f32[12,128]{1,0:T(8,128)S(1)}, f32[12,128]{1,0:T(8,128)S(1)}, u32[]{:S(2)}, u32[]{:S(2)}) collective-permute-start(f32[12,128]{1,0:T(8,128)S(1)} %get-tuple-element.94), channel_id=1, source_target_pairs={{0,1},{1,2},{2,3},{3,4},{4,5},{5,6},{6,7},{7,8},{8,9},{9,10},{10,1... | collective-permute-start | bytes 18440 | tf_op jit(solution)/shard_map/ppermute | solution.py:548
  89.8 8.8 %collective-permute-start.21 = (f32[12,128]{1,0:T(8,128)S(1)}, f32[12,128]{1,0:T(8,128)S(1)}, u32[]{:S(2)}, u32[]{:S(2)}) collective-permute-start(f32[12,128]{1,0:T(8,128)S(1)} %get-tuple-element.95), channel_id=1, source_target_pairs={{0,31},{1,0},{2,1},{3,2},{4,3},{5,4},{6,5},{7,6},{8,7},{9,8},{10,9... | collective-permute-start | bytes 18440 | tf_op jit(solution)/shard_map/ppermute | solution.py:548
  94.6 4.7 %collective-permute-start.22 = (f32[12,128]{1,0:T(8,128)S(1)}, f32[12,128]{1,0:T(8,128)S(1)}, u32[]{:S(2)}, u32[]{:S(2)}) collective-permute-start(f32[12,128]{1,0:T(8,128)S(1)} %get-tuple-element.96), channel_id=1, source_target_pairs={{0,32},{32,64},{64,96},{96,128},{128,160},{160,192},{192,224},{224... | collective-permute-start | bytes 18440 | tf_op jit(solution)/shard_map/ppermute | solution.py:548
  94.6 4.9 %collective-permute-start.23 = (f32[12,128]{1,0:T(8,128)S(1)}, f32[12,128]{1,0:T(8,128)S(1)}, u32[]{:S(2)}, u32[]{:S(2)}) collective-permute-start(f32[12,128]{1,0:T(8,128)S(1)} %get-tuple-element.97), channel_id=1, source_target_pairs={{0,224},{32,0},{64,32},{96,64},{128,96},{160,128},{192,160},{224,1... | collective-permute-start | bytes 18440 | tf_op jit(solution)/shard_map/ppermute | solution.py:548
  100.2 22.0 %all-to-all-start = ((f32[256,1,128]{2,1,0:T(1,128)}), f32[256,1,128]{2,1,0:T(1,128)S(1)}, u32[]{:S(2)}, u32[]{:S(2)}) async-start(f32[256,1,128]{2,1,0:T(1,128)} %bitcast.1), calls=%async_computation | async-start | bytes 262144 | tf_op jit(solution)/shard_map/all_to_all | solution.py:644
where the time goes:
time: 124 us
  starting transfers between devices  58.2 us (47%)
  Pallas kernels  36.7 us (30%)
  waiting for transfers between devices  22.7 us (18%)
  local copies, waits for them, and re-layouts  4.71 us (4%)
  between operations  1.39 us (1%)
    ppermute x24, starting transfers between devices, exchange(): lax.ppermute(packets[side ^ 1], axis, [(i, (i + toward) % count) for i in...  49.3 us
    pallas_call x8, Pallas kernels, call(): pl.pallas_call(body, out_shape=[jax.ShapeDtypeStruct(shape, kind) for sha...  36.7 us
    all_to_all x1, waiting for transfers between devices, per_device(): sums = lax.all_to_all(sums, AXES, 0, 0, tiled=True)  12.4 us
    ppermute x24, waiting for transfers between devices, exchange(): lax.ppermute(packets[side ^ 1], axis, [(i, (i + toward) % count) for i in...  10.3 us
    all_to_all x1, starting transfers between devices, per_device(): sums = lax.all_to_all(sums, AXES, 0, 0, tiled=True)  8.95 us
    unnamed x7, local copies, waits for them, and re-layouts  3.43 us
  transfers between devices with their start and end apart: 25, of which 13 were waited for; matrix products, arithmetic and copies ran while one was open for 0% of the time, Pallas kernels for 0%

commit v1 on v0

--- a/solution.py
+++ b/solution.py
@@ -13,6 +13,7 @@
 NODE_ROWS = 16
 ITEM_ROWS = 64
 SIDES = 4
+PARTS = 3
 AXES = ("band", "sector")
 epsilon = 1e-06
 F32 = jnp.float32
@@ -129,7 +130,7 @@
     return keys
 
 
-def make_plan(conn_ref, send_ref, conn_out, key_out, scan_out, end_out, inverse_out, send_scratch):
+def plan_kernel(conn_ref, send_ref, conn_out, key_out, scan_out, end_out, inverse_out, send_scratch):
     for half in range(8):
         start = (half % 2) * LANES
         send_scratch[half : half + 1, :] = send_ref[0, 0, half // 2 : half // 2 + 1, start : start + LANES]
@@ -192,7 +193,7 @@
             sorted_ref[eight_at(register, ITEM_ROWS * channel), :] = values
         return 0
 
-    lax.fori_loop(0, 8, bring, 0)
+    lax.fori_loop(0, 8, bring, 0, unroll=True)
     nodes = [key_ref[8 * register : 8 * register + 8, :] >> 13 for register in range(8)]
     scan = scan_ref[...]
     follows = [(scan & (1 << step)) != 0 for step in range(len(SCAN_STEPS) + 1)]
@@ -220,7 +221,48 @@
             out_ref[eight_at(half, NODE_ROWS * channel), :] = values
         return 0
 
-    lax.fori_loop(0, 2, deliver, 0)
+    lax.fori_loop(0, 2, deliver, 0, unroll=True)
+
+
+def bf16_parts(values, count):
+    parts = []
+    for _ in range(count):
+        part = values.astype(jnp.bfloat16).astype(F32)
+        parts.append(part)
+        values = values - part
+    return parts
+
+
+def one_line(rows):
+    return jnp.concatenate([rows[k : k + 1] for k in range(8)], axis=1)
+
+
+def scatter_sums(term_ref, channels, conn_ref, out_ref):
+    width = 8 * LANES
+    row_ids = lax.broadcasted_iota(I32, (NODE_ROWS, width), 0).astype(F32)
+    lane_ids = lax.broadcasted_iota(I32, (LANES, width), 0).astype(F32)
+    total = jnp.zeros((channels * PARTS * NODE_ROWS, LANES), F32)
+    for chunk in range(CHUNKS):
+        ids = conn_ref[8 * chunk : 8 * chunk + 8, :]
+        in_row = one_line((ids >> 7).astype(F32)) == row_ids
+        in_lane = one_line((ids & (LANES - 1)).astype(F32)) == lane_ids
+        left = []
+        for channel in range(channels):
+            base = ITEM_ROWS * channel + 8 * chunk
+            for part in bf16_parts(one_line(term_ref[base : base + 8, :]), PARTS):
+                left.append(jnp.where(in_row, part, 0.0).astype(jnp.bfloat16))
+        total = total + lax.dot_general(
+            jnp.concatenate(left, axis=0),
+            jnp.where(in_lane, 1.0, 0.0).astype(jnp.bfloat16),
+            (((1,), (1,)), ((), ())),
+            preferred_element_type=F32,
+        )
+    for channel in range(channels):
+        base = PARTS * NODE_ROWS * channel
+        out = total[base : base + NODE_ROWS]
+        for part in range(1, PARTS):
+            out = out + total[base + part * NODE_ROWS : base + (part + 1) * NODE_ROWS]
+        out_ref[NODE_ROWS * channel : NODE_ROWS * (channel + 1), :] = out
 
 
 def node_picks(table_ref, channels, conn_ref, chunk):
@@ -228,24 +270,28 @@
     return table_picks(tables, NODE_ROWS, conn_ref[eight_at(chunk), :])
 
 
-def measure_blocks(blocks_ref, row_ref, scale_ref, conn_ref, term_ref, max_ref):
-    def one(chunk, _):
-        scales = node_picks(scale_ref, 3, conn_ref, chunk)
+def row_maxima(blocks_ref, picked, at, max_ref):
+    for r in range(STRAINS):
+        sized = [jnp.abs(blocks_ref[0, 0, r, 8 * c : 8 * c + 8, at]) for c in range(3)]
+        for k, scales in enumerate(picked):
+            whole = sized[0] * scales[0]
+            for c in range(1, 3):
+                whole = jnp.maximum(whole, sized[c] * scales[c])
+            max_ref[STRAINS * k + r : STRAINS * k + r + 1, at] = jnp.max(whole, axis=0, keepdims=True)
+
+
+def column_maxima(blocks_ref, row_ref, term_ref, first_channel):
+    for chunk in range(CHUNKS):
+        at = slice(chunk * LANES, (chunk + 1) * LANES)
         best = [jnp.zeros((8, LANES), F32)] * 3
-        at = chunk_at(chunk)
         for r in range(STRAINS):
-            sized = [
-                jnp.abs(blocks_ref[0, 0, r, 8 * c : 8 * c + 8, at]) * scales[c] for c in range(3)
-            ]
-            whole = jnp.maximum(jnp.maximum(sized[0], sized[1]), sized[2])
-            max_ref[r : r + 1, at] = jnp.max(whole, axis=0, keepdims=True)
-            row = row_ref[r : r + 1, at]
-            best = [jnp.maximum(best[c], sized[c] * row) for c in range(3)]
+            row = 1.0 if row_ref is None else row_ref[r : r + 1, at]
+            for c in range(3):
+                size = jnp.abs(blocks_ref[0, 0, r, 8 * c : 8 * c + 8, at]) * row
+                best[c] = jnp.maximum(best[c], size)
         for c in range(3):
-            term_ref[eight_at(chunk, ITEM_ROWS * c), :] = best[c]
-        return 0
-
-    lax.fori_loop(0, CHUNKS, one, 0)
+            base = ITEM_ROWS * (first_channel + c) + 8 * chunk
+            term_ref[base : base + 8, :] = best[c]
 
 
 def apply_blocks(blocks_ref, table_ref, sets, conn_ref, strain_ref):
@@ -262,7 +308,7 @@
                 )
         return 0
 
-    lax.fori_loop(0, CHUNKS, one, 0)
+    lax.fori_loop(0, CHUNKS, one, 0, unroll=True)
 
 
 def apply_transpose(blocks_ref, strain_ref, sets, term_ref):
@@ -279,39 +325,60 @@
             term_ref[eight_at(chunk, ITEM_ROWS * channel), :] = totals[channel]
         return 0
 
-    lax.fori_loop(0, CHUNKS, one, 0)
+    lax.fori_loop(0, CHUNKS, one, 0, unroll=True)
+
+
+def even_places():
+    return lax.axis_index("sector") % 2 == 0, lax.axis_index("band") % 2 == 0
+
+
+def side_rows(part_ref, side, channel, length=2):
+    base = NODE_ROWS * channel + 2 * side
+    return part_ref[base : base + length, :]
 
 
 def pack(part_ref, channels, packet_refs):
+    even_sector, even_band = even_places()
+    for slot, (even, low, high) in enumerate(
+        ((even_sector, 1, 0), (even_band, 3, 2), (even_sector, 0, 1), (even_band, 2, 3))
+    ):
+        for channel in range(channels):
+            for part in range(2):
+                packet_refs[slot][4 * channel + 2 * part : 4 * channel + 2 * part + 2, :] = jnp.where(
+                    even,
+                    side_rows(part_ref, high + 4 * part, channel),
+                    side_rows(part_ref, low + 4 * part, channel),
+                )
+
+
+def by_side(arrived_refs):
+    even_sector, even_band = even_places()
+    odd_cycle, odd_band, even_cycle, even_pair = [ref[...] for ref in arrived_refs]
+    below, above = live_sides()
+    return [
+        jnp.where(even_sector, odd_cycle, even_cycle),
+        jnp.where(even_sector, even_cycle, odd_cycle),
+        jnp.where(below, jnp.where(even_band, odd_band, even_pair), 0.0),
+        jnp.where(above, jnp.where(even_band, even_pair, odd_band), 0.0),
+    ]
+
+
+def live_sides():
+    band = lax.axis_index("band")
+    return [band > 0, band < lax.axis_size("band") - 1]
+
+
+def unpack(part_ref, channels, arrived, merge, out_ref):
     for side in range(SIDES):
         for channel in range(channels):
             base = NODE_ROWS * channel + 2 * side
-            packet_refs[side][4 * channel : 4 * channel + 2, :] = part_ref[base : base + 2, :]
-            packet_refs[side][4 * channel + 2 : 4 * channel + 4, :] = part_ref[base + 8 : base + 10, :]
-
-
-def live_sides():
-    band = lax.axis_index("band")
-    return [None, None, band > 0, band < lax.axis_size("band") - 1]
-
-
-def unpack(part_ref, channels, arrived_refs, merge, out_ref, groups=True):
-    live = live_sides()
-    for side in range(SIDES):
-        for channel in range(channels):
-            base = NODE_ROWS * channel + 2 * side
-            theirs = arrived_refs[side][4 * channel + 2 : 4 * channel + 4, :]
-            if live[side] is not None:
-                theirs = jnp.where(live[side], theirs, 0.0)
-            out_ref[base : base + 2, :] = merge(part_ref[base : base + 2, :], theirs)
-            if groups:
-                theirs = arrived_refs[side][4 * channel : 4 * channel + 2, :]
-                if live[side] is not None:
-                    theirs = jnp.where(live[side], theirs, 0.0)
-                out_ref[base + 8 : base + 10, :] = merge(part_ref[base + 8 : base + 10, :], theirs)
+            theirs = arrived[side][4 * channel : 4 * channel + 4]
+            out_ref[base : base + 2, :] = merge(part_ref[base : base + 2, :], theirs[2:4])
+            out_ref[base + 8 : base + 10, :] = merge(part_ref[base + 8 : base + 10, :], theirs[0:2])
 
 
 def rescale(scale, peak):
+    peak = scale * peak
     seen = peak > 0.0
     return jnp.where(seen, scale / jnp.sqrt(jnp.where(seen, peak, 1.0)), 0.0)
 
@@ -333,73 +400,65 @@
 
 
 def start_kernel(
-    blocks_ref,
-    conn_ref,
-    send_ref,
-    loads_ref,
-    conn_out,
-    key_out,
-    scan_out,
-    end_out,
-    inverse_out,
-    row_out,
-    scale_out,
-    part_out,
-    own_loads_out,
-    *rest,
+    blocks_ref, ids_ref, loads_ref, send_ref, key_ref, scan_ref, end_ref, row_out, part_out, loads_out, *rest
 ):
-    packets, (send_ids, term, items, peaks, ones) = rest[:4], rest[4:]
-    make_plan(conn_ref, send_ref, conn_out, key_out, scan_out, end_out, inverse_out, send_ids)
+    packets, (term, items, peaks) = rest[:4], rest[4:]
+    below, above = [live.astype(F32) for live in live_sides()]
+    for chunk in range(CHUNKS):
+        at = slice(chunk * LANES, (chunk + 1) * LANES)
+        ids = ids_ref[0, 0, :, at]
+        scale = jnp.where(ids < 1536, 1.0, jnp.where(ids < 1792, below, above))
+        row_maxima(blocks_ref, [[scale] * 3], at, peaks)
+    row_out[...] = 1.0 / jnp.sqrt(peaks[...])
+    column_maxima(blocks_ref, None, term, 0)
+    column_maxima(blocks_ref, row_out, term, 3)
+    scatter_items(term, 6, (key_ref, scan_ref, end_ref), items, part_out, jnp.maximum)
+    pack(part_out, 6, packets)
+    tables = [rows_of(loads_ref, 8 * c) for c in range(3)]
+    for c, values in enumerate(table_picks(tables, 8, send_ref[...])):
+        loads_out[8 * c : 8 * c + 8, :] = values
+    even_sector, even_band = even_places()
+    for slot, (even, low, high) in enumerate(
+        ((even_sector, 1, 0), (even_band, 3, 2), (even_sector, 0, 1), (even_band, 2, 3))
+    ):
+        for c in range(3):
+            packets[slot][24 + 2 * c : 26 + 2 * c, :] = jnp.where(
+                even,
+                loads_out[8 * c + 2 * high : 8 * c + 2 * high + 2, :],
+                loads_out[8 * c + 2 * low : 8 * c + 2 * low + 2, :],
+            )
+
+
+def sweep_kernel(
+    blocks_ref, conn_ref, key_ref, scan_ref, end_ref, row_ref, part_ref, own_loads, *rest
+):
+    arrived, rest = by_side(rest[:4]), rest[4:]
+    row_out, scale_out, part_out, loads_out, rest = rest[0], rest[1], rest[2], rest[3], rest[4:]
+    packets, (term, items, peaks, merged, second_row) = rest[:4], rest[4:]
+    unpack(part_ref, 6, arrived, jnp.maximum, merged)
+    for c in range(3):
+        loads_out[NODE_ROWS * c : NODE_ROWS * c + 8, :] = own_loads[8 * c : 8 * c + 8, :]
+        for side in range(SIDES):
+            base = NODE_ROWS * c + 8 + 2 * side
+            loads_out[base : base + 2, :] = arrived[side][24 + 2 * c : 26 + 2 * c]
     row = lax.broadcasted_iota(I32, (NODE_ROWS, LANES), 0)
-    below, above = live_sides()[2:]
-    first = jnp.where(row < 12, 1.0, jnp.where(row < 14, below.astype(F32), above.astype(F32)))
+    below, above = [live.astype(F32) for live in live_sides()]
+    start = jnp.where(row < 12, 1.0, jnp.where(row < 14, below, above))
     for c in range(3):
-        scale_out[NODE_ROWS * c : NODE_ROWS * (c + 1), :] = first
-    ones[...] = jnp.ones_like(ones)
-    measure_blocks(blocks_ref, ones, scale_out, conn_out, term, peaks)
-    row_out[...] = 1.0 / jnp.sqrt(peaks[...])
-    scatter_items(term, 3, (key_out, scan_out, end_out), items, part_out, jnp.maximum)
-    pack(part_out, 3, packets)
-    tables = [
-        lambda r, c=c: loads_ref[0, 0, c : c + 1, r * LANES : (r + 1) * LANES] for c in range(3)
-    ]
-    for c, values in enumerate(table_picks(tables, 8, send_ids[...])):
-        own_loads_out[8 * c : 8 * c + 8, :] = values
-        for side in range(SIDES):
-            packets[side][12 + 2 * c : 14 + 2 * c, :] = own_loads_out[
-                8 * c + 2 * side : 8 * c + 2 * side + 2, :
-            ]
-
-
-def sweep_kernel(
-    with_loads,
-    blocks_ref,
-    conn_ref,
-    key_ref,
-    scan_ref,
-    end_ref,
-    row_ref,
-    scale_ref,
-    part_ref,
-    *rest,
-):
-    arrived, rest = rest[:4], rest[4:]
-    if with_loads:
-        own_loads, rest = rest[0], rest[1:]
-    row_out, scale_out, part_out, rest = rest[0], rest[1], rest[2], rest[3:]
-    if with_loads:
-        loads_out, rest = rest[0], rest[1:]
-    packets, (term, items, peaks, merged) = rest[:4], rest[4:]
-    unpack(part_ref, 3, arrived, jnp.maximum, merged)
-    scale_out[...] = rescale(scale_ref[...], merged[...])
-    if with_loads:
-        for c in range(3):
-            loads_out[NODE_ROWS * c : NODE_ROWS * c + 8, :] = own_loads[8 * c : 8 * c + 8, :]
-            for side in range(SIDES):
-                base = NODE_ROWS * c + 8 + 2 * side
-                loads_out[base : base + 2, :] = arrived[side][12 + 2 * c : 14 + 2 * c, :]
-    measure_blocks(blocks_ref, row_ref, scale_out, conn_ref, term, peaks)
-    row_out[...] = row_ref[...] / jnp.sqrt(row_ref[...] * peaks[...])
+        first = rescale(start, merged[NODE_ROWS * c : NODE_ROWS * (c + 1), :])
+        later = NODE_ROWS * (c + 3)
+        second = rescale(first, merged[later : later + NODE_ROWS, :])
+        merged[NODE_ROWS * c : NODE_ROWS * (c + 1), :] = first
+        merged[later : later + NODE_ROWS, :] = second
+        scale_out[NODE_ROWS * c : NODE_ROWS * (c + 1), :] = second
+    for chunk in range(CHUNKS):
+        at = slice(chunk * LANES, (chunk + 1) * LANES)
+        scales = node_picks(merged, 6, conn_ref, chunk)
+        row_maxima(blocks_ref, [scales[0:3], scales[3:6]], at, peaks)
+    first_row = row_ref[...]
+    second_row[...] = first_row / jnp.sqrt(first_row * peaks[0:STRAINS, :])
+    row_out[...] = second_row[...] / jnp.sqrt(second_row[...] * peaks[STRAINS : 2 * STRAINS, :])
+    column_maxima(blocks_ref, second_row, term, 0)
     scatter_items(term, 3, (key_ref, scan_ref, end_ref), items, part_out, jnp.maximum)
     pack(part_out, 3, packets)
 
@@ -407,9 +466,6 @@
 def target_kernel(
     blocks_ref,
     conn_ref,
-    key_ref,
-    scan_ref,
-    end_ref,
     row_ref,
     scale_ref,
     part_ref,
@@ -418,7 +474,8 @@
 ):
     arrived, rest = rest[:4], rest[4:]
     scale_out, strain_out, part_out, rest = rest[0], rest[1], rest[2], rest[3:]
-    packets, (term, items, table, strain, cones) = rest[:4], rest[4:]
+    packets, (term, table, strain, cones) = rest[:4], rest[4:]
+    arrived = by_side(arrived)
     unpack(part_ref, 3, arrived, jnp.maximum, table)
     scale = rescale(scale_ref[...], table[...])
     scale_out[...] = scale
@@ -432,18 +489,19 @@
     strain[STRAINS : 2 * STRAINS, :] = row * cones[...]
     strain_out[...] = 3.0 * image + 2.0 * cones[...]
     apply_transpose(blocks_ref, strain, 2, term)
-    scatter_items(term, 6, (key_ref, scan_ref, end_ref), items, part_out, jnp.add)
+    scatter_sums(term, 6, conn_ref, part_out)
     part_out[0:48, :] = part_out[0:48, :] * scale
     part_out[48:96, :] = part_out[48:96, :] * scale
     pack(part_out, 6, packets)
 
 
 def second_kernel(
-    blocks_ref, conn_ref, key_ref, scan_ref, end_ref, row_ref, scale_ref, part_ref, *rest
+    blocks_ref, conn_ref, row_ref, scale_ref, part_ref, *rest
 ):
     arrived, rest = rest[:4], rest[4:]
     joint_out, strain_out, part_out, rest = rest[0], rest[1], rest[2], rest[3:]
-    packets, (term, items, table, strain) = rest[:4], rest[4:]
+    packets, (term, table, strain) = rest[:4], rest[4:]
+    arrived = by_side(arrived)
     unpack(part_ref, 6, arrived, jnp.add, table)
     joint_out[...] = table[48:96, :]
     scale = scale_ref[...]
@@ -454,7 +512,7 @@
     strain_out[...] = row * strain[STRAINS : 2 * STRAINS, :]
     strain[0:STRAINS, :] = row * (row * strain[0:STRAINS, :])
     apply_transpose(blocks_ref, strain, 1, term)
-    scatter_items(term, 3, (key_ref, scan_ref, end_ref), items, part_out, jnp.add)
+    scatter_sums(term, 3, conn_ref, part_out)
     part_out[...] = part_out[...] * scale
     pack(part_out, 3, packets)
 
@@ -468,12 +526,11 @@
 
 
 def third_kernel(
-    blocks_ref, conn_ref, key_ref, scan_ref, end_ref, row_ref, scale_ref, part_ref, *rest
+    blocks_ref, conn_ref, row_ref, scale_ref, part_ref, *rest
 ):
     arrived, rest = rest[:4], rest[4:]
-    norm_out, part_out, rest = rest[0], rest[1], rest[2:]
-    packets, (term, items, table, strain) = rest[:4], rest[4:]
-    unpack(part_ref, 3, arrived, jnp.add, table)
+    norm_out, part_out, right_out, above_out, term, table, strain = rest
+    unpack(part_ref, 3, by_side(arrived), jnp.add, table)
     norm_out[...] = own_square(table)
     scale = scale_ref[...]
     table[...] = scale * table[...]
@@ -481,18 +538,31 @@
     row = row_ref[...]
     strain[...] = row * (row * strain[...])
     apply_transpose(blocks_ref, strain, 1, term)
-    scatter_items(term, 3, (key_ref, scan_ref, end_ref), items, part_out, jnp.add)
+    scatter_sums(term, 3, conn_ref, part_out)
     part_out[...] = part_out[...] * scale
-    pack(part_out, 3, packets)
+    for packet, side in ((right_out, 1), (above_out, 3)):
+        for channel in range(3):
+            packet[4 * channel : 4 * channel + 2, :] = side_rows(part_out, side, channel)
+            packet[4 * channel + 2 : 4 * channel + 4, :] = side_rows(part_out, side + 4, channel)
 
 
 def norm_kernel(
-    part_ref, norm_ref, scale_ref, loads_ref, joint_ref, inverse_ref, *rest
+    part_ref, norm_ref, scale_ref, loads_ref, joint_ref, inverse_ref, left_ref, below_ref, *rest
 ):
-    arrived, (sums_out, velocity_out, table, lines) = rest[:4], rest[4:]
-    unpack(part_ref, 3, arrived, jnp.add, table, groups=False)
+    sums_out, velocity_out, lines = rest
+    below, above = live_sides()
+    squares = jnp.zeros((2, LANES), F32)
+    for channel in range(3):
+        for side, arrived, live in ((0, left_ref, True), (2, below_ref, below)):
+            theirs = arrived[4 * channel : 4 * channel + 4, :]
+            theirs = jnp.where(live, theirs, 0.0)
+            own = side_rows(part_ref, side, channel) + theirs[2:4]
+            copy = side_rows(part_ref, side + 4, channel) + theirs[0:2]
+            squares = squares + own * own + copy * copy
+        alone = jnp.where(above, 0.0, side_rows(part_ref, 3, channel))
+        squares = squares + alone * alone
     first = jnp.sum(norm_ref[...], axis=1, keepdims=True)
-    last = jnp.sum(own_square(table), axis=1, keepdims=True)
+    last = jnp.sum(jnp.sum(squares, axis=0, keepdims=True), axis=1, keepdims=True)
     lane = lax.broadcasted_iota(I32, (1, LANES), 1)
     line = jnp.where(lane == 0, first, jnp.where(lane == 1, last, 0.0))
     sums_out[...] = jnp.broadcast_to(line, sums_out.shape)
@@ -503,13 +573,13 @@
         lines[24 + 8 * c : 32 + 8 * c, :] = scale * joint_ref[base : base + 8, :]
     tables = [rows_of(lines, 8 * channel) for channel in range(6)]
     for channel, values in enumerate(table_picks(tables, 8, inverse_ref[...])):
-        for r in range(8):
-            velocity_out[channel : channel + 1, r * LANES : (r + 1) * LANES] = values[r : r + 1, :]
+        velocity_out[8 * channel : 8 * channel + 8, :] = values
 
 
 def final_kernel(
-    sums_ref, step_ref, velocity_ref, base_ref, joint_ref, row_ref, velocity_out, multiplier_out, cones
+    sums_ref, step_ref, velocity_ref, base_ref, joint_ref, row_ref, velocity_out, multiplier_out, *rest
 ):
+    velocity, cones, flat, semaphores = rest
     sums = jnp.sum(sums_ref[...], axis=0, keepdims=True)
     lane = lax.broadcasted_iota(I32, (1, LANES), 1)
     before = jnp.sum(jnp.where(lane == 0, sums, 0.0), axis=1, keepdims=True)
@@ -517,36 +587,58 @@
     largest = jnp.sqrt(after + epsilon) / jnp.sqrt(before + epsilon)
     step = step_ref[0] / jnp.sqrt(largest)
     square = step * step
-    target = velocity_ref[0:3, :]
-    joint = velocity_ref[3:6, :]
-    velocity_out[0, 0] = (2.0 * step) * (square * joint - target)
+    velocity[...] = (2.0 * step) * (square * velocity_ref[24:48, :] - velocity_ref[0:24, :])
+    first = pltpu.make_async_copy(velocity, velocity_out, semaphores.at[0])
+    first.start()
     cones[...] = square * (base_ref[...] - (4.0 * square) * joint_ref[...])
     project_rows(cones)
-    multiplier_out[0, 0] = row_ref[...] * cones[...]
-
-
-def call(body, out_shapes, scratch, *arrays, smem=()):
-    specs = [
-        pl.BlockSpec(memory_space=pltpu.SMEM if i in smem else pltpu.VMEM) for i in range(len(arrays))
-    ]
+    cones[...] = row_ref[...] * cones[...]
+    for r in range(STRAINS):
+        for chunk in range(CHUNKS):
+            flat[8 * r + chunk : 8 * r + chunk + 1, :] = cones[
+                r : r + 1, chunk * LANES : (chunk + 1) * LANES
+            ]
+    second = pltpu.make_async_copy(flat, multiplier_out, semaphores.at[1])
+    second.start()
+    first.wait()
+    second.wait()
+
+
+def call(body, out_shapes, scratch, *arrays, smem=(), outside_results=False, work=0):
+    def space(i):
+        return pltpu.SMEM if i in smem else pltpu.VMEM
+
+    result = pltpu.HBM if outside_results else pltpu.VMEM
     return pl.pallas_call(
         body,
         out_shape=[jax.ShapeDtypeStruct(shape, kind) for shape, kind in out_shapes],
-        in_specs=specs,
-        out_specs=[pl.BlockSpec(memory_space=pltpu.VMEM) for _ in out_shapes],
-        scratch_shapes=[pltpu.VMEM(shape, kind) for shape, kind in scratch],
+        in_specs=[pl.BlockSpec(memory_space=space(i)) for i in range(len(arrays))],
+        out_specs=[pl.BlockSpec(memory_space=result) for _ in out_shapes],
+        scratch_shapes=[
+            entry if not isinstance(entry, tuple) else pltpu.VMEM(*entry) for entry in scratch
+        ],
+        cost_estimate=pl.CostEstimate(flops=work, bytes_accessed=work // 256, transcendentals=0),
         compiler_params=pltpu.CompilerParams(vmem_limit_bytes=24 * 1024 * 1024),
     )(*arrays)
 
 
+def swap_pairs(axis, odd):
+    count = lax.axis_size(axis)
+    return [(i, (((i - odd) ^ 1) + odd) % count) for i in range(count)]
+
+
+PAIRS = (("sector", 1), ("band", 1), ("sector", 0), ("band", 0))
+
+
 def exchange(packets):
-    arrived = []
-    for side, packet in enumerate(packets):
-        axis = "sector" if side < 2 else "band"
-        count = lax.axis_size(axis)
-        toward = 1 if side % 2 == 0 else -1
-        arrived.append(lax.ppermute(packets[side ^ 1], axis, [(i, (i + toward) % count) for i in range(count)]))
-    return arrived
+    return [
+        lax.ppermute(packet, axis, swap_pairs(axis, odd)) for packet, (axis, odd) in zip(packets, PAIRS)
+    ]
+
+
+def shift_up(packet, axis):
+    count = lax.axis_size(axis)
+    return lax.ppermute(packet, axis, [(i, (i + 1) % count) for i in range(count)])
 
 
 def per_device(blocks, connectivity, send_lists, nodal_loads, step_scale):
@@ -554,54 +646,49 @@
     nodes = ((48, LANES), F32)
     rows = ((STRAINS, 1024), F32)
     items = ((3 * ITEM_ROWS, LANES), F32)
-    (conn, key, scan, end, inverse, row, scale, part, own_loads, *packets) = call(
+    twice = ((6 * ITEM_ROWS, LANES), F32)
+    ids = ((64, LANES), I32)
+    few = ((8, LANES), I32)
+    conn, key, scan, end, inverse, send = call(
+        plan_kernel,
+        [ids, ids, few, ((16, LANES), I32), few, few],
+        [],
+        connectivity,
+        send_lists,
+        work=4_000_000_000,
+    )
+    row, part, own_loads, *packets = call(
         start_kernel,
-        [
-            ((64, LANES), I32),
-            ((64, LANES), I32),
-            ((8, LANES), I32),
-            ((16, LANES), I32),
-            ((8, LANES), I32),
-            rows,
-            nodes,
-            nodes,
-            ((24, LANES), F32),
-        ]
-        + [((18, LANES), F32)] * 4,
-        [((8, LANES), I32), items, items, rows, rows],
+        [rows, ((96, LANES), F32), ((24, LANES), F32)] + [((30, LANES), F32)] * 4,
+        [twice, twice, rows],
         blocks,
         connectivity,
-        send_lists,
-        nodal_loads,
-    )
-    plan = (blocks, conn, key, scan, end)
+        nodal_loads.reshape(24, LANES),
+        send,
+        key,
+        scan,
+        end,
+    )
     row, scale, part, loads, *packets = call(
-        functools.partial(sweep_kernel, True),
+        sweep_kernel,
         [rows, nodes, nodes, nodes] + packet,
-        [items, items, rows, nodes],
-        *plan,
+        [items, items, ((2 * STRAINS, 1024), F32), ((96, LANES), F32), rows],
+        blocks,
+        conn,
+        key,
+        scan,
+        end,
         row,
-        scale,
         part,
+        own_loads,
         *exchange(packets),
-        own_loads,
-    )
-    row, scale, part, *packets = call(
-        functools.partial(sweep_kernel, False),
-        [rows, nodes, nodes] + packet,
-        [items, items, rows, nodes],
-        *plan,
-        row,
-        scale,
-        part,
-        *exchange(packets),
-    )
-    twice = ((6 * ITEM_ROWS, LANES), F32)
+    )
     scale, base, part, *packets = call(
         target_kernel,
         [nodes, rows, ((96, LANES), F32)] + [((24, LANES), F32)] * 4,
-        [twice, twice, nodes, ((2 * STRAINS, 1024), F32), rows],
-        *plan,
+        [twice, nodes, ((2 * STRAINS, 1024), F32), rows],
+        blocks,
+        conn,
         row,
         scale,
         part,
@@ -611,18 +698,20 @@
     joint, image, part, *packets = call(
         second_kernel,
         [nodes, rows, nodes] + packet,
-        [items, items, ((96, LANES), F32), ((2 * STRAINS, 1024), F32)],
-        *plan,
+        [items, ((96, LANES), F32), ((2 * STRAINS, 1024), F32)],
+        blocks,
+        conn,
         row,
         scale,
         part,
         *exchange(packets),
     )
-    norm, part, *packets = call(
+    norm, part, right, above = call(
         third_kernel,
-        [((1, LANES), F32), nodes] + packet,
-        [items, items, nodes, rows],
-        *plan,
+        [((1, LANES), F32), nodes] + packet[:2],
+        [items, nodes, rows],
+        blocks,
+        conn,
         row,
         scale,
         part,
@@ -631,31 +720,32 @@
     count = lax.axis_size("band") * lax.axis_size("sector")
     sums, lines = call(
         norm_kernel,
-        [((count, LANES), F32), ((6, 1024), F32)],
-        [nodes, nodes],
+        [((count, LANES), F32), ((48, LANES), F32)],
+        [nodes],
         part,
         norm,
         scale,
         loads,
         joint,
         inverse,
-        *exchange(packets),
+        shift_up(right, "sector"),
+        shift_up(above, "band"),
     )
     sums = lax.all_to_all(sums, AXES, 0, 0, tiled=True)
-    return tuple(
-        call(
-            final_kernel,
-            [((1, 1, 3, 1024), F32), ((1, 1, STRAINS, 1024), F32)],
-            [rows],
-            sums,
-            step_scale,
-            lines,
-            base,
-            image,
-            row,
-            smem=(1,),
-        )
-    )
+    velocities, multipliers = call(
+        final_kernel,
+        [((24, LANES), F32), ((96, LANES), F32)],
+        [((24, LANES), F32), rows, ((96, LANES), F32), pltpu.SemaphoreType.DMA((2,))],
+        sums,
+        step_scale,
+        lines,
+        base,
+        image,
+        row,
+        smem=(1,),
+        outside_results=True,
+    )
+    return velocities.reshape(1, 1, 3, 1024), multipliers.reshape(1, 1, STRAINS, 1024)
 
 
 def solution(mesh):

time: 124 us -> 88.8 us (0.72)
  starting transfers between devices: 58.2 us -> 34.8 us
  Pallas kernels: 36.7 us -> 24 us
  waiting for transfers between devices: 22.7 us -> 26.8 us
  local copies, waits for them, and re-layouts: 4.71 us -> 1.54 us
    ppermute x24 -> x18, starting transfers between devices: 49.3 us -> 26.8 us  [the longest x16 25.2 us: exchange(): lax.ppermute(packet, axis, swap_pairs(axis, odd))]
    pallas_call x8, Pallas kernels: 36.7 us -> 24 us  [call(): pl.pallas_call(body, out_shape=[jax.ShapeDtypeStruct(shape, kind) for sha...]
    ppermute x24 -> x18, waiting for transfers between devices: 10.3 us -> 14.3 us  [the longest x16 9.91 us: exchange(): lax.ppermute(packet, axis, swap_pairs(axis, odd))]
    unnamed x7 -> x8, local copies, waits for them, and re-layouts: 3.43 us -> 1.54 us
    pallas_call x2 -> x0, local copies, waits for them, and re-layouts: 1.28 us -> none  [call(): pl.pallas_call(body, out_shape=[jax.ShapeDtypeStruct(shape, kind) for sha...]
  transfers between devices with their start and end apart: 25 -> 19, of which waited for: 13 -> 9; matrix products, arithmetic and copies ran while one was open for 0% -> 0% of each run, Pallas kernels for 0% -> 0%
where the time goes in v1:
time: 88.8 us; the launch traced here: 88.7 us
  starting transfers between devices  34.8 us (39%)
  waiting for transfers between devices  26.8 us (30%)
  Pallas kernels  24 us (27%)
  local copies, waits for them, and re-layouts  1.54 us (2%)
  between operations  1.52 us (2%)
    ppermute x16, starting transfers between devices, exchange(): lax.ppermute(packet, axis, swap_pairs(axis, odd))  25.2 us
    pallas_call x8, Pallas kernels, call(): pl.pallas_call(body, out_shape=[jax.ShapeDtypeStruct(shape, kind) for sha...  24 us
    all_to_all x1, waiting for transfers between devices, per_device(): sums = lax.all_to_all(sums, AXES, 0, 0, tiled=True)  12.5 us
    ppermute x16, waiting for transfers between devices, exchange(): lax.ppermute(packet, axis, swap_pairs(axis, odd))  9.91 us
    all_to_all x1, starting transfers between devices, per_device(): sums = lax.all_to_all(sums, AXES, 0, 0, tiled=True)  8.03 us
    ppermute x2, waiting for transfers between devices, shift_up(): lax.ppermute(packet, axis, [(i, (i + 1) % count) for i in range(count)])  4.36 us
  transfers between devices with their start and end apart: 19, of which 9 were waited for; matrix products, arithmetic and copies ran while one was open for 0% of the time, Pallas kernels for 0%

profile of v1, /device:TPU:1, one launch (start us, length us, event | category | flops | bytes accessed | tf_op | source)
XLA Modules:
  0.0 88.7 jit_solution(14176742945783179215)
XLA Ops:
  0.7 0.8 copy-done.1
  1.5 0.7 copy-done.3
  2.2 3.3 %shard_map.68 = (s32[64,128]{1,0:T(8,128)S(1)}, s32[64,128]{1,0:T(8,128)S(1)}, s32[8,128]{1,0:T(8,128)S(1)}, s32[16,128]{1,0:T(8,128)S(1)}, s32[8,128]{1,0:T(8,128)S(1)}, /*index=5*/s32[8,128]{1,0:T(8,128)S(1)}) custom-call(s32[1,1,8,1024]{3,2,1,0:T(8,128)S(1)} %copy-done.1, s32[1,1,4,256]{3,2,1,0:T(4,128)S(1)} %copy-done.3), custom_call_target="tpu_custom_call" | custom-call | flops 4000000000 | bytes 15625000 | tf_op jit(solution)/shard_map/pallas_call | solution.py:612
  5.5 8.3 %shard_map.69 = (f32[12,1024]{1,0:T(8,128)S(1)}, f32[96,128]{1,0:T(8,128)S(1)}, f32[24,128]{1,0:T(8,128)S(1)}, f32[30,128]{1,0:T(8,128)S(1)}, f32[30,128]{1,0:T(...) custom-call(f32[1,1,12,24,1024]{4,3,2,1,0:T(8,128)S(1)} %copy-done, s32[1,1,8,1024]{3,2,1,0:T(8,128)S(1)} %copy-done.1, ...), custom_call_target="tpu_custom_call" | custom-call | tf_op jit(solution)/shard_map/pallas_call | solution.py:612
  13.9 8.7 %collective-permute-start = (f32[30,128]{1,0:T(8,128)S(1)}, f32[30,128]{1,0:T(8,128)S(1)}, u32[]{:S(2)}, u32[]{:S(2)}) collective-permute-start(f32[30,128]{1,0:T(8,128)S(1)} %get-tuple-element.53), channel_id=1, source_target_pairs={{0,31},{1,2},{2,1},{3,4},{4,3},{5,6},{6,5},{7,8},{8,7},{9,10},{10,... | collective-permute-start | bytes 46088 | tf_op jit(solution)/shard_map/ppermute | solution.py:635
  22.5 2.1 %collective-permute-start.1 = (f32[30,128]{1,0:T(8,128)S(1)}, f32[30,128]{1,0:T(8,128)S(1)}, u32[]{:S(2)}, u32[]{:S(2)}) collective-permute-start(f32[30,128]{1,0:T(8,128)S(1)} %get-tuple-element.54), channel_id=1, source_target_pairs={{0,224},{32,64},{64,32},{96,128},{128,96},{160,192},{192,160},{224... | collective-permute-start | bytes 46088 | tf_op jit(solution)/shard_map/ppermute | solution.py:635
  24.7 0.0 collective-permute-start.2
  24.7 1.0 %collective-permute-start.3 = (f32[30,128]{1,0:T(8,128)S(1)}, f32[30,128]{1,0:T(8,128)S(1)}, u32[]{:S(2)}, u32[]{:S(2)}) collective-permute-start(f32[30,128]{1,0:T(8,128)S(1)} %get-tuple-element.56), channel_id=1, source_target_pairs={{0,32},{32,0},{64,96},{96,64},{128,160},{160,128},{192,224},{224,1... | collective-permute-start | bytes 46088 | tf_op jit(solution)/shard_map/ppermute | solution.py:635
  25.7 0.0 collective-permute-done.rest_0_
  25.7 0.4 collective-permute-done.1.rest_1_
  26.1 1.4 %collective-permute-done.2.rest_2_ = f32[30,128]{1,0:T(8,128)S(1)} collective-permute-done((f32[30,128]{1,0:T(8,128)S(1)}, f32[30,128]{1,0:T(8,128)S(1)}, u32[]{:S(2)}, u32[]{:S(2)}) %collective-permute-start.2) | collective-permute-done | bytes 15392 | tf_op jit(solution)/shard_map/ppermute | solution.py:635
  27.5 0.0 collective-permute-done.3.rest_3_
  27.5 5.1 %shard_map.70 = (f32[12,1024]{1,0:T(8,128)S(1)}, f32[48,128]{1,0:T(8,128)S(1)}, f32[48,128]{1,0:T(8,128)S(1)}, f32[48,128]{1,0:T(8,128)S(1)}, f32[12,128]{1,0:T(...) custom-call(f32[1,1,12,24,1024]{4,3,2,1,0:T(8,128)S(1)} %copy-done, ...), custom_call_target="tpu_custom_call" | custom-call | tf_op jit(solution)/shard_map/pallas_call | solution.py:612
  32.6 1.1 %collective-permute-start.4 = (f32[12,128]{1,0:T(8,128)S(1)}, f32[12,128]{1,0:T(8,128)S(1)}, u32[]{:S(2)}, u32[]{:S(2)}) collective-permute-start(f32[12,128]{1,0:T(8,128)S(1)} %get-tuple-element.61), channel_id=1, source_target_pairs={{0,31},{1,2},{2,1},{3,4},{4,3},{5,6},{6,5},{7,8},{8,7},{9,10},{10,... | collective-permute-start | bytes 18440 | tf_op jit(solution)/shard_map/ppermute | solution.py:635
  33.6 3.3 %collective-permute-start.5 = (f32[12,128]{1,0:T(8,128)S(1)}, f32[12,128]{1,0:T(8,128)S(1)}, u32[]{:S(2)}, u32[]{:S(2)}) collective-permute-start(f32[12,128]{1,0:T(8,128)S(1)} %get-tuple-element.62), channel_id=1, source_target_pairs={{0,224},{32,64},{64,32},{96,128},{128,96},{160,192},{192,160},{224... | collective-permute-start | bytes 18440 | tf_op jit(solution)/shard_map/ppermute | solution.py:635
  36.9 0.0 collective-permute-start.6
  36.9 0.0 collective-permute-start.7
  36.9 1.5 %collective-permute-done.4.rest_0_ = f32[12,128]{1,0:T(8,128)S(1)} collective-permute-done((f32[12,128]{1,0:T(8,128)S(1)}, f32[12,128]{1,0:T(8,128)S(1)}, u32[]{:S(2)}, u32[]{:S(2)}) %collective-permute-start.4) | collective-permute-done | bytes 6176 | tf_op jit(solution)/shard_map/ppermute | solution.py:635
  38.5 0.0 collective-permute-done.5.rest_1_
  38.5 1.2 %collective-permute-done.6.rest_2_ = f32[12,128]{1,0:T(8,128)S(1)} collective-permute-done((f32[12,128]{1,0:T(8,128)S(1)}, f32[12,128]{1,0:T(8,128)S(1)}, u32[]{:S(2)}, u32[]{:S(2)}) %collective-permute-start.6) | collective-permute-done | bytes 6176 | tf_op jit(solution)/shard_map/ppermute | solution.py:635
  39.7 0.0 collective-permute-done.7.rest_3_
  39.7 2.6 %shard_map.71 = (f32[48,128]{1,0:T(8,128)S(1)}, f32[12,1024]{1,0:T(8,128)S(1)}, f32[96,128]{1,0:T(8,128)S(1)}, f32[24,128]{1,0:T(8,128)S(1)}, f32[24,128]{1,0:T(...) custom-call(f32[1,1,12,24,1024]{4,3,2,1,0:T(8,128)S(1)} %copy-done, s32[64,128]{1,0:T(8,128)S(1)} %get-tuple-element.45.conn_ref, ...), custom_call_target="tpu_custom_call" | custom-call | tf_op jit(solution)/shard_map/pallas_call | solution.py:612
  42.4 0.1 collective-permute-start.10
  42.5 1.9 %collective-permute-start.11 = (f32[24,128]{1,0:T(8,128)S(1)}, f32[24,128]{1,0:T(8,128)S(1)}, u32[]{:S(2)}, u32[]{:S(2)}) collective-permute-start(f32[24,128]{1,0:T(8,128)S(1)} %get-tuple-element.70), channel_id=1, source_target_pairs={{0,32},{32,0},{64,96},{96,64},{128,160},{160,128},{192,224},{224,1... | collective-permute-start | bytes 36872 | tf_op jit(solution)/shard_map/ppermute | solution.py:635
  44.4 2.4 %collective-permute-start.8 = (f32[24,128]{1,0:T(8,128)S(1)}, f32[24,128]{1,0:T(8,128)S(1)}, u32[]{:S(2)}, u32[]{:S(2)}) collective-permute-start(f32[24,128]{1,0:T(8,128)S(1)} %get-tuple-element.67), channel_id=1, source_target_pairs={{0,31},{1,2},{2,1},{3,4},{4,3},{5,6},{6,5},{7,8},{8,7},{9,10},{10,... | collective-permute-start | bytes 36872 | tf_op jit(solution)/shard_map/ppermute | solution.py:635
  46.8 0.1 collective-permute-start.9
  46.9 0.0 collective-permute-done.10.rest_2_
  46.9 0.0 collective-permute-done.11.rest_3_
  46.9 3.4 %collective-permute-done.8.rest_0_ = f32[24,128]{1,0:T(8,128)S(1)} collective-permute-done((f32[24,128]{1,0:T(8,128)S(1)}, f32[24,128]{1,0:T(8,128)S(1)}, u32[]{:S(2)}, u32[]{:S(2)}) %collective-permute-start.8) | collective-permute-done | bytes 12320 | tf_op jit(solution)/shard_map/ppermute | solution.py:635
  50.3 0.0 collective-permute-done.9.rest_1_
  50.3 1.6 %shard_map.72 = (f32[48,128]{1,0:T(8,128)S(1)}, f32[12,1024]{1,0:T(8,128)S(1)}, f32[48,128]{1,0:T(8,128)S(1)}, f32[12,128]{1,0:T(8,128)S(1)}, f32[12,128]{1,0:T(...) custom-call(f32[1,1,12,24,1024]{4,3,2,1,0:T(8,128)S(1)} %copy-done, s32[64,128]{1,0:T(8,128)S(1)} %get-tuple-element.45.conn_ref, ...), custom_call_target="tpu_custom_call" | custom-call | tf_op jit(solution)/shard_map/pallas_call | solution.py:612
  51.9 2.5 %collective-permute-start.12 = (f32[12,128]{1,0:T(8,128)S(1)}, f32[12,128]{1,0:T(8,128)S(1)}, u32[]{:S(2)}, u32[]{:S(2)}) collective-permute-start(f32[12,128]{1,0:T(8,128)S(1)} %get-tuple-element.72), channel_id=1, source_target_pairs={{0,31},{1,2},{2,1},{3,4},{4,3},{5,6},{6,5},{7,8},{8,7},{9,10},{10,... | collective-permute-start | bytes 18440 | tf_op jit(solution)/shard_map/ppermute | solution.py:635
  54.4 1.2 %collective-permute-start.13 = (f32[12,128]{1,0:T(8,128)S(1)}, f32[12,128]{1,0:T(8,128)S(1)}, u32[]{:S(2)}, u32[]{:S(2)}) collective-permute-start(f32[12,128]{1,0:T(8,128)S(1)} %get-tuple-element.73), channel_id=1, source_target_pairs={{0,224},{32,64},{64,32},{96,128},{128,96},{160,192},{192,160},{224... | collective-permute-start | bytes 18440 | tf_op jit(solution)/shard_map/ppermute | solution.py:635
  55.6 0.0 collective-permute-start.14
  55.6 0.9 %collective-permute-start.15 = (f32[12,128]{1,0:T(8,128)S(1)}, f32[12,128]{1,0:T(8,128)S(1)}, u32[]{:S(2)}, u32[]{:S(2)}) collective-permute-start(f32[12,128]{1,0:T(8,128)S(1)} %get-tuple-element.75), channel_id=1, source_target_pairs={{0,32},{32,0},{64,96},{96,64},{128,160},{160,128},{192,224},{224,1... | collective-permute-start | bytes 18440 | tf_op jit(solution)/shard_map/ppermute | solution.py:635
  56.5 1.3 %collective-permute-done.12.rest_0_ = f32[12,128]{1,0:T(8,128)S(1)} collective-permute-done((f32[12,128]{1,0:T(8,128)S(1)}, f32[12,128]{1,0:T(8,128)S(1)}, u32[]{:S(2)}, u32[]{:S(2)}) %collective-permute-start.12) | collective-permute-done | bytes 6176 | tf_op jit(solution)/shard_map/ppermute | solution.py:635
  57.8 0.0 collective-permute-done.13.rest_1_
  57.8 0.5 collective-permute-done.14.rest_2_
  58.4 0.0 collective-permute-done.15.rest_3_
  58.4 1.3 %shard_map.73 = (f32[1,128]{1,0:T(1,128)S(1)}, f32[48,128]{1,0:T(8,128)S(1)}, f32[12,128]{1,0:T(8,128)S(1)}, f32[12,128]{1,0:T(8,128)S(1)}) custom-call(f32[1,1,12,24,1024]{4,3,2,1,0:T(8,128)S(1)} %copy-done, s32[64,128]{1,0:T(8,128)S(1)} %get-tuple-element.45.conn_ref, f32[12,1024]{1,0:T(8,128)S(1)} %get-tuple-element.57.row_ref, ...), custom_call_target="tpu_custom_call" | custom-call | tf_op jit(solution)/shard_map/pallas_call | solution.py:612
  59.7 0.8 collective-permute-start.16
  60.5 0.8 collective-permute-start.17
  61.2 4.4 %collective-permute-done.16.left_ref = f32[12,128]{1,0:T(8,128)S(1)} collective-permute-done((f32[12,128]{1,0:T(8,128)S(1)}, f32[12,128]{1,0:T(8,128)S(1)}, u32[]{:S(2)}, u32[]{:S(2)}) %collective-permute-start.16) | collective-permute-done | bytes 6176 | tf_op jit(solution)/shard_map/ppermute | solution.py:641
  65.6 0.0 collective-permute-done.17.below_ref
  65.6 0.8 shard_map.74
  66.4 8.0 %all-to-all-start = ((f32[256,1,128]{2,1,0:T(1,128)}), f32[256,1,128]{2,1,0:T(1,128)S(1)}, u32[]{:S(2)}, u32[]{:S(2)}) async-start(f32[256,1,128]{2,1,0:T(1,128)} %bitcast.2), calls=%async_computation | async-start | bytes 262144 | tf_op jit(solution)/shard_map/all_to_all | solution.py:734
  75.1 12.5 %all-to-all-done = f32[256,1,128]{2,1,0:T(1,128)S(1)} async-done(((f32[256,1,128]{2,1,0:T(1,128)}), f32[256,1,128]{2,1,0:T(1,128)S(1)}, u32[]{:S(2)}, u32[]{:S(2)}) %all-to-all-start) | async-done | bytes 131104 | tf_op jit(solution)/shard_map/all_to_all | solution.py:734
  87.6 0.9 %shard_map.75 = (f32[24,128]{1,0:T(8,128)}, f32[96,128]{1,0:T(8,128)}) custom-call(f32[256,128]{1,0:T(8,128)S(1)} %bitcast.7, f32[1]{0:T(128)S(6)} %copy.14.step_ref, f32[48,128]{1,0:T(8,128)S(1)} %get-tuple-element.83.velocity_ref, f32[12,1024]{1,0:T(8,128)S(1)} %get-tuple-element.84.base_ref, f32[12,1024]{1,0:T(8,128)S(1)} %get-tuple-element.85.joint_ref, ...), custom_call_target="tpu_custom_call" | custom-call | tf_op jit(solution)/shard_map/pallas_call | solution.py:612
  (6 shorter events, 0.0 us)
Async XLA Ops:
  0.6 4.9 %copy-start = (f32[1,1,12,24,1024]{4,3,2,1,0:T(8,128)S(1)}, f32[1,1,12,24,1024]{4,3,2,1,0:T(8,128)}, u32[]{:S(2)}) copy-start(f32[1,1,12,24,1024]{4,3,2,1,0:T(8,128)} %blocks_ref.9) | copy-start | bytes 3538948
  0.6 0.9 copy-start.1
  1.5 0.7 copy-start.3
  2.2 3.3 %copy-start.2 = (f32[1,1,3,1024]{3,1,2,0:T(1,128)S(1)}, f32[1,1,3,1024]{3,1,2,0:T(1,128)}, u32[]{:S(2)}) copy-start(f32[1,1,3,1024]{3,1,2,0:T(1,128)} %param.8) | copy-start | bytes 36868
  13.9 11.8 %collective-permute-start = (f32[30,128]{1,0:T(8,128)S(1)}, f32[30,128]{1,0:T(8,128)S(1)}, u32[]{:S(2)}, u32[]{:S(2)}) collective-permute-start(f32[30,128]{1,0:T(8,128)S(1)} %get-tuple-element.53), channel_id=1, source_target_pairs={{0,31},{1,2},{2,1},{3,4},{4,3},{5,6},{6,5},{7,8},{8,7},{9,10},{10,... | collective-permute-start | bytes 46088 | tf_op jit(solution)/shard_map/ppermute | solution.py:635
  22.5 3.6 %collective-permute-start.1 = (f32[30,128]{1,0:T(8,128)S(1)}, f32[30,128]{1,0:T(8,128)S(1)}, u32[]{:S(2)}, u32[]{:S(2)}) collective-permute-start(f32[30,128]{1,0:T(8,128)S(1)} %get-tuple-element.54), channel_id=1, source_target_pairs={{0,224},{32,64},{64,32},{96,128},{128,96},{160,192},{192,160},{224... | collective-permute-start | bytes 46088 | tf_op jit(solution)/shard_map/ppermute | solution.py:635
  24.7 2.8 %collective-permute-start.2 = (f32[30,128]{1,0:T(8,128)S(1)}, f32[30,128]{1,0:T(8,128)S(1)}, u32[]{:S(2)}, u32[]{:S(2)}) collective-permute-start(f32[30,128]{1,0:T(8,128)S(1)} %get-tuple-element.55), channel_id=1, source_target_pairs={{0,1},{1,0},{2,3},{3,2},{4,5},{5,4},{6,7},{7,6},{8,9},{9,8},{10,11... | collective-permute-start | bytes 46088 | tf_op jit(solution)/shard_map/ppermute | solution.py:635
  24.7 2.8 %collective-permute-start.3 = (f32[30,128]{1,0:T(8,128)S(1)}, f32[30,128]{1,0:T(8,128)S(1)}, u32[]{:S(2)}, u32[]{:S(2)}) collective-permute-start(f32[30,128]{1,0:T(8,128)S(1)} %get-tuple-element.56), channel_id=1, source_target_pairs={{0,32},{32,0},{64,96},{96,64},{128,160},{160,128},{192,224},{224,1... | collective-permute-start | bytes 46088 | tf_op jit(solution)/shard_map/ppermute | solution.py:635
  32.6 5.9 %collective-permute-start.4 = (f32[12,128]{1,0:T(8,128)S(1)}, f32[12,128]{1,0:T(8,128)S(1)}, u32[]{:S(2)}, u32[]{:S(2)}) collective-permute-start(f32[12,128]{1,0:T(8,128)S(1)} %get-tuple-element.61), channel_id=1, source_target_pairs={{0,31},{1,2},{2,1},{3,4},{4,3},{5,6},{6,5},{7,8},{8,7},{9,10},{10,... | collective-permute-start | bytes 18440 | tf_op jit(solution)/shard_map/ppermute | solution.py:635
  33.6 4.8 %collective-permute-start.5 = (f32[12,128]{1,0:T(8,128)S(1)}, f32[12,128]{1,0:T(8,128)S(1)}, u32[]{:S(2)}, u32[]{:S(2)}) collective-permute-start(f32[12,128]{1,0:T(8,128)S(1)} %get-tuple-element.62), channel_id=1, source_target_pairs={{0,224},{32,64},{64,32},{96,128},{128,96},{160,192},{192,160},{224... | collective-permute-start | bytes 18440 | tf_op jit(solution)/shard_map/ppermute | solution.py:635
  36.9 2.8 %collective-permute-start.6 = (f32[12,128]{1,0:T(8,128)S(1)}, f32[12,128]{1,0:T(8,128)S(1)}, u32[]{:S(2)}, u32[]{:S(2)}) collective-permute-start(f32[12,128]{1,0:T(8,128)S(1)} %get-tuple-element.63), channel_id=1, source_target_pairs={{0,1},{1,0},{2,3},{3,2},{4,5},{5,4},{6,7},{7,6},{8,9},{9,8},{10,11... | collective-permute-start | bytes 18440 | tf_op jit(solution)/shard_map/ppermute | solution.py:635
  36.9 2.8 %collective-permute-start.7 = (f32[12,128]{1,0:T(8,128)S(1)}, f32[12,128]{1,0:T(8,128)S(1)}, u32[]{:S(2)}, u32[]{:S(2)}) collective-permute-start(f32[12,128]{1,0:T(8,128)S(1)} %get-tuple-element.64), channel_id=1, source_target_pairs={{0,32},{32,0},{64,96},{96,64},{128,160},{160,128},{192,224},{224,1... | collective-permute-start | bytes 18440 | tf_op jit(solution)/shard_map/ppermute | solution.py:635
  42.4 4.5 %collective-permute-start.10 = (f32[24,128]{1,0:T(8,128)S(1)}, f32[24,128]{1,0:T(8,128)S(1)}, u32[]{:S(2)}, u32[]{:S(2)}) collective-permute-start(f32[24,128]{1,0:T(8,128)S(1)} %get-tuple-element.69), channel_id=1, source_target_pairs={{0,1},{1,0},{2,3},{3,2},{4,5},{5,4},{6,7},{7,6},{8,9},{9,8},{10,11... | collective-permute-start | bytes 36872 | tf_op jit(solution)/shard_map/ppermute | solution.py:635
  42.5 4.3 %collective-permute-start.11 = (f32[24,128]{1,0:T(8,128)S(1)}, f32[24,128]{1,0:T(8,128)S(1)}, u32[]{:S(2)}, u32[]{:S(2)}) collective-permute-start(f32[24,128]{1,0:T(8,128)S(1)} %get-tuple-element.70), channel_id=1, source_target_pairs={{0,32},{32,0},{64,96},{96,64},{128,160},{160,128},{192,224},{224,1... | collective-permute-start | bytes 36872 | tf_op jit(solution)/shard_map/ppermute | solution.py:635
  44.4 5.9 %collective-permute-start.8 = (f32[24,128]{1,0:T(8,128)S(1)}, f32[24,128]{1,0:T(8,128)S(1)}, u32[]{:S(2)}, u32[]{:S(2)}) collective-permute-start(f32[24,128]{1,0:T(8,128)S(1)} %get-tuple-element.67), channel_id=1, source_target_pairs={{0,31},{1,2},{2,1},{3,4},{4,3},{5,6},{6,5},{7,8},{8,7},{9,10},{10,... | collective-permute-start | bytes 36872 | tf_op jit(solution)/shard_map/ppermute | solution.py:635
  46.8 3.5 %collective-permute-start.9 = (f32[24,128]{1,0:T(8,128)S(1)}, f32[24,128]{1,0:T(8,128)S(1)}, u32[]{:S(2)}, u32[]{:S(2)}) collective-permute-start(f32[24,128]{1,0:T(8,128)S(1)} %get-tuple-element.68), channel_id=1, source_target_pairs={{0,224},{32,64},{64,32},{96,128},{128,96},{160,192},{192,160},{224... | collective-permute-start | bytes 36872 | tf_op jit(solution)/shard_map/ppermute | solution.py:635
  51.9 5.9 %collective-permute-start.12 = (f32[12,128]{1,0:T(8,128)S(1)}, f32[12,128]{1,0:T(8,128)S(1)}, u32[]{:S(2)}, u32[]{:S(2)}) collective-permute-start(f32[12,128]{1,0:T(8,128)S(1)} %get-tuple-element.72), channel_id=1, source_target_pairs={{0,31},{1,2},{2,1},{3,4},{4,3},{5,6},{6,5},{7,8},{8,7},{9,10},{10,... | collective-permute-start | bytes 18440 | tf_op jit(solution)/shard_map/ppermute | solution.py:635
  54.4 3.5 %collective-permute-start.13 = (f32[12,128]{1,0:T(8,128)S(1)}, f32[12,128]{1,0:T(8,128)S(1)}, u32[]{:S(2)}, u32[]{:S(2)}) collective-permute-start(f32[12,128]{1,0:T(8,128)S(1)} %get-tuple-element.73), channel_id=1, source_target_pairs={{0,224},{32,64},{64,32},{96,128},{128,96},{160,192},{192,160},{224... | collective-permute-start | bytes 18440 | tf_op jit(solution)/shard_map/ppermute | solution.py:635
  55.6 2.8 %collective-permute-start.14 = (f32[12,128]{1,0:T(8,128)S(1)}, f32[12,128]{1,0:T(8,128)S(1)}, u32[]{:S(2)}, u32[]{:S(2)}) collective-permute-start(f32[12,128]{1,0:T(8,128)S(1)} %get-tuple-element.74), channel_id=1, source_target_pairs={{0,1},{1,0},{2,3},{3,2},{4,5},{5,4},{6,7},{7,6},{8,9},{9,8},{10,11... | collective-permute-start | bytes 18440 | tf_op jit(solution)/shard_map/ppermute | solution.py:635
  55.6 2.8 %collective-permute-start.15 = (f32[12,128]{1,0:T(8,128)S(1)}, f32[12,128]{1,0:T(8,128)S(1)}, u32[]{:S(2)}, u32[]{:S(2)}) collective-permute-start(f32[12,128]{1,0:T(8,128)S(1)} %get-tuple-element.75), channel_id=1, source_target_pairs={{0,32},{32,0},{64,96},{96,64},{128,160},{160,128},{192,224},{224,1... | collective-permute-start | bytes 18440 | tf_op jit(solution)/shard_map/ppermute | solution.py:635
  59.7 5.9 %collective-permute-start.16 = (f32[12,128]{1,0:T(8,128)S(1)}, f32[12,128]{1,0:T(8,128)S(1)}, u32[]{:S(2)}, u32[]{:S(2)}) collective-permute-start(f32[12,128]{1,0:T(8,128)S(1)} %get-tuple-element.80), channel_id=1, source_target_pairs={{0,1},{1,2},{2,3},{3,4},{4,5},{5,6},{6,7},{7,8},{8,9},{9,10},{10,1... | collective-permute-start | bytes 18440 | tf_op jit(solution)/shard_map/ppermute | solution.py:641
  60.5 5.1 %collective-permute-start.17 = (f32[12,128]{1,0:T(8,128)S(1)}, f32[12,128]{1,0:T(8,128)S(1)}, u32[]{:S(2)}, u32[]{:S(2)}) collective-permute-start(f32[12,128]{1,0:T(8,128)S(1)} %get-tuple-element.81), channel_id=1, source_target_pairs={{0,32},{32,64},{64,96},{96,128},{128,160},{160,192},{192,224},{224... | collective-permute-start | bytes 18440 | tf_op jit(solution)/shard_map/ppermute | solution.py:641
  66.4 21.2 %all-to-all-start = ((f32[256,1,128]{2,1,0:T(1,128)}), f32[256,1,128]{2,1,0:T(1,128)S(1)}, u32[]{:S(2)}, u32[]{:S(2)}) async-start(f32[256,1,128]{2,1,0:T(1,128)} %bitcast.2), calls=%async_computation | async-start | bytes 262144 | tf_op jit(solution)/shard_map/all_to_all | solution.py:734

commit v2 on v1

--- a/solution.py
+++ b/solution.py
@@ -13,7 +13,7 @@
 NODE_ROWS = 16
 ITEM_ROWS = 64
 SIDES = 4
-PARTS = 3
+PARTS = 2
 AXES = ("band", "sector")
 epsilon = 1e-06
 F32 = jnp.float32
@@ -41,16 +41,19 @@
     )
 
 
-def table_picks(row_getters, count, flat):
+def table_picks(row_getters, rows, flat):
+    rows = tuple(range(rows)) if isinstance(rows, int) else rows
     lanes = flat & (LANES - 1)
-    levels = count.bit_length() - 1
+    levels = rows[-1].bit_length()
     bits = [(flat & (LANES << level)) != 0 for level in range(levels)]
 
     def descend(row_at, level, base):
         if level < 0:
-            return pick(jnp.broadcast_to(row_at(base), (8, LANES)), lanes, 1)
+            return pick(jnp.broadcast_to(row_at(base), (8, LANES)), lanes, 1) if base in rows else None
         low = descend(row_at, level - 1, base)
         high = descend(row_at, level - 1, base + (1 << level))
+        if low is None or high is None:
+            return high if low is None else low
         return jnp.where(bits[level], high, low)
 
     return [descend(row_at, levels - 1, 0) for row_at in row_getters]
@@ -58,14 +61,6 @@
 
 def rows_of(ref, offset):
     return lambda row: ref[offset + row : offset + row + 1, :]
-
-
-def chunk_at(chunk):
-    return pl.ds(pl.multiple_of(chunk * LANES, LANES), LANES)
-
-
-def eight_at(chunk, offset=0):
-    return pl.ds(pl.multiple_of(offset + chunk * 8, 8), 8)
 
 
 def group_shift(values, distance):
@@ -76,6 +71,9 @@
 
 
 SCAN_STEPS = tuple(1 << step for step in range(10))
+RUNS = 5
+SORTED_ROWS = 8 * RUNS
+LOOSE_ROWS = tuple(row for row in range(ITEM_ROWS) if row % 8 >= 3)
 
 
 def sort_items(keys):
@@ -130,24 +128,34 @@
     return keys
 
 
-def plan_kernel(conn_ref, send_ref, conn_out, key_out, scan_out, end_out, inverse_out, send_scratch):
-    for half in range(8):
-        start = (half % 2) * LANES
-        send_scratch[half : half + 1, :] = send_ref[0, 0, half // 2 : half // 2 + 1, start : start + LANES]
-    send_line = jnp.concatenate([send_scratch[row : row + 1, :] for row in range(8)], axis=1)
-    place = lax.broadcasted_iota(I32, (8, 8 * LANES), 1)
-    in_row = (send_line >> 7) == lax.broadcasted_iota(I32, (8, 8 * LANES), 0)
+def one_line(rows):
+    return jnp.concatenate([rows[k : k + 1] for k in range(rows.shape[0])], axis=1)
+
+
+def inverse_of(line, code, rows):
+    width = line.shape[1]
+    in_row = (line >> 7) == lax.broadcasted_iota(I32, (rows, width), 0)
     left = jnp.concatenate(
         [
-            jnp.where(in_row, (place >> 5).astype(F32), 0.0),
-            jnp.where(in_row, (place & 31).astype(F32), 0.0),
+            jnp.where(in_row, (code >> 7).astype(F32), 0.0),
+            jnp.where(in_row, (code & (LANES - 1)).astype(F32), 0.0),
         ],
         axis=0,
     ).astype(jnp.bfloat16)
-    in_lane = (send_line & (LANES - 1)) == lax.broadcasted_iota(I32, (LANES, 8 * LANES), 0)
+    in_lane = (line & (LANES - 1)) == lax.broadcasted_iota(I32, (LANES, width), 0)
     right = jnp.where(in_lane, 1.0, 0.0).astype(jnp.bfloat16)
     found = lax.dot_general(left, right, (((1,), (1,)), ((), ())), preferred_element_type=F32)
-    inverse_out[...] = (found[0:8] * 32.0 + found[8:16]).astype(I32)
+    return (found[0:rows] * 128.0 + found[rows : 2 * rows]).astype(I32)
+
+
+def plan_kernel(
+    conn_ref, send_ref, conn_out, key_out, scan_out, end_out, own_out, pair_out, inverse_out, send_out, keys_ref
+):
+    for half in range(8):
+        start = (half % 2) * LANES
+        send_out[half : half + 1, :] = send_ref[0, 0, half // 2 : half // 2 + 1, start : start + LANES]
+    place = lax.broadcasted_iota(I32, (1, 8 * LANES), 1)
+    inverse_out[...] = inverse_of(one_line(send_out[...]), place, 8)
     sub, lane = tile_iota(0), tile_iota(1)
     keys = []
     for chunk in range(CHUNKS):
@@ -155,19 +163,33 @@
         (label,) = table_picks([rows_of(inverse_out, 0)], 8, ids & 1023)
         ids = jnp.where(ids < 1024, label, ids)
         conn_out[8 * chunk : 8 * chunk + 8, :] = ids
-        keys.append(ids * 8192 + (chunk * 1024 + sub * LANES + lane))
+        item = ids * 8192 + (chunk * 1024 + sub * LANES + lane)
+        keys.append(jnp.where(sub < 3, 2048 * 8192, item))
+    first_line = jnp.concatenate([conn_out[8 * chunk : 8 * chunk + 1, :] for chunk in range(CHUNKS)], axis=1)
+    own_out[...] = inverse_of(first_line, place, 8)
+    pair_line = jnp.concatenate(
+        [conn_out[8 * chunk + k : 8 * chunk + k + 1, :] for chunk in range(CHUNKS) for k in (1, 2)], axis=1
+    )
+    pair_out[...] = inverse_of(pair_line, lax.broadcasted_iota(I32, (1, 16 * LANES), 1), NODE_ROWS)
     keys = sort_items(keys)
     for register in range(8):
-        key_out[8 * register : 8 * register + 8, :] = keys[register]
-    first, last = keys[0] >> 13, keys[7] >> 13
+        keys_ref[8 * register : 8 * register + 8, :] = keys[register]
     group = lane * 8 + sub
+    runs = []
+    for register in range(RUNS):
+        place = group * RUNS + register
+        row = (place & 7) * 8 + ((place >> 3) & 7)
+        (moved,) = table_picks([rows_of(keys_ref, 0)], ITEM_ROWS, row * LANES + (place >> 6))
+        runs.append(moved)
+        key_out[8 * register : 8 * register + 8, :] = moved
+    first, last = runs[0] >> 13, runs[-1] >> 13
     scan = jnp.zeros((8, LANES), I32)
     for step, distance in enumerate(SCAN_STEPS):
         same = (group >= distance) & (group_shift(last, distance) == last)
         scan = jnp.where(same, scan | (1 << step), scan)
     same = (group >= 1) & (group_shift(last, 1) == first)
     scan_out[...] = jnp.where(same, scan | (1 << len(SCAN_STEPS)), scan)
-    lane_last = jnp.broadcast_to(key_out[63:64, :] >> 13, (8, LANES))
+    lane_last = jnp.broadcast_to(keys_ref[63:64, :] >> 13, (8, LANES))
     for half in range(2):
         node = (half * 8 + sub) * LANES + lane
         column = jnp.zeros((8, LANES), I32)
@@ -175,53 +197,67 @@
             seen = pick(lane_last, column + (step - 1), 1)
             column = jnp.where(seen <= node, column + step, column)
         count = column * 64
+        before = pick(lane_last, jnp.maximum(column - 1, 0), 1)
+        named = (column > 0) & (before == node)
         for row in range(ITEM_ROWS):
-            seen = pick(jnp.broadcast_to(key_out[row : row + 1, :], (8, LANES)), column, 1)
-            count = count + jnp.where((seen >> 13) <= node, 1, 0)
-        place = count - 1
-        row = (place & 7) * 8 + ((place >> 3) & 7)
-        end_out[8 * half : 8 * half + 8, :] = row * LANES + (place >> 6)
-
-
-def scatter_items(term_ref, channels, plan, sorted_ref, out_ref, merge):
-    key_ref, scan_ref, end_ref = plan
-
-    def bring(register, _):
-        item = key_ref[eight_at(register), :] & 8191
-        tables = [rows_of(term_ref, ITEM_ROWS * channel) for channel in range(channels)]
-        for channel, values in enumerate(table_picks(tables, ITEM_ROWS, item)):
-            sorted_ref[eight_at(register, ITEM_ROWS * channel), :] = values
-        return 0
-
-    lax.fori_loop(0, 8, bring, 0, unroll=True)
-    nodes = [key_ref[8 * register : 8 * register + 8, :] >> 13 for register in range(8)]
+            seen = pick(jnp.broadcast_to(keys_ref[row : row + 1, :], (8, LANES)), column, 1) >> 13
+            count = count + jnp.where(seen <= node, 1, 0)
+            named = named | (seen == node)
+        place = jnp.maximum(count - 1, 0)
+        place = jnp.where(named, place, 0)
+        share = (place * 52429) >> 18
+        row = (place - share * RUNS) * 8 + (share & 7)
+        end = row * LANES + (share >> 3)
+        end_out[8 * half : 8 * half + 8, :] = jnp.where(named, end, 8192)
+
+
+def scatter_maxima(term_ref, channels, plan, sorted_ref, out_ref):
+    key_ref, scan_ref, end_ref, own_ref, pair_ref = plan
+    tables = [rows_of(term_ref, ITEM_ROWS * channel) for channel in range(channels)]
+    nodes = []
+    for register in range(RUNS):
+        key = key_ref[8 * register : 8 * register + 8, :]
+        nodes.append(key >> 13)
+        for channel, values in enumerate(table_picks(tables, LOOSE_ROWS, key & 8191)):
+            base = SORTED_ROWS * channel + 8 * register
+            sorted_ref[base : base + 8, :] = values
     scan = scan_ref[...]
     follows = [(scan & (1 << step)) != 0 for step in range(len(SCAN_STEPS) + 1)]
     for channel in range(channels):
-        base = ITEM_ROWS * channel
+        base = SORTED_ROWS * channel
         runs = [sorted_ref[base : base + 8, :]]
-        for register in range(1, 8):
+        for register in range(1, RUNS):
             same = nodes[register] == nodes[register - 1]
             here = sorted_ref[base + 8 * register : base + 8 * register + 8, :]
-            runs.append(merge(here, jnp.where(same, runs[-1], 0.0)))
-        total = runs[7]
+            runs.append(jnp.maximum(here, jnp.where(same, runs[-1], 0.0)))
+        total = runs[-1]
         for step, distance in enumerate(SCAN_STEPS):
-            total = merge(total, jnp.where(follows[step], group_shift(total, distance), 0.0))
+            total = jnp.maximum(total, jnp.where(follows[step], group_shift(total, distance), 0.0))
         carry = jnp.where(follows[-1], group_shift(total, 1), 0.0)
-        for register in range(8):
+        for register in range(RUNS):
             open_run = nodes[register] == nodes[0]
-            sorted_ref[base + 8 * register : base + 8 * register + 8, :] = merge(
+            sorted_ref[base + 8 * register : base + 8 * register + 8, :] = jnp.maximum(
                 runs[register], jnp.where(open_run, carry, 0.0)
             )
-
-    def deliver(half, _):
-        index = end_ref[eight_at(half), :]
-        tables = [rows_of(sorted_ref, ITEM_ROWS * channel) for channel in range(channels)]
-        for channel, values in enumerate(table_picks(tables, ITEM_ROWS, index)):
-            out_ref[eight_at(half, NODE_ROWS * channel), :] = values
-        return 0
-
-    lax.fori_loop(0, 2, deliver, 0, unroll=True)
+    sorted_tables = [rows_of(sorted_ref, SORTED_ROWS * channel) for channel in range(channels)]
+    first_tables = [lambda row, at=at: at(8 * row) for at in tables]
+    pair_tables = [lambda row, at=at: at((row >> 1) * 8 + (row & 1) + 1) for at in tables]
+    own = table_picks(first_tables, 8, own_ref[...])
+    for half in range(2):
+        index = end_ref[8 * half : 8 * half + 8, :]
+        loose = table_picks(sorted_tables, SORTED_ROWS, index & 8191)
+        paired = table_picks(pair_tables, NODE_ROWS, pair_ref[8 * half : 8 * half + 8, :])
+        for channel in range(channels):
+            best = jnp.maximum(jnp.where(index < 8192, loose[channel], 0.0), paired[channel])
+            if half == 0:
+                best = jnp.maximum(best, own[channel])
+            base = NODE_ROWS * channel + 8 * half
+            out_ref[base : base + 8, :] = best
+
+
+def node_picks(table_ref, channels, conn_ref, chunk):
+    tables = [rows_of(table_ref, NODE_ROWS * channel) for channel in range(channels)]
+    return table_picks(tables, NODE_ROWS, conn_ref[8 * chunk : 8 * chunk + 8, :])
 
 
 def bf16_parts(values, count):
@@ -231,10 +267,6 @@
         parts.append(part)
         values = values - part
     return parts
-
-
-def one_line(rows):
-    return jnp.concatenate([rows[k : k + 1] for k in range(8)], axis=1)
 
 
 def scatter_sums(term_ref, channels, conn_ref, out_ref):
@@ -265,11 +297,6 @@
         out_ref[NODE_ROWS * channel : NODE_ROWS * (channel + 1), :] = out
 
 
-def node_picks(table_ref, channels, conn_ref, chunk):
-    tables = [rows_of(table_ref, NODE_ROWS * channel) for channel in range(channels)]
-    return table_picks(tables, NODE_ROWS, conn_ref[eight_at(chunk), :])
-
-
 def row_maxima(blocks_ref, picked, at, max_ref):
     for r in range(STRAINS):
         sized = [jnp.abs(blocks_ref[0, 0, r, 8 * c : 8 * c + 8, at]) for c in range(3)]
@@ -295,9 +322,9 @@
 
 
 def apply_blocks(blocks_ref, table_ref, sets, conn_ref, strain_ref):
-    def one(chunk, _):
+    for chunk in range(CHUNKS):
         values = node_picks(table_ref, 3 * sets, conn_ref, chunk)
-        at = chunk_at(chunk)
+        at = slice(chunk * LANES, (chunk + 1) * LANES)
         for r in range(STRAINS):
             parts = [blocks_ref[0, 0, r, 8 * c : 8 * c + 8, at] for c in range(3)]
             for k in range(sets):
@@ -306,14 +333,11 @@
                 strain_ref[STRAINS * k + r : STRAINS * k + r + 1, at] = jnp.sum(
                     total, axis=0, keepdims=True
                 )
-        return 0
-
-    lax.fori_loop(0, CHUNKS, one, 0, unroll=True)
 
 
 def apply_transpose(blocks_ref, strain_ref, sets, term_ref):
-    def one(chunk, _):
-        at = chunk_at(chunk)
+    for chunk in range(CHUNKS):
+        at = slice(chunk * LANES, (chunk + 1) * LANES)
         totals = [jnp.zeros((8, LANES), F32)] * (3 * sets)
         for r in range(STRAINS):
             parts = [blocks_ref[0, 0, r, 8 * c : 8 * c + 8, at] for c in range(3)]
@@ -322,10 +346,8 @@
                 for c in range(3):
                     totals[3 * k + c] = totals[3 * k + c] + parts[c] * strain
         for channel in range(3 * sets):
-            term_ref[eight_at(chunk, ITEM_ROWS * channel), :] = totals[channel]
-        return 0
-
-    lax.fori_loop(0, CHUNKS, one, 0, unroll=True)
+            row = ITEM_ROWS * channel + 8 * chunk
+            term_ref[row : row + 8, :] = totals[channel]
 
 
 def even_places():
@@ -400,8 +422,9 @@
 
 
 def start_kernel(
-    blocks_ref, ids_ref, loads_ref, send_ref, key_ref, scan_ref, end_ref, row_out, part_out, loads_out, *rest
+    blocks_ref, ids_ref, loads_ref, send_ref, *rest
 ):
+    plan, (row_out, part_out, loads_out), rest = rest[:5], rest[5:8], rest[8:]
     packets, (term, items, peaks) = rest[:4], rest[4:]
     below, above = [live.astype(F32) for live in live_sides()]
     for chunk in range(CHUNKS):
@@ -412,7 +435,7 @@
     row_out[...] = 1.0 / jnp.sqrt(peaks[...])
     column_maxima(blocks_ref, None, term, 0)
     column_maxima(blocks_ref, row_out, term, 3)
-    scatter_items(term, 6, (key_ref, scan_ref, end_ref), items, part_out, jnp.maximum)
+    scatter_maxima(term, 6, plan, items, part_out)
     pack(part_out, 6, packets)
     tables = [rows_of(loads_ref, 8 * c) for c in range(3)]
     for c, values in enumerate(table_picks(tables, 8, send_ref[...])):
@@ -430,8 +453,9 @@
 
 
 def sweep_kernel(
-    blocks_ref, conn_ref, key_ref, scan_ref, end_ref, row_ref, part_ref, own_loads, *rest
+    blocks_ref, conn_ref, row_ref, part_ref, own_loads, *rest
 ):
+    plan, rest = rest[:5], rest[5:]
     arrived, rest = by_side(rest[:4]), rest[4:]
     row_out, scale_out, part_out, loads_out, rest = rest[0], rest[1], rest[2], rest[3], rest[4:]
     packets, (term, items, peaks, merged, second_row) = rest[:4], rest[4:]
@@ -459,7 +483,7 @@
     second_row[...] = first_row / jnp.sqrt(first_row * peaks[0:STRAINS, :])
     row_out[...] = second_row[...] / jnp.sqrt(second_row[...] * peaks[STRAINS : 2 * STRAINS, :])
     column_maxima(blocks_ref, second_row, term, 0)
-    scatter_items(term, 3, (key_ref, scan_ref, end_ref), items, part_out, jnp.maximum)
+    scatter_maxima(term, 3, plan, items, part_out)
     pack(part_out, 3, packets)
 
 
@@ -649,10 +673,10 @@
     twice = ((6 * ITEM_ROWS, LANES), F32)
     ids = ((64, LANES), I32)
     few = ((8, LANES), I32)
-    conn, key, scan, end, inverse, send = call(
+    conn, *plan, inverse, send = call(
         plan_kernel,
-        [ids, ids, few, ((16, LANES), I32), few, few],
-        [],
+        [ids, ((SORTED_ROWS, LANES), I32), few, ((16, LANES), I32), few, ((16, LANES), I32), few, few],
+        [ids],
         connectivity,
         send_lists,
         work=4_000_000_000,
@@ -660,27 +684,23 @@
     row, part, own_loads, *packets = call(
         start_kernel,
         [rows, ((96, LANES), F32), ((24, LANES), F32)] + [((30, LANES), F32)] * 4,
-        [twice, twice, rows],
+        [twice, ((6 * SORTED_ROWS, LANES), F32), rows],
         blocks,
         connectivity,
         nodal_loads.reshape(24, LANES),
         send,
-        key,
-        scan,
-        end,
+        *plan,
     )
     row, scale, part, loads, *packets = call(
         sweep_kernel,
         [rows, nodes, nodes, nodes] + packet,
-        [items, items, ((2 * STRAINS, 1024), F32), ((96, LANES), F32), rows],
+        [items, ((3 * SORTED_ROWS, LANES), F32), ((2 * STRAINS, 1024), F32), ((96, LANES), F32), rows],
         blocks,
         conn,
-        key,
-        scan,
-        end,
         row,
         part,
         own_loads,
+        *plan,
         *exchange(packets),
     )
     scale, base, part, *packets = call(

time: 88.8 us -> 85.4 us (0.962)
  Pallas kernels: 24 us -> 20.5 us
    pallas_call x8, Pallas kernels: 24 us -> 20.5 us  [call(): pl.pallas_call(body, out_shape=[jax.ShapeDtypeStruct(shape, kind) for sha...]
where the time goes in v2:
time: 85.4 us; the launch traced here: 85.2 us
  starting transfers between devices  34.8 us (41%)
  waiting for transfers between devices  26.8 us (31%)
  Pallas kernels  20.5 us (24%)
  local copies, waits for them, and re-layouts  1.54 us (2%)
  between operations  1.52 us (2%)
    ppermute x16, starting transfers between devices, exchange(): lax.ppermute(packet, axis, swap_pairs(axis, odd))  25.3 us
    pallas_call x8, Pallas kernels, call(): pl.pallas_call(body, out_shape=[jax.ShapeDtypeStruct(shape, kind) for sha...  20.5 us
    all_to_all x1, waiting for transfers between devices, per_device(): sums = lax.all_to_all(sums, AXES, 0, 0, tiled=True)  12.5 us
    ppermute x16, waiting for transfers between devices, exchange(): lax.ppermute(packet, axis, swap_pairs(axis, odd))  9.9 us
    all_to_all x1, starting transfers between devices, per_device(): sums = lax.all_to_all(sums, AXES, 0, 0, tiled=True)  8.03 us
    ppermute x2, waiting for transfers between devices, shift_up(): lax.ppermute(packet, axis, [(i, (i + 1) % count) for i in range(count)])  4.36 us
  transfers between devices with their start and end apart: 19, of which 9 were waited for; matrix products, arithmetic and copies ran while one was open for 0% of the time, Pallas kernels for 0%

profile of v2, /device:TPU:1, one launch (start us, length us, event | category | flops | bytes accessed | tf_op | source)
XLA Modules:
  0.0 85.2 jit_solution(15107350606547635030)
XLA Ops:
  0.7 0.8 copy-done.1
  1.5 0.7 copy-done.3
  2.2 3.8 %shard_map.68 = (s32[64,128]{1,0:T(8,128)S(1)}, s32[40,128]{1,0:T(8,128)S(1)}, s32[8,128]{1,0:T(8,128)S(1)}, s32[16,128]{1,0:T(8,128)S(1)}, s32[8,128]{1,0:T(8,1...) custom-call(s32[1,1,8,1024]{3,2,1,0:T(8,128)S(1)} %copy-done.1, ...), custom_call_target="tpu_custom_call" | custom-call | flops 4000000000 | bytes 15625000 | tf_op jit(solution)/shard_map/pallas_call | solution.py:636
  6.0 6.3 %shard_map.69 = (f32[12,1024]{1,0:T(8,128)S(1)}, f32[96,128]{1,0:T(8,128)S(1)}, f32[24,128]{1,0:T(8,128)S(1)}, f32[30,128]{1,0:T(8,128)S(1)}, f32[30,128]{1,0:T(...) custom-call(f32[1,1,12,24,1024]{4,3,2,1,0:T(8,128)S(1)} %copy-done, s32[1,1,8,1024]{3,2,1,0:T(8,128)S(1)} %copy-done.1, ...), custom_call_target="tpu_custom_call" | custom-call | tf_op jit(solution)/shard_map/pallas_call | solution.py:636
  12.4 8.7 %collective-permute-start = (f32[30,128]{1,0:T(8,128)S(1)}, f32[30,128]{1,0:T(8,128)S(1)}, u32[]{:S(2)}, u32[]{:S(2)}) collective-permute-start(f32[30,128]{1,0:T(8,128)S(1)} %get-tuple-element.57), channel_id=1, source_target_pairs={{0,31},{1,2},{2,1},{3,4},{4,3},{5,6},{6,5},{7,8},{8,7},{9,10},{10,... | collective-permute-start | bytes 46088 | tf_op jit(solution)/shard_map/ppermute | solution.py:659
  21.1 2.1 %collective-permute-start.1 = (f32[30,128]{1,0:T(8,128)S(1)}, f32[30,128]{1,0:T(8,128)S(1)}, u32[]{:S(2)}, u32[]{:S(2)}) collective-permute-start(f32[30,128]{1,0:T(8,128)S(1)} %get-tuple-element.58), channel_id=1, source_target_pairs={{0,224},{32,64},{64,32},{96,128},{128,96},{160,192},{192,160},{224... | collective-permute-start | bytes 46088 | tf_op jit(solution)/shard_map/ppermute | solution.py:659
  23.2 0.0 collective-permute-start.2
  23.2 1.0 %collective-permute-start.3 = (f32[30,128]{1,0:T(8,128)S(1)}, f32[30,128]{1,0:T(8,128)S(1)}, u32[]{:S(2)}, u32[]{:S(2)}) collective-permute-start(f32[30,128]{1,0:T(8,128)S(1)} %get-tuple-element.60), channel_id=1, source_target_pairs={{0,32},{32,0},{64,96},{96,64},{128,160},{160,128},{192,224},{224,1... | collective-permute-start | bytes 46088 | tf_op jit(solution)/shard_map/ppermute | solution.py:659
  24.2 0.0 collective-permute-done.rest_5_
  24.2 0.4 collective-permute-done.1.rest_6_
  24.6 1.4 %collective-permute-done.2.rest_7_ = f32[30,128]{1,0:T(8,128)S(1)} collective-permute-done((f32[30,128]{1,0:T(8,128)S(1)}, f32[30,128]{1,0:T(8,128)S(1)}, u32[]{:S(2)}, u32[]{:S(2)}) %collective-permute-start.2) | collective-permute-done | bytes 15392 | tf_op jit(solution)/shard_map/ppermute | solution.py:659
  26.0 0.0 collective-permute-done.3.rest_8_
  26.0 4.0 %shard_map.70 = (f32[12,1024]{1,0:T(8,128)S(1)}, f32[48,128]{1,0:T(8,128)S(1)}, f32[48,128]{1,0:T(8,128)S(1)}, f32[48,128]{1,0:T(8,128)S(1)}, f32[12,128]{1,0:T(...) custom-call(f32[1,1,12,24,1024]{4,3,2,1,0:T(8,128)S(1)} %copy-done, ...), custom_call_target="tpu_custom_call" | custom-call | tf_op jit(solution)/shard_map/pallas_call | solution.py:636
  30.1 1.1 %collective-permute-start.4 = (f32[12,128]{1,0:T(8,128)S(1)}, f32[12,128]{1,0:T(8,128)S(1)}, u32[]{:S(2)}, u32[]{:S(2)}) collective-permute-start(f32[12,128]{1,0:T(8,128)S(1)} %get-tuple-element.65), channel_id=1, source_target_pairs={{0,31},{1,2},{2,1},{3,4},{4,3},{5,6},{6,5},{7,8},{8,7},{9,10},{10,... | collective-permute-start | bytes 18440 | tf_op jit(solution)/shard_map/ppermute | solution.py:659
  31.1 3.3 %collective-permute-start.5 = (f32[12,128]{1,0:T(8,128)S(1)}, f32[12,128]{1,0:T(8,128)S(1)}, u32[]{:S(2)}, u32[]{:S(2)}) collective-permute-start(f32[12,128]{1,0:T(8,128)S(1)} %get-tuple-element.66), channel_id=1, source_target_pairs={{0,224},{32,64},{64,32},{96,128},{128,96},{160,192},{192,160},{224... | collective-permute-start | bytes 18440 | tf_op jit(solution)/shard_map/ppermute | solution.py:659
  34.4 0.0 collective-permute-start.6
  34.4 0.0 collective-permute-start.7
  34.4 1.5 %collective-permute-done.4.rest_0_ = f32[12,128]{1,0:T(8,128)S(1)} collective-permute-done((f32[12,128]{1,0:T(8,128)S(1)}, f32[12,128]{1,0:T(8,128)S(1)}, u32[]{:S(2)}, u32[]{:S(2)}) %collective-permute-start.4) | collective-permute-done | bytes 6176 | tf_op jit(solution)/shard_map/ppermute | solution.py:659
  36.0 0.0 collective-permute-done.5.rest_1_
  36.0 1.3 %collective-permute-done.6.rest_2_ = f32[12,128]{1,0:T(8,128)S(1)} collective-permute-done((f32[12,128]{1,0:T(8,128)S(1)}, f32[12,128]{1,0:T(8,128)S(1)}, u32[]{:S(2)}, u32[]{:S(2)}) %collective-permute-start.6) | collective-permute-done | bytes 6176 | tf_op jit(solution)/shard_map/ppermute | solution.py:659
  37.2 0.0 collective-permute-done.7.rest_3_
  37.2 2.0 %shard_map.71 = (f32[48,128]{1,0:T(8,128)S(1)}, f32[12,1024]{1,0:T(8,128)S(1)}, f32[96,128]{1,0:T(8,128)S(1)}, f32[24,128]{1,0:T(8,128)S(1)}, f32[24,128]{1,0:T(...) custom-call(f32[1,1,12,24,1024]{4,3,2,1,0:T(8,128)S(1)} %copy-done, s32[64,128]{1,0:T(8,128)S(1)} %get-tuple-element.47.conn_ref, ...), custom_call_target="tpu_custom_call" | custom-call | tf_op jit(solution)/shard_map/pallas_call | solution.py:636
  39.2 0.2 collective-permute-start.10
  39.4 1.9 %collective-permute-start.11 = (f32[24,128]{1,0:T(8,128)S(1)}, f32[24,128]{1,0:T(8,128)S(1)}, u32[]{:S(2)}, u32[]{:S(2)}) collective-permute-start(f32[24,128]{1,0:T(8,128)S(1)} %get-tuple-element.74), channel_id=1, source_target_pairs={{0,32},{32,0},{64,96},{96,64},{128,160},{160,128},{192,224},{224,1... | collective-permute-start | bytes 36872 | tf_op jit(solution)/shard_map/ppermute | solution.py:659
  41.3 2.4 %collective-permute-start.8 = (f32[24,128]{1,0:T(8,128)S(1)}, f32[24,128]{1,0:T(8,128)S(1)}, u32[]{:S(2)}, u32[]{:S(2)}) collective-permute-start(f32[24,128]{1,0:T(8,128)S(1)} %get-tuple-element.71), channel_id=1, source_target_pairs={{0,31},{1,2},{2,1},{3,4},{4,3},{5,6},{6,5},{7,8},{8,7},{9,10},{10,... | collective-permute-start | bytes 36872 | tf_op jit(solution)/shard_map/ppermute | solution.py:659
  43.7 0.1 collective-permute-start.9
  43.7 0.0 collective-permute-done.10.rest_2_
  43.7 0.0 collective-permute-done.11.rest_3_
  43.7 3.4 %collective-permute-done.8.rest_0_ = f32[24,128]{1,0:T(8,128)S(1)} collective-permute-done((f32[24,128]{1,0:T(8,128)S(1)}, f32[24,128]{1,0:T(8,128)S(1)}, u32[]{:S(2)}, u32[]{:S(2)}) %collective-permute-start.8) | collective-permute-done | bytes 12320 | tf_op jit(solution)/shard_map/ppermute | solution.py:659
  47.2 0.0 collective-permute-done.9.rest_1_
  47.2 1.5 %shard_map.72 = (f32[48,128]{1,0:T(8,128)S(1)}, f32[12,1024]{1,0:T(8,128)S(1)}, f32[48,128]{1,0:T(8,128)S(1)}, f32[12,128]{1,0:T(8,128)S(1)}, f32[12,128]{1,0:T(...) custom-call(f32[1,1,12,24,1024]{4,3,2,1,0:T(8,128)S(1)} %copy-done, s32[64,128]{1,0:T(8,128)S(1)} %get-tuple-element.47.conn_ref, ...), custom_call_target="tpu_custom_call" | custom-call | tf_op jit(solution)/shard_map/pallas_call | solution.py:636
  48.6 2.5 %collective-permute-start.12 = (f32[12,128]{1,0:T(8,128)S(1)}, f32[12,128]{1,0:T(8,128)S(1)}, u32[]{:S(2)}, u32[]{:S(2)}) collective-permute-start(f32[12,128]{1,0:T(8,128)S(1)} %get-tuple-element.76), channel_id=1, source_target_pairs={{0,31},{1,2},{2,1},{3,4},{4,3},{5,6},{6,5},{7,8},{8,7},{9,10},{10,... | collective-permute-start | bytes 18440 | tf_op jit(solution)/shard_map/ppermute | solution.py:659
  51.1 1.2 %collective-permute-start.13 = (f32[12,128]{1,0:T(8,128)S(1)}, f32[12,128]{1,0:T(8,128)S(1)}, u32[]{:S(2)}, u32[]{:S(2)}) collective-permute-start(f32[12,128]{1,0:T(8,128)S(1)} %get-tuple-element.77), channel_id=1, source_target_pairs={{0,224},{32,64},{64,32},{96,128},{128,96},{160,192},{192,160},{224... | collective-permute-start | bytes 18440 | tf_op jit(solution)/shard_map/ppermute | solution.py:659
  52.3 0.0 collective-permute-start.14
  52.3 0.9 %collective-permute-start.15 = (f32[12,128]{1,0:T(8,128)S(1)}, f32[12,128]{1,0:T(8,128)S(1)}, u32[]{:S(2)}, u32[]{:S(2)}) collective-permute-start(f32[12,128]{1,0:T(8,128)S(1)} %get-tuple-element.79), channel_id=1, source_target_pairs={{0,32},{32,0},{64,96},{96,64},{128,160},{160,128},{192,224},{224,1... | collective-permute-start | bytes 18440 | tf_op jit(solution)/shard_map/ppermute | solution.py:659
  53.2 1.3 %collective-permute-done.12.rest_0_ = f32[12,128]{1,0:T(8,128)S(1)} collective-permute-done((f32[12,128]{1,0:T(8,128)S(1)}, f32[12,128]{1,0:T(8,128)S(1)}, u32[]{:S(2)}, u32[]{:S(2)}) %collective-permute-start.12) | collective-permute-done | bytes 6176 | tf_op jit(solution)/shard_map/ppermute | solution.py:659
  54.5 0.0 collective-permute-done.13.rest_1_
  54.5 0.5 collective-permute-done.14.rest_2_
  55.1 0.0 collective-permute-done.15.rest_3_
  55.1 1.1 %shard_map.73 = (f32[1,128]{1,0:T(1,128)S(1)}, f32[48,128]{1,0:T(8,128)S(1)}, f32[12,128]{1,0:T(8,128)S(1)}, f32[12,128]{1,0:T(8,128)S(1)}) custom-call(f32[1,1,12,24,1024]{4,3,2,1,0:T(8,128)S(1)} %copy-done, s32[64,128]{1,0:T(8,128)S(1)} %get-tuple-element.47.conn_ref, f32[12,1024]{1,0:T(8,128)S(1)} %get-tuple-element.61.row_ref, ...), custom_call_target="tpu_custom_call" | custom-call | tf_op jit(solution)/shard_map/pallas_call | solution.py:636
  56.2 0.8 collective-permute-start.16
  57.0 0.8 collective-permute-start.17
  57.8 4.4 %collective-permute-done.16.left_ref = f32[12,128]{1,0:T(8,128)S(1)} collective-permute-done((f32[12,128]{1,0:T(8,128)S(1)}, f32[12,128]{1,0:T(8,128)S(1)}, u32[]{:S(2)}, u32[]{:S(2)}) %collective-permute-start.16) | collective-permute-done | bytes 6176 | tf_op jit(solution)/shard_map/ppermute | solution.py:665
  62.1 0.0 collective-permute-done.17.below_ref
  62.1 0.8 shard_map.74
  62.9 8.0 %all-to-all-start = ((f32[256,1,128]{2,1,0:T(1,128)}), f32[256,1,128]{2,1,0:T(1,128)S(1)}, u32[]{:S(2)}, u32[]{:S(2)}) async-start(f32[256,1,128]{2,1,0:T(1,128)} %bitcast.2), calls=%async_computation | async-start | bytes 262144 | tf_op jit(solution)/shard_map/all_to_all | solution.py:754
  71.6 12.5 %all-to-all-done = f32[256,1,128]{2,1,0:T(1,128)S(1)} async-done(((f32[256,1,128]{2,1,0:T(1,128)}), f32[256,1,128]{2,1,0:T(1,128)S(1)}, u32[]{:S(2)}, u32[]{:S(2)}) %all-to-all-start) | async-done | bytes 131104 | tf_op jit(solution)/shard_map/all_to_all | solution.py:754
  84.1 0.9 %shard_map.75 = (f32[24,128]{1,0:T(8,128)}, f32[96,128]{1,0:T(8,128)}) custom-call(f32[256,128]{1,0:T(8,128)S(1)} %bitcast.7, f32[1]{0:T(128)S(6)} %copy.14.step_ref, f32[48,128]{1,0:T(8,128)S(1)} %get-tuple-element.87.velocity_ref, f32[12,1024]{1,0:T(8,128)S(1)} %get-tuple-element.88.base_ref, f32[12,1024]{1,0:T(8,128)S(1)} %get-tuple-element.89.joint_ref, ...), custom_call_target="tpu_custom_call" | custom-call | tf_op jit(solution)/shard_map/pallas_call | solution.py:636
  (6 shorter events, 0.0 us)
Async XLA Ops:
  0.6 5.4 %copy-start = (f32[1,1,12,24,1024]{4,3,2,1,0:T(8,128)S(1)}, f32[1,1,12,24,1024]{4,3,2,1,0:T(8,128)}, u32[]{:S(2)}) copy-start(f32[1,1,12,24,1024]{4,3,2,1,0:T(8,128)} %blocks_ref.9) | copy-start | bytes 3538948
  0.6 0.9 %copy-start.1 = (s32[1,1,8,1024]{3,2,1,0:T(8,128)S(1)}, s32[1,1,8,1024]{3,2,1,0:T(8,128)}, u32[]{:S(2)}) copy-start(s32[1,1,8,1024]{3,2,1,0:T(8,128)} %ids_ref.1) | copy-start | bytes 98308
  1.5 0.7 copy-start.3
  2.2 3.9 %copy-start.2 = (f32[1,1,3,1024]{3,1,2,0:T(1,128)S(1)}, f32[1,1,3,1024]{3,1,2,0:T(1,128)}, u32[]{:S(2)}) copy-start(f32[1,1,3,1024]{3,1,2,0:T(1,128)} %param.8) | copy-start | bytes 36868
  12.4 11.8 %collective-permute-start = (f32[30,128]{1,0:T(8,128)S(1)}, f32[30,128]{1,0:T(8,128)S(1)}, u32[]{:S(2)}, u32[]{:S(2)}) collective-permute-start(f32[30,128]{1,0:T(8,128)S(1)} %get-tuple-element.57), channel_id=1, source_target_pairs={{0,31},{1,2},{2,1},{3,4},{4,3},{5,6},{6,5},{7,8},{8,7},{9,10},{10,... | collective-permute-start | bytes 46088 | tf_op jit(solution)/shard_map/ppermute | solution.py:659
  21.1 3.6 %collective-permute-start.1 = (f32[30,128]{1,0:T(8,128)S(1)}, f32[30,128]{1,0:T(8,128)S(1)}, u32[]{:S(2)}, u32[]{:S(2)}) collective-permute-start(f32[30,128]{1,0:T(8,128)S(1)} %get-tuple-element.58), channel_id=1, source_target_pairs={{0,224},{32,64},{64,32},{96,128},{128,96},{160,192},{192,160},{224... | collective-permute-start | bytes 46088 | tf_op jit(solution)/shard_map/ppermute | solution.py:659
  23.2 2.8 %collective-permute-start.2 = (f32[30,128]{1,0:T(8,128)S(1)}, f32[30,128]{1,0:T(8,128)S(1)}, u32[]{:S(2)}, u32[]{:S(2)}) collective-permute-start(f32[30,128]{1,0:T(8,128)S(1)} %get-tuple-element.59), channel_id=1, source_target_pairs={{0,1},{1,0},{2,3},{3,2},{4,5},{5,4},{6,7},{7,6},{8,9},{9,8},{10,11... | collective-permute-start | bytes 46088 | tf_op jit(solution)/shard_map/ppermute | solution.py:659
  23.2 2.8 %collective-permute-start.3 = (f32[30,128]{1,0:T(8,128)S(1)}, f32[30,128]{1,0:T(8,128)S(1)}, u32[]{:S(2)}, u32[]{:S(2)}) collective-permute-start(f32[30,128]{1,0:T(8,128)S(1)} %get-tuple-element.60), channel_id=1, source_target_pairs={{0,32},{32,0},{64,96},{96,64},{128,160},{160,128},{192,224},{224,1... | collective-permute-start | bytes 46088 | tf_op jit(solution)/shard_map/ppermute | solution.py:659
  30.1 5.9 %collective-permute-start.4 = (f32[12,128]{1,0:T(8,128)S(1)}, f32[12,128]{1,0:T(8,128)S(1)}, u32[]{:S(2)}, u32[]{:S(2)}) collective-permute-start(f32[12,128]{1,0:T(8,128)S(1)} %get-tuple-element.65), channel_id=1, source_target_pairs={{0,31},{1,2},{2,1},{3,4},{4,3},{5,6},{6,5},{7,8},{8,7},{9,10},{10,... | collective-permute-start | bytes 18440 | tf_op jit(solution)/shard_map/ppermute | solution.py:659
  31.1 4.8 %collective-permute-start.5 = (f32[12,128]{1,0:T(8,128)S(1)}, f32[12,128]{1,0:T(8,128)S(1)}, u32[]{:S(2)}, u32[]{:S(2)}) collective-permute-start(f32[12,128]{1,0:T(8,128)S(1)} %get-tuple-element.66), channel_id=1, source_target_pairs={{0,224},{32,64},{64,32},{96,128},{128,96},{160,192},{192,160},{224... | collective-permute-start | bytes 18440 | tf_op jit(solution)/shard_map/ppermute | solution.py:659
  34.4 2.8 %collective-permute-start.6 = (f32[12,128]{1,0:T(8,128)S(1)}, f32[12,128]{1,0:T(8,128)S(1)}, u32[]{:S(2)}, u32[]{:S(2)}) collective-permute-start(f32[12,128]{1,0:T(8,128)S(1)} %get-tuple-element.67), channel_id=1, source_target_pairs={{0,1},{1,0},{2,3},{3,2},{4,5},{5,4},{6,7},{7,6},{8,9},{9,8},{10,11... | collective-permute-start | bytes 18440 | tf_op jit(solution)/shard_map/ppermute | solution.py:659
  34.4 2.8 %collective-permute-start.7 = (f32[12,128]{1,0:T(8,128)S(1)}, f32[12,128]{1,0:T(8,128)S(1)}, u32[]{:S(2)}, u32[]{:S(2)}) collective-permute-start(f32[12,128]{1,0:T(8,128)S(1)} %get-tuple-element.68), channel_id=1, source_target_pairs={{0,32},{32,0},{64,96},{96,64},{128,160},{160,128},{192,224},{224,1... | collective-permute-start | bytes 18440 | tf_op jit(solution)/shard_map/ppermute | solution.py:659
  39.2 4.5 %collective-permute-start.10 = (f32[24,128]{1,0:T(8,128)S(1)}, f32[24,128]{1,0:T(8,128)S(1)}, u32[]{:S(2)}, u32[]{:S(2)}) collective-permute-start(f32[24,128]{1,0:T(8,128)S(1)} %get-tuple-element.73), channel_id=1, source_target_pairs={{0,1},{1,0},{2,3},{3,2},{4,5},{5,4},{6,7},{7,6},{8,9},{9,8},{10,11... | collective-permute-start | bytes 36872 | tf_op jit(solution)/shard_map/ppermute | solution.py:659
  39.4 4.3 %collective-permute-start.11 = (f32[24,128]{1,0:T(8,128)S(1)}, f32[24,128]{1,0:T(8,128)S(1)}, u32[]{:S(2)}, u32[]{:S(2)}) collective-permute-start(f32[24,128]{1,0:T(8,128)S(1)} %get-tuple-element.74), channel_id=1, source_target_pairs={{0,32},{32,0},{64,96},{96,64},{128,160},{160,128},{192,224},{224,1... | collective-permute-start | bytes 36872 | tf_op jit(solution)/shard_map/ppermute | solution.py:659
  41.3 5.9 %collective-permute-start.8 = (f32[24,128]{1,0:T(8,128)S(1)}, f32[24,128]{1,0:T(8,128)S(1)}, u32[]{:S(2)}, u32[]{:S(2)}) collective-permute-start(f32[24,128]{1,0:T(8,128)S(1)} %get-tuple-element.71), channel_id=1, source_target_pairs={{0,31},{1,2},{2,1},{3,4},{4,3},{5,6},{6,5},{7,8},{8,7},{9,10},{10,... | collective-permute-start | bytes 36872 | tf_op jit(solution)/shard_map/ppermute | solution.py:659
  43.7 3.5 %collective-permute-start.9 = (f32[24,128]{1,0:T(8,128)S(1)}, f32[24,128]{1,0:T(8,128)S(1)}, u32[]{:S(2)}, u32[]{:S(2)}) collective-permute-start(f32[24,128]{1,0:T(8,128)S(1)} %get-tuple-element.72), channel_id=1, source_target_pairs={{0,224},{32,64},{64,32},{96,128},{128,96},{160,192},{192,160},{224... | collective-permute-start | bytes 36872 | tf_op jit(solution)/shard_map/ppermute | solution.py:659
  48.6 5.9 %collective-permute-start.12 = (f32[12,128]{1,0:T(8,128)S(1)}, f32[12,128]{1,0:T(8,128)S(1)}, u32[]{:S(2)}, u32[]{:S(2)}) collective-permute-start(f32[12,128]{1,0:T(8,128)S(1)} %get-tuple-element.76), channel_id=1, source_target_pairs={{0,31},{1,2},{2,1},{3,4},{4,3},{5,6},{6,5},{7,8},{8,7},{9,10},{10,... | collective-permute-start | bytes 18440 | tf_op jit(solution)/shard_map/ppermute | solution.py:659
  51.1 3.5 %collective-permute-start.13 = (f32[12,128]{1,0:T(8,128)S(1)}, f32[12,128]{1,0:T(8,128)S(1)}, u32[]{:S(2)}, u32[]{:S(2)}) collective-permute-start(f32[12,128]{1,0:T(8,128)S(1)} %get-tuple-element.77), channel_id=1, source_target_pairs={{0,224},{32,64},{64,32},{96,128},{128,96},{160,192},{192,160},{224... | collective-permute-start | bytes 18440 | tf_op jit(solution)/shard_map/ppermute | solution.py:659
  52.3 2.8 %collective-permute-start.14 = (f32[12,128]{1,0:T(8,128)S(1)}, f32[12,128]{1,0:T(8,128)S(1)}, u32[]{:S(2)}, u32[]{:S(2)}) collective-permute-start(f32[12,128]{1,0:T(8,128)S(1)} %get-tuple-element.78), channel_id=1, source_target_pairs={{0,1},{1,0},{2,3},{3,2},{4,5},{5,4},{6,7},{7,6},{8,9},{9,8},{10,11... | collective-permute-start | bytes 18440 | tf_op jit(solution)/shard_map/ppermute | solution.py:659
  52.3 2.8 %collective-permute-start.15 = (f32[12,128]{1,0:T(8,128)S(1)}, f32[12,128]{1,0:T(8,128)S(1)}, u32[]{:S(2)}, u32[]{:S(2)}) collective-permute-start(f32[12,128]{1,0:T(8,128)S(1)} %get-tuple-element.79), channel_id=1, source_target_pairs={{0,32},{32,0},{64,96},{96,64},{128,160},{160,128},{192,224},{224,1... | collective-permute-start | bytes 18440 | tf_op jit(solution)/shard_map/ppermute | solution.py:659
  56.2 5.9 %collective-permute-start.16 = (f32[12,128]{1,0:T(8,128)S(1)}, f32[12,128]{1,0:T(8,128)S(1)}, u32[]{:S(2)}, u32[]{:S(2)}) collective-permute-start(f32[12,128]{1,0:T(8,128)S(1)} %get-tuple-element.84), channel_id=1, source_target_pairs={{0,1},{1,2},{2,3},{3,4},{4,5},{5,6},{6,7},{7,8},{8,9},{9,10},{10,1... | collective-permute-start | bytes 18440 | tf_op jit(solution)/shard_map/ppermute | solution.py:665
  57.0 5.1 %collective-permute-start.17 = (f32[12,128]{1,0:T(8,128)S(1)}, f32[12,128]{1,0:T(8,128)S(1)}, u32[]{:S(2)}, u32[]{:S(2)}) collective-permute-start(f32[12,128]{1,0:T(8,128)S(1)} %get-tuple-element.85), channel_id=1, source_target_pairs={{0,32},{32,64},{64,96},{96,128},{128,160},{160,192},{192,224},{224... | collective-permute-start | bytes 18440 | tf_op jit(solution)/shard_map/ppermute | solution.py:665
  62.9 21.2 %all-to-all-start = ((f32[256,1,128]{2,1,0:T(1,128)}), f32[256,1,128]{2,1,0:T(1,128)S(1)}, u32[]{:S(2)}, u32[]{:S(2)}) async-start(f32[256,1,128]{2,1,0:T(1,128)} %bitcast.2), calls=%async_computation | async-start | bytes 262144 | tf_op jit(solution)/shard_map/all_to_all | solution.py:754

commit v3 on v2

--- a/solution.py
+++ b/solution.py
@@ -14,6 +14,7 @@
 ITEM_ROWS = 64
 SIDES = 4
 PARTS = 2
+LIMIT = 54000
 AXES = ("band", "sector")
 epsilon = 1e-06
 F32 = jnp.float32
@@ -148,7 +149,7 @@
     return (found[0:rows] * 128.0 + found[rows : 2 * rows]).astype(I32)
 
 
-def plan_kernel(
+def make_plan(
     conn_ref, send_ref, conn_out, key_out, scan_out, end_out, own_out, pair_out, inverse_out, send_out, keys_ref
 ):
     for half in range(8):
@@ -421,11 +422,21 @@
             ref[3 * cone + start : 3 * cone + start + 1, :] = values[cone : cone + 1, :]
 
 
-def start_kernel(
-    blocks_ref, ids_ref, loads_ref, send_ref, *rest
-):
-    plan, (row_out, part_out, loads_out), rest = rest[:5], rest[5:8], rest[8:]
-    packets, (term, items, peaks) = rest[:4], rest[4:]
+def start_kernel(blocks_at, ids_at, send_at, *rest):
+    conn_out, plan, (inverse_out, send_out), rest = rest[0], rest[1:6], rest[6:8], rest[8:]
+    (row_out, part_out), packets, rest = rest[:2], rest[2:6], rest[6:]
+    blocks_ref, ids_ref, send_ref, keys, term, items, peaks, semaphores = rest
+    pairs = ((ids_at, ids_ref), (send_at, send_ref), (blocks_at, blocks_ref))
+    copies = [
+        pltpu.make_async_copy(source, target, semaphores.at[k])
+        for k, (source, target) in enumerate(pairs)
+    ]
+    for copy in copies:
+        copy.start()
+    copies[0].wait()
+    copies[1].wait()
+    copies[2].wait()
+    make_plan(ids_ref, send_ref, conn_out, *plan, inverse_out, send_out, keys)
     below, above = [live.astype(F32) for live in live_sides()]
     for chunk in range(CHUNKS):
         at = slice(chunk * LANES, (chunk + 1) * LANES)
@@ -437,34 +448,16 @@
     column_maxima(blocks_ref, row_out, term, 3)
     scatter_maxima(term, 6, plan, items, part_out)
     pack(part_out, 6, packets)
-    tables = [rows_of(loads_ref, 8 * c) for c in range(3)]
-    for c, values in enumerate(table_picks(tables, 8, send_ref[...])):
-        loads_out[8 * c : 8 * c + 8, :] = values
-    even_sector, even_band = even_places()
-    for slot, (even, low, high) in enumerate(
-        ((even_sector, 1, 0), (even_band, 3, 2), (even_sector, 0, 1), (even_band, 2, 3))
-    ):
-        for c in range(3):
-            packets[slot][24 + 2 * c : 26 + 2 * c, :] = jnp.where(
-                even,
-                loads_out[8 * c + 2 * high : 8 * c + 2 * high + 2, :],
-                loads_out[8 * c + 2 * low : 8 * c + 2 * low + 2, :],
-            )
 
 
 def sweep_kernel(
-    blocks_ref, conn_ref, row_ref, part_ref, own_loads, *rest
+    blocks_ref, conn_ref, row_ref, part_ref, loads_ref, send_ref, *rest
 ):
     plan, rest = rest[:5], rest[5:]
     arrived, rest = by_side(rest[:4]), rest[4:]
     row_out, scale_out, part_out, loads_out, rest = rest[0], rest[1], rest[2], rest[3], rest[4:]
     packets, (term, items, peaks, merged, second_row) = rest[:4], rest[4:]
     unpack(part_ref, 6, arrived, jnp.maximum, merged)
-    for c in range(3):
-        loads_out[NODE_ROWS * c : NODE_ROWS * c + 8, :] = own_loads[8 * c : 8 * c + 8, :]
-        for side in range(SIDES):
-            base = NODE_ROWS * c + 8 + 2 * side
-            loads_out[base : base + 2, :] = arrived[side][24 + 2 * c : 26 + 2 * c]
     row = lax.broadcasted_iota(I32, (NODE_ROWS, LANES), 0)
     below, above = [live.astype(F32) for live in live_sides()]
     start = jnp.where(row < 12, 1.0, jnp.where(row < 14, below, above))
@@ -485,6 +478,19 @@
     column_maxima(blocks_ref, second_row, term, 0)
     scatter_maxima(term, 3, plan, items, part_out)
     pack(part_out, 3, packets)
+    tables = [rows_of(loads_ref, 8 * c) for c in range(3)]
+    for c, values in enumerate(table_picks(tables, 8, send_ref[...])):
+        loads_out[8 * c : 8 * c + 8, :] = values
+    even_sector, even_band = even_places()
+    for slot, (even, low, high) in enumerate(
+        ((even_sector, 1, 0), (even_band, 3, 2), (even_sector, 0, 1), (even_band, 2, 3))
+    ):
+        for c in range(3):
+            packets[slot][12 + 2 * c : 14 + 2 * c, :] = jnp.where(
+                even,
+                loads_out[8 * c + 2 * high : 8 * c + 2 * high + 2, :],
+                loads_out[8 * c + 2 * low : 8 * c + 2 * low + 2, :],
+            )
 
 
 def target_kernel(
@@ -496,14 +502,18 @@
     loads_ref,
     *rest,
 ):
-    arrived, rest = rest[:4], rest[4:]
+    arrived, rest = by_side(rest[:4]), rest[4:]
     scale_out, strain_out, part_out, rest = rest[0], rest[1], rest[2], rest[3:]
     packets, (term, table, strain, cones) = rest[:4], rest[4:]
-    arrived = by_side(arrived)
     unpack(part_ref, 3, arrived, jnp.maximum, table)
     scale = rescale(scale_ref[...], table[...])
     scale_out[...] = scale
-    table[...] = scale * (scale * loads_ref[...])
+    for c in range(3):
+        table[NODE_ROWS * c : NODE_ROWS * c + 8, :] = loads_ref[8 * c : 8 * c + 8, :]
+        for side in range(SIDES):
+            base = NODE_ROWS * c + 8 + 2 * side
+            table[base : base + 2, :] = arrived[side][12 + 2 * c : 14 + 2 * c]
+    table[...] = scale * (scale * table[...])
     apply_blocks(blocks_ref, table, 1, conn_ref, strain)
     row = row_ref[...]
     image = row * strain[0:STRAINS, :]
@@ -570,10 +580,7 @@
             packet[4 * channel + 2 : 4 * channel + 4, :] = side_rows(part_out, side + 4, channel)
 
 
-def norm_kernel(
-    part_ref, norm_ref, scale_ref, loads_ref, joint_ref, inverse_ref, left_ref, below_ref, *rest
-):
-    sums_out, velocity_out, lines = rest
+def norm_kernel(part_ref, norm_ref, left_ref, below_ref, sums_out):
     below, above = live_sides()
     squares = jnp.zeros((2, LANES), F32)
     for channel in range(3):
@@ -585,15 +592,18 @@
             squares = squares + own * own + copy * copy
         alone = jnp.where(above, 0.0, side_rows(part_ref, 3, channel))
         squares = squares + alone * alone
-    first = jnp.sum(norm_ref[...], axis=1, keepdims=True)
-    last = jnp.sum(jnp.sum(squares, axis=0, keepdims=True), axis=1, keepdims=True)
+    last = jnp.sum(squares, axis=0, keepdims=True)
+    first = norm_ref[...]
     lane = lax.broadcasted_iota(I32, (1, LANES), 1)
-    line = jnp.where(lane == 0, first, jnp.where(lane == 1, last, 0.0))
+    line = jnp.where(lane < 64, first + pltpu.roll(first, 64, 1), last + pltpu.roll(last, 64, 1))
     sums_out[...] = jnp.broadcast_to(line, sums_out.shape)
+
+
+def lines_kernel(scale_ref, loads_ref, joint_ref, inverse_ref, velocity_out, lines):
     for c in range(3):
         base = NODE_ROWS * c
         scale = scale_ref[base : base + 8, :]
-        lines[8 * c : 8 * c + 8, :] = scale * (scale * loads_ref[base : base + 8, :])
+        lines[8 * c : 8 * c + 8, :] = scale * (scale * loads_ref[8 * c : 8 * c + 8, :])
         lines[24 + 8 * c : 32 + 8 * c, :] = scale * joint_ref[base : base + 8, :]
     tables = [rows_of(lines, 8 * channel) for channel in range(6)]
     for channel, values in enumerate(table_picks(tables, 8, inverse_ref[...])):
@@ -606,8 +616,8 @@
     velocity, cones, flat, semaphores = rest
     sums = jnp.sum(sums_ref[...], axis=0, keepdims=True)
     lane = lax.broadcasted_iota(I32, (1, LANES), 1)
-    before = jnp.sum(jnp.where(lane == 0, sums, 0.0), axis=1, keepdims=True)
-    after = jnp.sum(jnp.where(lane == 1, sums, 0.0), axis=1, keepdims=True)
+    before = jnp.sum(jnp.where(lane < 64, sums, 0.0), axis=1, keepdims=True)
+    after = jnp.sum(jnp.where(lane < 64, 0.0, sums), axis=1, keepdims=True)
     largest = jnp.sqrt(after + epsilon) / jnp.sqrt(before + epsilon)
     step = step_ref[0] / jnp.sqrt(largest)
     square = step * step
@@ -628,9 +638,9 @@
     second.wait()
 
 
-def call(body, out_shapes, scratch, *arrays, smem=(), outside_results=False, work=0):
+def call(body, out_shapes, scratch, *arrays, smem=(), outside=(), outside_results=False, work=0, limit=24 * 1024):
     def space(i):
-        return pltpu.SMEM if i in smem else pltpu.VMEM
+        return pltpu.SMEM if i in smem else pltpu.HBM if i in outside else pltpu.VMEM
 
     result = pltpu.HBM if outside_results else pltpu.VMEM
     return pl.pallas_call(
@@ -642,7 +652,7 @@
             entry if not isinstance(entry, tuple) else pltpu.VMEM(*entry) for entry in scratch
         ],
         cost_estimate=pl.CostEstimate(flops=work, bytes_accessed=work // 256, transcendentals=0),
-        compiler_params=pltpu.CompilerParams(vmem_limit_bytes=24 * 1024 * 1024),
+        compiler_params=pltpu.CompilerParams(vmem_limit_bytes=limit * 1024),
     )(*arrays)
 
 
@@ -673,33 +683,39 @@
     twice = ((6 * ITEM_ROWS, LANES), F32)
     ids = ((64, LANES), I32)
     few = ((8, LANES), I32)
-    conn, *plan, inverse, send = call(
-        plan_kernel,
-        [ids, ((SORTED_ROWS, LANES), I32), few, ((16, LANES), I32), few, ((16, LANES), I32), few, few],
-        [ids],
+    conn, *rest = call(
+        start_kernel,
+        [ids, ((SORTED_ROWS, LANES), I32), few, ((16, LANES), I32), few, ((16, LANES), I32), few, few]
+        + [rows, ((96, LANES), F32)]
+        + [((24, LANES), F32)] * 4,
+        [
+            ((1, 1, STRAINS, 24, 1024), F32),
+            ((1, 1, 8, 1024), I32),
+            ((1, 1, SIDES, 256), I32),
+            ids,
+            twice,
+            ((6 * SORTED_ROWS, LANES), F32),
+            rows,
+            pltpu.SemaphoreType.DMA((3,)),
+        ],
+        blocks,
         connectivity,
         send_lists,
-        work=4_000_000_000,
-    )
-    row, part, own_loads, *packets = call(
-        start_kernel,
-        [rows, ((96, LANES), F32), ((24, LANES), F32)] + [((30, LANES), F32)] * 4,
-        [twice, ((6 * SORTED_ROWS, LANES), F32), rows],
-        blocks,
-        connectivity,
-        nodal_loads.reshape(24, LANES),
-        send,
-        *plan,
-    )
+        outside=(0, 1, 2),
+        limit=LIMIT,
+        work=12_000_000_000,
+    )
+    plan, (inverse, send, row, part), packets = rest[:5], rest[5:9], rest[9:]
     row, scale, part, loads, *packets = call(
         sweep_kernel,
-        [rows, nodes, nodes, nodes] + packet,
+        [rows, nodes, nodes, ((24, LANES), F32)] + [((18, LANES), F32)] * 4,
         [items, ((3 * SORTED_ROWS, LANES), F32), ((2 * STRAINS, 1024), F32), ((96, LANES), F32), rows],
         blocks,
         conn,
         row,
         part,
-        own_loads,
+        nodal_loads.reshape(24, LANES),
+        send,
         *plan,
         *exchange(packets),
     )
@@ -738,18 +754,24 @@
         *exchange(packets),
     )
     count = lax.axis_size("band") * lax.axis_size("sector")
-    sums, lines = call(
+    (sums,) = call(
         norm_kernel,
-        [((count, LANES), F32), ((48, LANES), F32)],
-        [nodes],
+        [((count, LANES), F32)],
+        [],
         part,
         norm,
+        shift_up(right, "sector"),
+        shift_up(above, "band"),
+    )
+    (lines,) = call(
+        lines_kernel,
+        [((48, LANES), F32)],
+        [nodes],
         scale,
         loads,
         joint,
         inverse,
-        shift_up(right, "sector"),
-        shift_up(above, "band"),
+        work=600_000_000,
     )
     sums = lax.all_to_all(sums, AXES, 0, 0, tiled=True)
     velocities, multipliers = call(

time: 85.4 us -> 83.5 us (0.978)
  Pallas kernels: 20.5 us -> 18.6 us
    pallas_call x8, Pallas kernels: 20.5 us -> 18.6 us  [call(): pl.pallas_call(body, out_shape=[jax.ShapeDtypeStruct(shape, kind) for sha...]
where the time goes in v3:
time: 83.5 us; the launch traced here: 83.3 us
  starting transfers between devices  34.9 us (42%)
  waiting for transfers between devices  26.7 us (32%)
  Pallas kernels  18.6 us (22%)
  local copies, waits for them, and re-layouts  1.54 us (2%)
  between operations  1.53 us (2%)
    ppermute x16, starting transfers between devices, exchange(): lax.ppermute(packet, axis, swap_pairs(axis, odd))  25.4 us
    pallas_call x8, Pallas kernels, call(): pl.pallas_call(body, out_shape=[jax.ShapeDtypeStruct(shape, kind) for sha...  18.6 us
    all_to_all x1, waiting for transfers between devices, per_device(): sums = lax.all_to_all(sums, AXES, 0, 0, tiled=True)  12.4 us
    ppermute x16, waiting for transfers between devices, exchange(): lax.ppermute(packet, axis, swap_pairs(axis, odd))  9.91 us
    all_to_all x1, starting transfers between devices, per_device(): sums = lax.all_to_all(sums, AXES, 0, 0, tiled=True)  7.97 us
    ppermute x2, waiting for transfers between devices, shift_up(): lax.ppermute(packet, axis, [(i, (i + 1) % count) for i in range(count)])  4.36 us
  transfers between devices with their start and end apart: 19, of which 9 were waited for; matrix products, arithmetic and copies ran while one was open for 0% of the time, Pallas kernels for 0%

profile of v3, /device:TPU:1, one launch (start us, length us, event | category | flops | bytes accessed | tf_op | source)
XLA Modules:
  0.0 83.3 jit_solution(12213044928233532420)
XLA Ops:
  0.7 0.8 %copy-done.2 = s32[1,1,8,1024]{3,2,1,0:T(8,128)S(1)} copy-done((s32[1,1,8,1024]{3,2,1,0:T(8,128)S(1)}, s32[1,1,8,1024]{3,2,1,0:T(8,128)}, u32[]{:S(2)}) %copy-start.2) | copy-done | bytes 32792
  1.5 0.7 copy-done.3
  2.2 7.8 %shard_map.68 = (s32[64,128]{1,0:T(8,128)S(1)}, s32[40,128]{1,0:T(8,128)S(1)}, s32[8,128]{1,0:T(8,128)S(1)}, s32[16,128]{1,0:T(8,128)S(1)}, s32[8,128]{1,0:T(8,1...) custom-call(f32[1,1,12,24,1024]{4,3,2,1,0:T(8,128)} %blocks_ref.7, ...), custom_call_target="tpu_custom_call" | custom-call | flops 12000000000 | bytes 46875000 | tf_op jit(solution)/shard_map/pallas_call | solution.py:646
  10.0 8.7 %collective-permute-start = (f32[24,128]{1,0:T(8,128)S(1)}, f32[24,128]{1,0:T(8,128)S(1)}, u32[]{:S(2)}, u32[]{:S(2)}) collective-permute-start(f32[24,128]{1,0:T(8,128)S(1)} %get-tuple-element.53), channel_id=1, source_target_pairs={{0,31},{1,2},{2,1},{3,4},{4,3},{5,6},{6,5},{7,8},{8,7},{9,10},{10,... | collective-permute-start | bytes 36872 | tf_op jit(solution)/shard_map/ppermute | solution.py:669
  18.7 2.1 %collective-permute-start.1 = (f32[24,128]{1,0:T(8,128)S(1)}, f32[24,128]{1,0:T(8,128)S(1)}, u32[]{:S(2)}, u32[]{:S(2)}) collective-permute-start(f32[24,128]{1,0:T(8,128)S(1)} %get-tuple-element.54), channel_id=1, source_target_pairs={{0,224},{32,64},{64,32},{96,128},{128,96},{160,192},{192,160},{224... | collective-permute-start | bytes 36872 | tf_op jit(solution)/shard_map/ppermute | solution.py:669
  20.8 0.0 collective-permute-start.2
  20.8 1.0 %collective-permute-start.3 = (f32[24,128]{1,0:T(8,128)S(1)}, f32[24,128]{1,0:T(8,128)S(1)}, u32[]{:S(2)}, u32[]{:S(2)}) collective-permute-start(f32[24,128]{1,0:T(8,128)S(1)} %get-tuple-element.56), channel_id=1, source_target_pairs={{0,32},{32,0},{64,96},{96,64},{128,160},{160,128},{192,224},{224,1... | collective-permute-start | bytes 36872 | tf_op jit(solution)/shard_map/ppermute | solution.py:669
  21.8 0.0 collective-permute-done.rest_5_
  21.8 0.4 collective-permute-done.1.rest_6_
  22.2 1.4 %collective-permute-done.2.rest_7_ = f32[24,128]{1,0:T(8,128)S(1)} collective-permute-done((f32[24,128]{1,0:T(8,128)S(1)}, f32[24,128]{1,0:T(8,128)S(1)}, u32[]{:S(2)}, u32[]{:S(2)}) %collective-permute-start.2) | collective-permute-done | bytes 12320 | tf_op jit(solution)/shard_map/ppermute | solution.py:669
  23.6 0.0 collective-permute-done.3.rest_8_
  23.6 4.1 %shard_map.69 = (f32[12,1024]{1,0:T(8,128)S(1)}, f32[48,128]{1,0:T(8,128)S(1)}, f32[48,128]{1,0:T(8,128)S(1)}, f32[24,128]{1,0:T(8,128)S(1)}, f32[18,128]{1,0:T(...) custom-call(f32[1,1,12,24,1024]{4,3,2,1,0:T(8,128)S(1)} %copy-done, ...), custom_call_target="tpu_custom_call" | custom-call | tf_op jit(solution)/shard_map/pallas_call | solution.py:646
  27.7 1.1 %collective-permute-start.4 = (f32[18,128]{1,0:T(8,128)S(1)}, f32[18,128]{1,0:T(8,128)S(1)}, u32[]{:S(2)}, u32[]{:S(2)}) collective-permute-start(f32[18,128]{1,0:T(8,128)S(1)} %get-tuple-element.61), channel_id=1, source_target_pairs={{0,31},{1,2},{2,1},{3,4},{4,3},{5,6},{6,5},{7,8},{8,7},{9,10},{10,... | collective-permute-start | bytes 27656 | tf_op jit(solution)/shard_map/ppermute | solution.py:669
  28.8 3.3 %collective-permute-start.5 = (f32[18,128]{1,0:T(8,128)S(1)}, f32[18,128]{1,0:T(8,128)S(1)}, u32[]{:S(2)}, u32[]{:S(2)}) collective-permute-start(f32[18,128]{1,0:T(8,128)S(1)} %get-tuple-element.62), channel_id=1, source_target_pairs={{0,224},{32,64},{64,32},{96,128},{128,96},{160,192},{192,160},{224... | collective-permute-start | bytes 27656 | tf_op jit(solution)/shard_map/ppermute | solution.py:669
  32.1 0.0 collective-permute-start.6
  32.1 0.0 collective-permute-start.7
  32.1 1.6 %collective-permute-done.4.rest_0_ = f32[18,128]{1,0:T(8,128)S(1)} collective-permute-done((f32[18,128]{1,0:T(8,128)S(1)}, f32[18,128]{1,0:T(8,128)S(1)}, u32[]{:S(2)}, u32[]{:S(2)}) %collective-permute-start.4) | collective-permute-done | bytes 9248 | tf_op jit(solution)/shard_map/ppermute | solution.py:669
  33.7 0.0 collective-permute-done.5.rest_1_
  33.7 1.3 %collective-permute-done.6.rest_2_ = f32[18,128]{1,0:T(8,128)S(1)} collective-permute-done((f32[18,128]{1,0:T(8,128)S(1)}, f32[18,128]{1,0:T(8,128)S(1)}, u32[]{:S(2)}, u32[]{:S(2)}) %collective-permute-start.6) | collective-permute-done | bytes 9248 | tf_op jit(solution)/shard_map/ppermute | solution.py:669
  35.0 0.0 collective-permute-done.7.rest_3_
  35.0 2.1 %shard_map.70 = (f32[48,128]{1,0:T(8,128)S(1)}, f32[12,1024]{1,0:T(8,128)S(1)}, f32[96,128]{1,0:T(8,128)S(1)}, f32[24,128]{1,0:T(8,128)S(1)}, f32[24,128]{1,0:T(...) custom-call(f32[1,1,12,24,1024]{4,3,2,1,0:T(8,128)S(1)} %copy-done, s32[64,128]{1,0:T(8,128)S(1)} %get-tuple-element.44.conn_ref, ...), custom_call_target="tpu_custom_call" | custom-call | tf_op jit(solution)/shard_map/pallas_call | solution.py:646
  37.1 0.4 collective-permute-start.10
  37.5 1.8 %collective-permute-start.11 = (f32[24,128]{1,0:T(8,128)S(1)}, f32[24,128]{1,0:T(8,128)S(1)}, u32[]{:S(2)}, u32[]{:S(2)}) collective-permute-start(f32[24,128]{1,0:T(8,128)S(1)} %get-tuple-element.70), channel_id=1, source_target_pairs={{0,32},{32,0},{64,96},{96,64},{128,160},{160,128},{192,224},{224,1... | collective-permute-start | bytes 36872 | tf_op jit(solution)/shard_map/ppermute | solution.py:669
  39.3 2.4 %collective-permute-start.8 = (f32[24,128]{1,0:T(8,128)S(1)}, f32[24,128]{1,0:T(8,128)S(1)}, u32[]{:S(2)}, u32[]{:S(2)}) collective-permute-start(f32[24,128]{1,0:T(8,128)S(1)} %get-tuple-element.67), channel_id=1, source_target_pairs={{0,31},{1,2},{2,1},{3,4},{4,3},{5,6},{6,5},{7,8},{8,7},{9,10},{10,... | collective-permute-start | bytes 36872 | tf_op jit(solution)/shard_map/ppermute | solution.py:669
  41.7 0.1 collective-permute-start.9
  41.8 0.0 collective-permute-done.10.rest_2_
  41.8 0.0 collective-permute-done.11.rest_3_
  41.8 3.4 %collective-permute-done.8.rest_0_ = f32[24,128]{1,0:T(8,128)S(1)} collective-permute-done((f32[24,128]{1,0:T(8,128)S(1)}, f32[24,128]{1,0:T(8,128)S(1)}, u32[]{:S(2)}, u32[]{:S(2)}) %collective-permute-start.8) | collective-permute-done | bytes 12320 | tf_op jit(solution)/shard_map/ppermute | solution.py:669
  45.2 0.0 collective-permute-done.9.rest_1_
  45.2 1.5 %shard_map.71 = (f32[48,128]{1,0:T(8,128)S(1)}, f32[12,1024]{1,0:T(8,128)S(1)}, f32[48,128]{1,0:T(8,128)S(1)}, f32[12,128]{1,0:T(8,128)S(1)}, f32[12,128]{1,0:T(...) custom-call(f32[1,1,12,24,1024]{4,3,2,1,0:T(8,128)S(1)} %copy-done, s32[64,128]{1,0:T(8,128)S(1)} %get-tuple-element.44.conn_ref, ...), custom_call_target="tpu_custom_call" | custom-call | tf_op jit(solution)/shard_map/pallas_call | solution.py:646
  46.7 2.5 %collective-permute-start.12 = (f32[12,128]{1,0:T(8,128)S(1)}, f32[12,128]{1,0:T(8,128)S(1)}, u32[]{:S(2)}, u32[]{:S(2)}) collective-permute-start(f32[12,128]{1,0:T(8,128)S(1)} %get-tuple-element.72), channel_id=1, source_target_pairs={{0,31},{1,2},{2,1},{3,4},{4,3},{5,6},{6,5},{7,8},{8,7},{9,10},{10,... | collective-permute-start | bytes 18440 | tf_op jit(solution)/shard_map/ppermute | solution.py:669
  49.2 1.2 %collective-permute-start.13 = (f32[12,128]{1,0:T(8,128)S(1)}, f32[12,128]{1,0:T(8,128)S(1)}, u32[]{:S(2)}, u32[]{:S(2)}) collective-permute-start(f32[12,128]{1,0:T(8,128)S(1)} %get-tuple-element.73), channel_id=1, source_target_pairs={{0,224},{32,64},{64,32},{96,128},{128,96},{160,192},{192,160},{224... | collective-permute-start | bytes 18440 | tf_op jit(solution)/shard_map/ppermute | solution.py:669
  50.4 0.0 collective-permute-start.14
  50.4 0.9 %collective-permute-start.15 = (f32[12,128]{1,0:T(8,128)S(1)}, f32[12,128]{1,0:T(8,128)S(1)}, u32[]{:S(2)}, u32[]{:S(2)}) collective-permute-start(f32[12,128]{1,0:T(8,128)S(1)} %get-tuple-element.75), channel_id=1, source_target_pairs={{0,32},{32,0},{64,96},{96,64},{128,160},{160,128},{192,224},{224,1... | collective-permute-start | bytes 18440 | tf_op jit(solution)/shard_map/ppermute | solution.py:669
  51.3 1.3 %collective-permute-done.12.rest_0_ = f32[12,128]{1,0:T(8,128)S(1)} collective-permute-done((f32[12,128]{1,0:T(8,128)S(1)}, f32[12,128]{1,0:T(8,128)S(1)}, u32[]{:S(2)}, u32[]{:S(2)}) %collective-permute-start.12) | collective-permute-done | bytes 6176 | tf_op jit(solution)/shard_map/ppermute | solution.py:669
  52.6 0.0 collective-permute-done.13.rest_1_
  52.6 0.5 collective-permute-done.14.rest_2_
  53.2 0.0 collective-permute-done.15.rest_3_
  53.2 1.2 %shard_map.72 = (f32[1,128]{1,0:T(1,128)S(1)}, f32[48,128]{1,0:T(8,128)S(1)}, f32[12,128]{1,0:T(8,128)S(1)}, f32[12,128]{1,0:T(8,128)S(1)}) custom-call(f32[1,1,12,24,1024]{4,3,2,1,0:T(8,128)S(1)} %copy-done, s32[64,128]{1,0:T(8,128)S(1)} %get-tuple-element.44.conn_ref, f32[12,1024]{1,0:T(8,128)S(1)} %get-tuple-element.57.row_ref, ...), custom_call_target="tpu_custom_call" | custom-call | tf_op jit(solution)/shard_map/pallas_call | solution.py:646
  54.4 0.8 collective-permute-start.16
  55.2 0.8 collective-permute-start.17
  56.0 4.4 %collective-permute-done.16.left_ref = f32[12,128]{1,0:T(8,128)S(1)} collective-permute-done((f32[12,128]{1,0:T(8,128)S(1)}, f32[12,128]{1,0:T(8,128)S(1)}, u32[]{:S(2)}, u32[]{:S(2)}) %collective-permute-start.16) | collective-permute-done | bytes 6176 | tf_op jit(solution)/shard_map/ppermute | solution.py:675
  60.3 0.0 collective-permute-done.17.below_ref
  60.3 0.8 shard_map.73
  61.1 8.0 %all-to-all-start = ((f32[256,1,128]{2,1,0:T(1,128)}), f32[256,1,128]{2,1,0:T(1,128)S(1)}, u32[]{:S(2)}, u32[]{:S(2)}) async-start(f32[256,1,128]{2,1,0:T(1,128)} %bitcast.2), calls=%async_computation | async-start | bytes 262144 | tf_op jit(solution)/shard_map/all_to_all | solution.py:776
  69.7 0.1 shard_map.74.velocity_ref
  69.8 12.4 %all-to-all-done = f32[256,1,128]{2,1,0:T(1,128)S(1)} async-done(((f32[256,1,128]{2,1,0:T(1,128)}), f32[256,1,128]{2,1,0:T(1,128)S(1)}, u32[]{:S(2)}, u32[]{:S(2)}) %all-to-all-start) | async-done | bytes 131104 | tf_op jit(solution)/shard_map/all_to_all | solution.py:776
  82.2 0.9 %shard_map.75 = (f32[24,128]{1,0:T(8,128)}, f32[96,128]{1,0:T(8,128)}) custom-call(f32[256,128]{1,0:T(8,128)S(1)} %bitcast.7, f32[1]{0:T(128)S(6)} %copy.14.step_ref, f32[48,128]{1,0:T(8,128)S(1)} %shard_map.74.velocity_ref, f32[12,1024]{1,0:T(8,128)S(1)} %get-tuple-element.82.base_ref, f32[12,1024]{1,0:T(8,128)S(1)} %get-tuple-element.83.joint_ref, ...), custom_call_target="tpu_custom_call" | custom-call | tf_op jit(solution)/shard_map/pallas_call | solution.py:646
  (6 shorter events, 0.0 us)
Async XLA Ops:
  0.6 23.0 %copy-start = (f32[1,1,12,24,1024]{4,3,2,1,0:T(8,128)S(1)}, f32[1,1,12,24,1024]{4,3,2,1,0:T(8,128)}, u32[]{:S(2)}) copy-start(f32[1,1,12,24,1024]{4,3,2,1,0:T(8,128)} %blocks_ref.7) | copy-start | bytes 3538948
  0.6 23.0 %copy-start.1 = (f32[1,1,3,1024]{3,1,2,0:T(1,128)S(1)}, f32[1,1,3,1024]{3,1,2,0:T(1,128)}, u32[]{:S(2)}) copy-start(f32[1,1,3,1024]{3,1,2,0:T(1,128)} %param.8) | copy-start | bytes 36868
  0.7 0.9 %copy-start.2 = (s32[1,1,8,1024]{3,2,1,0:T(8,128)S(1)}, s32[1,1,8,1024]{3,2,1,0:T(8,128)}, u32[]{:S(2)}) copy-start(s32[1,1,8,1024]{3,2,1,0:T(8,128)} %ids_at.1) | copy-start | bytes 98308
  1.5 0.7 copy-start.3
  10.0 11.8 %collective-permute-start = (f32[24,128]{1,0:T(8,128)S(1)}, f32[24,128]{1,0:T(8,128)S(1)}, u32[]{:S(2)}, u32[]{:S(2)}) collective-permute-start(f32[24,128]{1,0:T(8,128)S(1)} %get-tuple-element.53), channel_id=1, source_target_pairs={{0,31},{1,2},{2,1},{3,4},{4,3},{5,6},{6,5},{7,8},{8,7},{9,10},{10,... | collective-permute-start | bytes 36872 | tf_op jit(solution)/shard_map/ppermute | solution.py:669
  18.7 3.5 %collective-permute-start.1 = (f32[24,128]{1,0:T(8,128)S(1)}, f32[24,128]{1,0:T(8,128)S(1)}, u32[]{:S(2)}, u32[]{:S(2)}) collective-permute-start(f32[24,128]{1,0:T(8,128)S(1)} %get-tuple-element.54), channel_id=1, source_target_pairs={{0,224},{32,64},{64,32},{96,128},{128,96},{160,192},{192,160},{224... | collective-permute-start | bytes 36872 | tf_op jit(solution)/shard_map/ppermute | solution.py:669
  20.8 2.8 %collective-permute-start.2 = (f32[24,128]{1,0:T(8,128)S(1)}, f32[24,128]{1,0:T(8,128)S(1)}, u32[]{:S(2)}, u32[]{:S(2)}) collective-permute-start(f32[24,128]{1,0:T(8,128)S(1)} %get-tuple-element.55), channel_id=1, source_target_pairs={{0,1},{1,0},{2,3},{3,2},{4,5},{5,4},{6,7},{7,6},{8,9},{9,8},{10,11... | collective-permute-start | bytes 36872 | tf_op jit(solution)/shard_map/ppermute | solution.py:669
  20.8 2.8 %collective-permute-start.3 = (f32[24,128]{1,0:T(8,128)S(1)}, f32[24,128]{1,0:T(8,128)S(1)}, u32[]{:S(2)}, u32[]{:S(2)}) collective-permute-start(f32[24,128]{1,0:T(8,128)S(1)} %get-tuple-element.56), channel_id=1, source_target_pairs={{0,32},{32,0},{64,96},{96,64},{128,160},{160,128},{192,224},{224,1... | collective-permute-start | bytes 36872 | tf_op jit(solution)/shard_map/ppermute | solution.py:669
  27.7 6.0 %collective-permute-start.4 = (f32[18,128]{1,0:T(8,128)S(1)}, f32[18,128]{1,0:T(8,128)S(1)}, u32[]{:S(2)}, u32[]{:S(2)}) collective-permute-start(f32[18,128]{1,0:T(8,128)S(1)} %get-tuple-element.61), channel_id=1, source_target_pairs={{0,31},{1,2},{2,1},{3,4},{4,3},{5,6},{6,5},{7,8},{8,7},{9,10},{10,... | collective-permute-start | bytes 27656 | tf_op jit(solution)/shard_map/ppermute | solution.py:669
  28.8 4.9 %collective-permute-start.5 = (f32[18,128]{1,0:T(8,128)S(1)}, f32[18,128]{1,0:T(8,128)S(1)}, u32[]{:S(2)}, u32[]{:S(2)}) collective-permute-start(f32[18,128]{1,0:T(8,128)S(1)} %get-tuple-element.62), channel_id=1, source_target_pairs={{0,224},{32,64},{64,32},{96,128},{128,96},{160,192},{192,160},{224... | collective-permute-start | bytes 27656 | tf_op jit(solution)/shard_map/ppermute | solution.py:669
  32.1 2.8 %collective-permute-start.6 = (f32[18,128]{1,0:T(8,128)S(1)}, f32[18,128]{1,0:T(8,128)S(1)}, u32[]{:S(2)}, u32[]{:S(2)}) collective-permute-start(f32[18,128]{1,0:T(8,128)S(1)} %get-tuple-element.63), channel_id=1, source_target_pairs={{0,1},{1,0},{2,3},{3,2},{4,5},{5,4},{6,7},{7,6},{8,9},{9,8},{10,11... | collective-permute-start | bytes 27656 | tf_op jit(solution)/shard_map/ppermute | solution.py:669
  32.1 2.8 %collective-permute-start.7 = (f32[18,128]{1,0:T(8,128)S(1)}, f32[18,128]{1,0:T(8,128)S(1)}, u32[]{:S(2)}, u32[]{:S(2)}) collective-permute-start(f32[18,128]{1,0:T(8,128)S(1)} %get-tuple-element.64), channel_id=1, source_target_pairs={{0,32},{32,0},{64,96},{96,64},{128,160},{160,128},{192,224},{224,1... | collective-permute-start | bytes 27656 | tf_op jit(solution)/shard_map/ppermute | solution.py:669
  37.1 4.7 %collective-permute-start.10 = (f32[24,128]{1,0:T(8,128)S(1)}, f32[24,128]{1,0:T(8,128)S(1)}, u32[]{:S(2)}, u32[]{:S(2)}) collective-permute-start(f32[24,128]{1,0:T(8,128)S(1)} %get-tuple-element.69), channel_id=1, source_target_pairs={{0,1},{1,0},{2,3},{3,2},{4,5},{5,4},{6,7},{7,6},{8,9},{9,8},{10,11... | collective-permute-start | bytes 36872 | tf_op jit(solution)/shard_map/ppermute | solution.py:669
  37.5 4.3 %collective-permute-start.11 = (f32[24,128]{1,0:T(8,128)S(1)}, f32[24,128]{1,0:T(8,128)S(1)}, u32[]{:S(2)}, u32[]{:S(2)}) collective-permute-start(f32[24,128]{1,0:T(8,128)S(1)} %get-tuple-element.70), channel_id=1, source_target_pairs={{0,32},{32,0},{64,96},{96,64},{128,160},{160,128},{192,224},{224,1... | collective-permute-start | bytes 36872 | tf_op jit(solution)/shard_map/ppermute | solution.py:669
  39.3 5.9 %collective-permute-start.8 = (f32[24,128]{1,0:T(8,128)S(1)}, f32[24,128]{1,0:T(8,128)S(1)}, u32[]{:S(2)}, u32[]{:S(2)}) collective-permute-start(f32[24,128]{1,0:T(8,128)S(1)} %get-tuple-element.67), channel_id=1, source_target_pairs={{0,31},{1,2},{2,1},{3,4},{4,3},{5,6},{6,5},{7,8},{8,7},{9,10},{10,... | collective-permute-start | bytes 36872 | tf_op jit(solution)/shard_map/ppermute | solution.py:669
  41.7 3.5 %collective-permute-start.9 = (f32[24,128]{1,0:T(8,128)S(1)}, f32[24,128]{1,0:T(8,128)S(1)}, u32[]{:S(2)}, u32[]{:S(2)}) collective-permute-start(f32[24,128]{1,0:T(8,128)S(1)} %get-tuple-element.68), channel_id=1, source_target_pairs={{0,224},{32,64},{64,32},{96,128},{128,96},{160,192},{192,160},{224... | collective-permute-start | bytes 36872 | tf_op jit(solution)/shard_map/ppermute | solution.py:669
  46.7 5.9 %collective-permute-start.12 = (f32[12,128]{1,0:T(8,128)S(1)}, f32[12,128]{1,0:T(8,128)S(1)}, u32[]{:S(2)}, u32[]{:S(2)}) collective-permute-start(f32[12,128]{1,0:T(8,128)S(1)} %get-tuple-element.72), channel_id=1, source_target_pairs={{0,31},{1,2},{2,1},{3,4},{4,3},{5,6},{6,5},{7,8},{8,7},{9,10},{10,... | collective-permute-start | bytes 18440 | tf_op jit(solution)/shard_map/ppermute | solution.py:669
  49.2 3.5 %collective-permute-start.13 = (f32[12,128]{1,0:T(8,128)S(1)}, f32[12,128]{1,0:T(8,128)S(1)}, u32[]{:S(2)}, u32[]{:S(2)}) collective-permute-start(f32[12,128]{1,0:T(8,128)S(1)} %get-tuple-element.73), channel_id=1, source_target_pairs={{0,224},{32,64},{64,32},{96,128},{128,96},{160,192},{192,160},{224... | collective-permute-start | bytes 18440 | tf_op jit(solution)/shard_map/ppermute | solution.py:669
  50.4 2.8 %collective-permute-start.14 = (f32[12,128]{1,0:T(8,128)S(1)}, f32[12,128]{1,0:T(8,128)S(1)}, u32[]{:S(2)}, u32[]{:S(2)}) collective-permute-start(f32[12,128]{1,0:T(8,128)S(1)} %get-tuple-element.74), channel_id=1, source_target_pairs={{0,1},{1,0},{2,3},{3,2},{4,5},{5,4},{6,7},{7,6},{8,9},{9,8},{10,11... | collective-permute-start | bytes 18440 | tf_op jit(solution)/shard_map/ppermute | solution.py:669
  50.4 2.8 %collective-permute-start.15 = (f32[12,128]{1,0:T(8,128)S(1)}, f32[12,128]{1,0:T(8,128)S(1)}, u32[]{:S(2)}, u32[]{:S(2)}) collective-permute-start(f32[12,128]{1,0:T(8,128)S(1)} %get-tuple-element.75), channel_id=1, source_target_pairs={{0,32},{32,0},{64,96},{96,64},{128,160},{160,128},{192,224},{224,1... | collective-permute-start | bytes 18440 | tf_op jit(solution)/shard_map/ppermute | solution.py:669
  54.4 5.9 %collective-permute-start.16 = (f32[12,128]{1,0:T(8,128)S(1)}, f32[12,128]{1,0:T(8,128)S(1)}, u32[]{:S(2)}, u32[]{:S(2)}) collective-permute-start(f32[12,128]{1,0:T(8,128)S(1)} %get-tuple-element.78), channel_id=1, source_target_pairs={{0,1},{1,2},{2,3},{3,4},{4,5},{5,6},{6,7},{7,8},{8,9},{9,10},{10,1... | collective-permute-start | bytes 18440 | tf_op jit(solution)/shard_map/ppermute | solution.py:675
  55.2 5.1 %collective-permute-start.17 = (f32[12,128]{1,0:T(8,128)S(1)}, f32[12,128]{1,0:T(8,128)S(1)}, u32[]{:S(2)}, u32[]{:S(2)}) collective-permute-start(f32[12,128]{1,0:T(8,128)S(1)} %get-tuple-element.79), channel_id=1, source_target_pairs={{0,32},{32,64},{64,96},{96,128},{128,160},{160,192},{192,224},{224... | collective-permute-start | bytes 18440 | tf_op jit(solution)/shard_map/ppermute | solution.py:675
  61.1 21.2 %all-to-all-start = ((f32[256,1,128]{2,1,0:T(1,128)}), f32[256,1,128]{2,1,0:T(1,128)S(1)}, u32[]{:S(2)}, u32[]{:S(2)}) async-start(f32[256,1,128]{2,1,0:T(1,128)} %bitcast.2), calls=%async_computation | async-start | bytes 262144 | tf_op jit(solution)/shard_map/all_to_all | solution.py:776

commit v4 on v3

--- a/solution.py
+++ b/solution.py
@@ -14,6 +14,7 @@
 ITEM_ROWS = 64
 SIDES = 4
 PARTS = 2
+BESIDE = 1_000_000_000
 LIMIT = 54000
 AXES = ("band", "sector")
 epsilon = 1e-06
@@ -149,9 +150,7 @@
     return (found[0:rows] * 128.0 + found[rows : 2 * rows]).astype(I32)
 
 
-def make_plan(
-    conn_ref, send_ref, conn_out, key_out, scan_out, end_out, own_out, pair_out, inverse_out, send_out, keys_ref
-):
+def relabel(conn_ref, send_ref, conn_out, own_out, pair_out, inverse_out, send_out):
     for half in range(8):
         start = (half % 2) * LANES
         send_out[half : half + 1, :] = send_ref[0, 0, half // 2 : half // 2 + 1, start : start + LANES]
@@ -172,6 +171,11 @@
         [conn_out[8 * chunk + k : 8 * chunk + k + 1, :] for chunk in range(CHUNKS) for k in (1, 2)], axis=1
     )
     pair_out[...] = inverse_of(pair_line, lax.broadcasted_iota(I32, (1, 16 * LANES), 1), NODE_ROWS)
+    return keys
+
+
+def make_order(keys, key_out, scan_out, end_out, keys_ref):
+    sub, lane = tile_iota(0), tile_iota(1)
     keys = sort_items(keys)
     for register in range(8):
         keys_ref[8 * register : 8 * register + 8, :] = keys[register]
@@ -435,8 +439,8 @@
         copy.start()
     copies[0].wait()
     copies[1].wait()
+    first_keys = relabel(ids_ref, send_ref, conn_out, *plan[3:], inverse_out, send_out)
     copies[2].wait()
-    make_plan(ids_ref, send_ref, conn_out, *plan, inverse_out, send_out, keys)
     below, above = [live.astype(F32) for live in live_sides()]
     for chunk in range(CHUNKS):
         at = slice(chunk * LANES, (chunk + 1) * LANES)
@@ -446,6 +450,7 @@
     row_out[...] = 1.0 / jnp.sqrt(peaks[...])
     column_maxima(blocks_ref, None, term, 0)
     column_maxima(blocks_ref, row_out, term, 3)
+    make_order(first_keys, *plan[:3], keys)
     scatter_maxima(term, 6, plan, items, part_out)
     pack(part_out, 6, packets)
 
@@ -456,7 +461,7 @@
     plan, rest = rest[:5], rest[5:]
     arrived, rest = by_side(rest[:4]), rest[4:]
     row_out, scale_out, part_out, loads_out, rest = rest[0], rest[1], rest[2], rest[3], rest[4:]
-    packets, (term, items, peaks, merged, second_row) = rest[:4], rest[4:]
+    packets, (term, items, peaks, merged) = rest[:4], rest[4:]
     unpack(part_ref, 6, arrived, jnp.maximum, merged)
     row = lax.broadcasted_iota(I32, (NODE_ROWS, LANES), 0)
     below, above = [live.astype(F32) for live in live_sides()]
@@ -466,16 +471,12 @@
         later = NODE_ROWS * (c + 3)
         second = rescale(first, merged[later : later + NODE_ROWS, :])
         merged[NODE_ROWS * c : NODE_ROWS * (c + 1), :] = first
-        merged[later : later + NODE_ROWS, :] = second
         scale_out[NODE_ROWS * c : NODE_ROWS * (c + 1), :] = second
     for chunk in range(CHUNKS):
         at = slice(chunk * LANES, (chunk + 1) * LANES)
-        scales = node_picks(merged, 6, conn_ref, chunk)
-        row_maxima(blocks_ref, [scales[0:3], scales[3:6]], at, peaks)
-    first_row = row_ref[...]
-    second_row[...] = first_row / jnp.sqrt(first_row * peaks[0:STRAINS, :])
-    row_out[...] = second_row[...] / jnp.sqrt(second_row[...] * peaks[STRAINS : 2 * STRAINS, :])
-    column_maxima(blocks_ref, second_row, term, 0)
+        row_maxima(blocks_ref, [node_picks(merged, 3, conn_ref, chunk)], at, peaks)
+    row_out[...] = row_ref[...] / jnp.sqrt(row_ref[...] * peaks[...])
+    column_maxima(blocks_ref, row_out, term, 0)
     scatter_maxima(term, 3, plan, items, part_out)
     pack(part_out, 3, packets)
     tables = [rows_of(loads_ref, 8 * c) for c in range(3)]
@@ -493,18 +494,17 @@
             )
 
 
-def target_kernel(
-    blocks_ref,
-    conn_ref,
-    row_ref,
-    scale_ref,
-    part_ref,
-    loads_ref,
-    *rest,
-):
+def row_kernel(blocks_ref, conn_ref, row_ref, scale_ref, row_out, peaks):
+    for chunk in range(CHUNKS):
+        at = slice(chunk * LANES, (chunk + 1) * LANES)
+        row_maxima(blocks_ref, [node_picks(scale_ref, 3, conn_ref, chunk)], at, peaks)
+    row_out[...] = row_ref[...] / jnp.sqrt(row_ref[...] * peaks[...])
+
+
+def target_kernel(blocks_ref, conn_ref, row_ref, scale_ref, part_ref, loads_ref, *rest):
     arrived, rest = by_side(rest[:4]), rest[4:]
-    scale_out, strain_out, part_out, rest = rest[0], rest[1], rest[2], rest[3:]
-    packets, (term, table, strain, cones) = rest[:4], rest[4:]
+    scale_out, image_out, part_out, rest = rest[0], rest[1], rest[2], rest[3:]
+    packets, (term, table, strain) = rest[:4], rest[4:]
     unpack(part_ref, 3, arrived, jnp.maximum, table)
     scale = rescale(scale_ref[...], table[...])
     scale_out[...] = scale
@@ -516,39 +516,45 @@
     table[...] = scale * (scale * table[...])
     apply_blocks(blocks_ref, table, 1, conn_ref, strain)
     row = row_ref[...]
-    image = row * strain[0:STRAINS, :]
-    cones[...] = image
-    project_rows(cones)
-    strain[0:STRAINS, :] = row * image
-    strain[STRAINS : 2 * STRAINS, :] = row * cones[...]
-    strain_out[...] = 3.0 * image + 2.0 * cones[...]
-    apply_transpose(blocks_ref, strain, 2, term)
-    scatter_sums(term, 6, conn_ref, part_out)
-    part_out[0:48, :] = part_out[0:48, :] * scale
-    part_out[48:96, :] = part_out[48:96, :] * scale
-    pack(part_out, 6, packets)
-
-
-def second_kernel(
-    blocks_ref, conn_ref, row_ref, scale_ref, part_ref, *rest
-):
-    arrived, rest = rest[:4], rest[4:]
-    joint_out, strain_out, part_out, rest = rest[0], rest[1], rest[2], rest[3:]
-    packets, (term, table, strain) = rest[:4], rest[4:]
-    arrived = by_side(arrived)
-    unpack(part_ref, 6, arrived, jnp.add, table)
-    joint_out[...] = table[48:96, :]
-    scale = scale_ref[...]
-    table[0:48, :] = scale * table[0:48, :]
-    table[48:96, :] = scale * table[48:96, :]
-    apply_blocks(blocks_ref, table, 2, conn_ref, strain)
-    row = row_ref[...]
-    strain_out[...] = row * strain[STRAINS : 2 * STRAINS, :]
-    strain[0:STRAINS, :] = row * (row * strain[0:STRAINS, :])
+    image = row * strain[...]
+    image_out[...] = image
+    strain[...] = row * image
     apply_transpose(blocks_ref, strain, 1, term)
     scatter_sums(term, 3, conn_ref, part_out)
     part_out[...] = part_out[...] * scale
     pack(part_out, 3, packets)
+
+
+def cone_kernel(blocks_ref, conn_ref, row_ref, scale_ref, image_ref, base_out, part_out, term, strain):
+    strain[...] = image_ref[...]
+    project_rows(strain)
+    base_out[...] = 3.0 * image_ref[...] + 2.0 * strain[...]
+    strain[...] = row_ref[...] * strain[...]
+    apply_transpose(blocks_ref, strain, 1, term)
+    scatter_sums(term, 3, conn_ref, part_out)
+    part_out[...] = part_out[...] * scale_ref[...]
+
+
+def second_kernel(blocks_ref, conn_ref, row_ref, scale_ref, part_ref, joint_ref, *rest):
+    arrived, rest = by_side(rest[:4]), rest[4:]
+    part_out, packets, (term, table, strain) = rest[0], rest[1:5], rest[5:]
+    unpack(part_ref, 3, arrived, jnp.add, table)
+    scale = scale_ref[...]
+    table[...] = scale * table[...]
+    apply_blocks(blocks_ref, table, 1, conn_ref, strain)
+    row = row_ref[...]
+    strain[...] = row * (row * strain[...])
+    apply_transpose(blocks_ref, strain, 1, term)
+    scatter_sums(term, 3, conn_ref, part_out)
+    part_out[0:48, :] = part_out[0:48, :] * scale
+    part_out[48:96, :] = joint_ref[...]
+    pack(part_out, 6, packets)
+
+
+def joint_kernel(blocks_ref, conn_ref, row_ref, scale_ref, joint_ref, line_ref, image_out, table, strain):
+    table[...] = scale_ref[...] * joint_ref[...]
+    apply_blocks(blocks_ref, table, 1, conn_ref, strain)
+    image_out[...] = row_ref[...] * strain[...]
 
 
 def own_square(ref):
@@ -562,12 +568,13 @@
 def third_kernel(
     blocks_ref, conn_ref, row_ref, scale_ref, part_ref, *rest
 ):
-    arrived, rest = rest[:4], rest[4:]
-    norm_out, part_out, right_out, above_out, term, table, strain = rest
-    unpack(part_ref, 3, by_side(arrived), jnp.add, table)
+    arrived, rest = by_side(rest[:4]), rest[4:]
+    norm_out, joint_out, part_out, right_out, above_out, term, table, strain = rest
+    unpack(part_ref, 6, arrived, jnp.add, table)
     norm_out[...] = own_square(table)
+    joint_out[...] = table[48:96, :]
     scale = scale_ref[...]
-    table[...] = scale * table[...]
+    table[0:48, :] = scale * table[0:48, :]
     apply_blocks(blocks_ref, table, 1, conn_ref, strain)
     row = row_ref[...]
     strain[...] = row * (row * strain[...])
@@ -580,7 +587,7 @@
             packet[4 * channel + 2 : 4 * channel + 4, :] = side_rows(part_out, side + 4, channel)
 
 
-def norm_kernel(part_ref, norm_ref, left_ref, below_ref, sums_out):
+def norm_kernel(part_ref, norm_ref, left_ref, below_ref, sums_out, line_out):
     below, above = live_sides()
     squares = jnp.zeros((2, LANES), F32)
     for channel in range(3):
@@ -597,9 +604,10 @@
     lane = lax.broadcasted_iota(I32, (1, LANES), 1)
     line = jnp.where(lane < 64, first + pltpu.roll(first, 64, 1), last + pltpu.roll(last, 64, 1))
     sums_out[...] = jnp.broadcast_to(line, sums_out.shape)
-
-
-def lines_kernel(scale_ref, loads_ref, joint_ref, inverse_ref, velocity_out, lines):
+    line_out[...] = line
+
+
+def lines_kernel(scale_ref, loads_ref, joint_ref, inverse_ref, line_ref, velocity_out, lines):
     for c in range(3):
         base = NODE_ROWS * c
         scale = scale_ref[base : base + 8, :]
@@ -709,7 +717,7 @@
     row, scale, part, loads, *packets = call(
         sweep_kernel,
         [rows, nodes, nodes, ((24, LANES), F32)] + [((18, LANES), F32)] * 4,
-        [items, ((3 * SORTED_ROWS, LANES), F32), ((2 * STRAINS, 1024), F32), ((96, LANES), F32), rows],
+        [items, ((3 * SORTED_ROWS, LANES), F32), rows, ((96, LANES), F32)],
         blocks,
         conn,
         row,
@@ -719,10 +727,11 @@
         *plan,
         *exchange(packets),
     )
-    scale, base, part, *packets = call(
+    (row,) = call(row_kernel, [rows], [rows], blocks, conn, row, scale, work=BESIDE)
+    scale, image, part, *packets = call(
         target_kernel,
-        [nodes, rows, ((96, LANES), F32)] + [((24, LANES), F32)] * 4,
-        [twice, nodes, ((2 * STRAINS, 1024), F32), rows],
+        [nodes, rows, nodes] + packet,
+        [items, nodes, rows],
         blocks,
         conn,
         row,
@@ -731,10 +740,25 @@
         loads,
         *exchange(packets),
     )
-    joint, image, part, *packets = call(
+    base, joint = call(
+        cone_kernel, [rows, nodes], [items, rows], blocks, conn, row, scale, image, work=BESIDE
+    )
+    part, *packets = call(
         second_kernel,
-        [nodes, rows, nodes] + packet,
-        [items, ((96, LANES), F32), ((2 * STRAINS, 1024), F32)],
+        [((96, LANES), F32)] + [((24, LANES), F32)] * 4,
+        [items, nodes, rows],
+        blocks,
+        conn,
+        row,
+        scale,
+        part,
+        joint,
+        *exchange(packets),
+    )
+    norm, joint, part, right, above = call(
+        third_kernel,
+        [((1, LANES), F32), nodes, nodes] + packet[:2],
+        [items, ((96, LANES), F32), rows],
         blocks,
         conn,
         row,
@@ -742,26 +766,18 @@
         part,
         *exchange(packets),
     )
-    norm, part, right, above = call(
-        third_kernel,
-        [((1, LANES), F32), nodes] + packet[:2],
-        [items, nodes, rows],
-        blocks,
-        conn,
-        row,
-        scale,
-        part,
-        *exchange(packets),
-    )
     count = lax.axis_size("band") * lax.axis_size("sector")
-    (sums,) = call(
+    sums, line = call(
         norm_kernel,
-        [((count, LANES), F32)],
+        [((count, LANES), F32), ((1, LANES), F32)],
         [],
         part,
         norm,
         shift_up(right, "sector"),
         shift_up(above, "band"),
+    )
+    (image,) = call(
+        joint_kernel, [rows], [nodes, rows], blocks, conn, row, scale, joint, line, work=BESIDE
     )
     (lines,) = call(
         lines_kernel,
@@ -771,7 +787,8 @@
         loads,
         joint,
         inverse,
-        work=600_000_000,
+        line,
+        work=BESIDE,
     )
     sums = lax.all_to_all(sums, AXES, 0, 0, tiled=True)
     velocities, multipliers = call(

time: 83.5 us -> 81.2 us (0.972)
  waiting for transfers between devices: 26.7 us -> 24.7 us
    ppermute x16, waiting for transfers between devices: 9.91 us -> 8.51 us  [exchange(): lax.ppermute(packet, axis, swap_pairs(axis, odd))]
    pallas_call x8 -> x11, Pallas kernels: 18.6 us -> 18.2 us  [call(): pl.pallas_call(body, out_shape=[jax.ShapeDtypeStruct(shape, kind) for sha...]
  transfers between devices with their start and end apart: 19 -> 19, of which waited for: 9 -> 9; matrix products, arithmetic and copies ran while one was open for 0% -> 0% of each run, Pallas kernels for 0% -> 3%
where the time goes in v4:
time: 81.2 us; the launch traced here: 81 us
  starting transfers between devices  35 us (43%)
  waiting for transfers between devices  24.7 us (30%)
  Pallas kernels  18.2 us (22%)
  between operations  1.56 us (2%)
  local copies, waits for them, and re-layouts  1.54 us (2%)
    ppermute x16, starting transfers between devices, exchange(): lax.ppermute(packet, axis, swap_pairs(axis, odd))  25.4 us
    pallas_call x11, Pallas kernels, call(): pl.pallas_call(body, out_shape=[jax.ShapeDtypeStruct(shape, kind) for sha...  18.2 us
    all_to_all x1, waiting for transfers between devices, per_device(): sums = lax.all_to_all(sums, AXES, 0, 0, tiled=True)  11.8 us
    ppermute x16, waiting for transfers between devices, exchange(): lax.ppermute(packet, axis, swap_pairs(axis, odd))  8.51 us
    all_to_all x1, starting transfers between devices, per_device(): sums = lax.all_to_all(sums, AXES, 0, 0, tiled=True)  8.03 us
    ppermute x2, waiting for transfers between devices, shift_up(): lax.ppermute(packet, axis, [(i, (i + 1) % count) for i in range(count)])  4.4 us
  transfers between devices with their start and end apart: 19, of which 9 were waited for; matrix products, arithmetic and copies ran while one was open for 0% of the time, Pallas kernels for 3%

profile of v4, /device:TPU:1, one launch (start us, length us, event | category | flops | bytes accessed | tf_op | source)
XLA Modules:
  0.0 81.0 jit_solution(13944105878732993982)
XLA Ops:
  0.7 0.8 %copy-done.2 = s32[1,1,8,1024]{3,2,1,0:T(8,128)S(1)} copy-done((s32[1,1,8,1024]{3,2,1,0:T(8,128)S(1)}, s32[1,1,8,1024]{3,2,1,0:T(8,128)}, u32[]{:S(2)}) %copy-start.2) | copy-done | bytes 32792
  1.5 0.7 copy-done.3
  2.2 7.3 %shard_map.68 = (s32[64,128]{1,0:T(8,128)S(1)}, s32[40,128]{1,0:T(8,128)S(1)}, s32[8,128]{1,0:T(8,128)S(1)}, s32[16,128]{1,0:T(8,128)S(1)}, s32[8,128]{1,0:T(8,1...) custom-call(f32[1,1,12,24,1024]{4,3,2,1,0:T(8,128)} %blocks_ref.13, ...), custom_call_target="tpu_custom_call" | custom-call | flops 12000000000 | bytes 46875000 | tf_op jit(solution)/shard_map/pallas_call | solution.py:654
  9.5 8.7 %collective-permute-start = (f32[24,128]{1,0:T(8,128)S(1)}, f32[24,128]{1,0:T(8,128)S(1)}, u32[]{:S(2)}, u32[]{:S(2)}) collective-permute-start(f32[24,128]{1,0:T(8,128)S(1)} %get-tuple-element.56), channel_id=1, source_target_pairs={{0,31},{1,2},{2,1},{3,4},{4,3},{5,6},{6,5},{7,8},{8,7},{9,10},{10,... | collective-permute-start | bytes 36872 | tf_op jit(solution)/shard_map/ppermute | solution.py:677
  18.2 2.1 %collective-permute-start.1 = (f32[24,128]{1,0:T(8,128)S(1)}, f32[24,128]{1,0:T(8,128)S(1)}, u32[]{:S(2)}, u32[]{:S(2)}) collective-permute-start(f32[24,128]{1,0:T(8,128)S(1)} %get-tuple-element.57), channel_id=1, source_target_pairs={{0,224},{32,64},{64,32},{96,128},{128,96},{160,192},{192,160},{224... | collective-permute-start | bytes 36872 | tf_op jit(solution)/shard_map/ppermute | solution.py:677
  20.3 0.0 collective-permute-start.2
  20.3 1.0 %collective-permute-start.3 = (f32[24,128]{1,0:T(8,128)S(1)}, f32[24,128]{1,0:T(8,128)S(1)}, u32[]{:S(2)}, u32[]{:S(2)}) collective-permute-start(f32[24,128]{1,0:T(8,128)S(1)} %get-tuple-element.59), channel_id=1, source_target_pairs={{0,32},{32,0},{64,96},{96,64},{128,160},{160,128},{192,224},{224,1... | collective-permute-start | bytes 36872 | tf_op jit(solution)/shard_map/ppermute | solution.py:677
  21.3 0.0 collective-permute-done.rest_5_
  21.3 0.4 collective-permute-done.1.rest_6_
  21.7 1.4 %collective-permute-done.2.rest_7_ = f32[24,128]{1,0:T(8,128)S(1)} collective-permute-done((f32[24,128]{1,0:T(8,128)S(1)}, f32[24,128]{1,0:T(8,128)S(1)}, u32[]{:S(2)}, u32[]{:S(2)}) %collective-permute-start.2) | collective-permute-done | bytes 12320 | tf_op jit(solution)/shard_map/ppermute | solution.py:677
  23.1 0.0 collective-permute-done.3.rest_8_
  23.1 3.8 %shard_map.69 = (f32[12,1024]{1,0:T(8,128)S(1)}, f32[48,128]{1,0:T(8,128)S(1)}, f32[48,128]{1,0:T(8,128)S(1)}, f32[24,128]{1,0:T(8,128)S(1)}, f32[18,128]{1,0:T(...) custom-call(f32[1,1,12,24,1024]{4,3,2,1,0:T(8,128)S(1)} %copy-done, ...), custom_call_target="tpu_custom_call" | custom-call | tf_op jit(solution)/shard_map/pallas_call | solution.py:654
  26.9 1.1 %collective-permute-start.4 = (f32[18,128]{1,0:T(8,128)S(1)}, f32[18,128]{1,0:T(8,128)S(1)}, u32[]{:S(2)}, u32[]{:S(2)}) collective-permute-start(f32[18,128]{1,0:T(8,128)S(1)} %get-tuple-element.64), channel_id=1, source_target_pairs={{0,31},{1,2},{2,1},{3,4},{4,3},{5,6},{6,5},{7,8},{8,7},{9,10},{10,... | collective-permute-start | bytes 27656 | tf_op jit(solution)/shard_map/ppermute | solution.py:677
  27.9 3.3 %collective-permute-start.5 = (f32[18,128]{1,0:T(8,128)S(1)}, f32[18,128]{1,0:T(8,128)S(1)}, u32[]{:S(2)}, u32[]{:S(2)}) collective-permute-start(f32[18,128]{1,0:T(8,128)S(1)} %get-tuple-element.65), channel_id=1, source_target_pairs={{0,224},{32,64},{64,32},{96,128},{128,96},{160,192},{192,160},{224... | collective-permute-start | bytes 27656 | tf_op jit(solution)/shard_map/ppermute | solution.py:677
  31.2 0.0 collective-permute-start.6
  31.2 0.0 collective-permute-start.7
  31.2 0.6 shard_map.70.row_ref
  31.8 1.0 %collective-permute-done.4.rest_0_ = f32[18,128]{1,0:T(8,128)S(1)} collective-permute-done((f32[18,128]{1,0:T(8,128)S(1)}, f32[18,128]{1,0:T(8,128)S(1)}, u32[]{:S(2)}, u32[]{:S(2)}) %collective-permute-start.4) | collective-permute-done | bytes 9248 | tf_op jit(solution)/shard_map/ppermute | solution.py:677
  32.8 0.0 collective-permute-done.5.rest_1_
  32.8 1.3 %collective-permute-done.6.rest_2_ = f32[18,128]{1,0:T(8,128)S(1)} collective-permute-done((f32[18,128]{1,0:T(8,128)S(1)}, f32[18,128]{1,0:T(8,128)S(1)}, u32[]{:S(2)}, u32[]{:S(2)}) %collective-permute-start.6) | collective-permute-done | bytes 9248 | tf_op jit(solution)/shard_map/ppermute | solution.py:677
  34.1 1.2 %shard_map.71 = (f32[48,128]{1,0:T(8,128)S(1)}, f32[12,1024]{1,0:T(8,128)S(1)}, f32[48,128]{1,0:T(8,128)S(1)}, f32[12,128]{1,0:T(8,128)S(1)}, f32[12,128]{1,0:T(...) custom-call(f32[1,1,12,24,1024]{4,3,2,1,0:T(8,128)S(1)} %copy-done, s32[64,128]{1,0:T(8,128)S(1)} %get-tuple-element.47.conn_ref, ...), custom_call_target="tpu_custom_call" | custom-call | tf_op jit(solution)/shard_map/pallas_call | solution.py:654
  35.2 0.2 collective-permute-start.10
  35.4 2.0 %collective-permute-start.11 = (f32[12,128]{1,0:T(8,128)S(1)}, f32[12,128]{1,0:T(8,128)S(1)}, u32[]{:S(2)}, u32[]{:S(2)}) collective-permute-start(f32[12,128]{1,0:T(8,128)S(1)} %get-tuple-element.75), channel_id=1, source_target_pairs={{0,32},{32,0},{64,96},{96,64},{128,160},{160,128},{192,224},{224,1... | collective-permute-start | bytes 18440 | tf_op jit(solution)/shard_map/ppermute | solution.py:677
  37.4 2.4 %collective-permute-start.8 = (f32[12,128]{1,0:T(8,128)S(1)}, f32[12,128]{1,0:T(8,128)S(1)}, u32[]{:S(2)}, u32[]{:S(2)}) collective-permute-start(f32[12,128]{1,0:T(8,128)S(1)} %get-tuple-element.72), channel_id=1, source_target_pairs={{0,31},{1,2},{2,1},{3,4},{4,3},{5,6},{6,5},{7,8},{8,7},{9,10},{10,... | collective-permute-start | bytes 18440 | tf_op jit(solution)/shard_map/ppermute | solution.py:677
  39.8 0.1 collective-permute-start.9
  39.9 0.8 shard_map.72
  40.7 0.0 collective-permute-done.10.rest_2_
  40.7 0.0 collective-permute-done.11.rest_3_
  40.7 2.6 %collective-permute-done.8.rest_0_ = f32[12,128]{1,0:T(8,128)S(1)} collective-permute-done((f32[12,128]{1,0:T(8,128)S(1)}, f32[12,128]{1,0:T(8,128)S(1)}, u32[]{:S(2)}, u32[]{:S(2)}) %collective-permute-start.8) | collective-permute-done | bytes 6176 | tf_op jit(solution)/shard_map/ppermute | solution.py:677
  43.3 1.1 %shard_map.73 = (f32[96,128]{1,0:T(8,128)S(1)}, f32[24,128]{1,0:T(8,128)S(1)}, f32[24,128]{1,0:T(8,128)S(1)}, f32[24,128]{1,0:T(8,128)S(1)}, f32[24,128]{1,0:T(8,128)S(1)}) custom-call(f32[1,1,12,24,1024]{4,3,2,1,0:T(8,128)S(1)} %copy-done, s32[64,128]{1,0:T(8,128)S(1)} %get-tuple-element.47.conn_ref, f32[12,1024]{1,0:T(8,128)S(1)} %shard_map.70.row_ref, ...), custom_call_target="tpu_custom_call" | custom-call | tf_op jit(solution)/shard_map/pallas_call | solution.py:654
  44.4 2.5 %collective-permute-start.12 = (f32[24,128]{1,0:T(8,128)S(1)}, f32[24,128]{1,0:T(8,128)S(1)}, u32[]{:S(2)}, u32[]{:S(2)}) collective-permute-start(f32[24,128]{1,0:T(8,128)S(1)} %get-tuple-element.77), channel_id=1, source_target_pairs={{0,31},{1,2},{2,1},{3,4},{4,3},{5,6},{6,5},{7,8},{8,7},{9,10},{10,... | collective-permute-start | bytes 36872 | tf_op jit(solution)/shard_map/ppermute | solution.py:677
  46.9 1.2 %collective-permute-start.13 = (f32[24,128]{1,0:T(8,128)S(1)}, f32[24,128]{1,0:T(8,128)S(1)}, u32[]{:S(2)}, u32[]{:S(2)}) collective-permute-start(f32[24,128]{1,0:T(8,128)S(1)} %get-tuple-element.78), channel_id=1, source_target_pairs={{0,224},{32,64},{64,32},{96,128},{128,96},{160,192},{192,160},{224... | collective-permute-start | bytes 36872 | tf_op jit(solution)/shard_map/ppermute | solution.py:677
  48.1 0.9 %collective-permute-start.15 = (f32[24,128]{1,0:T(8,128)S(1)}, f32[24,128]{1,0:T(8,128)S(1)}, u32[]{:S(2)}, u32[]{:S(2)}) collective-permute-start(f32[24,128]{1,0:T(8,128)S(1)} %get-tuple-element.80), channel_id=1, source_target_pairs={{0,32},{32,0},{64,96},{96,64},{128,160},{160,128},{192,224},{224,1... | collective-permute-start | bytes 36872 | tf_op jit(solution)/shard_map/ppermute | solution.py:677
  49.0 1.4 %collective-permute-done.12.rest_0_ = f32[24,128]{1,0:T(8,128)S(1)} collective-permute-done((f32[24,128]{1,0:T(8,128)S(1)}, f32[24,128]{1,0:T(8,128)S(1)}, u32[]{:S(2)}, u32[]{:S(2)}) %collective-permute-start.12) | collective-permute-done | bytes 12320 | tf_op jit(solution)/shard_map/ppermute | solution.py:677
  50.4 0.0 collective-permute-done.13.rest_1_
  50.4 0.5 collective-permute-done.14.rest_2_
  50.9 0.0 collective-permute-done.15.rest_3_
  50.9 1.1 %shard_map.74 = (f32[1,128]{1,0:T(1,128)S(1)}, f32[48,128]{1,0:T(8,128)S(1)}, f32[48,128]{1,0:T(8,128)S(1)}, f32[12,128]{1,0:T(8,128)S(1)}, f32[12,128]{1,0:T(8,128)S(1)}) custom-call(f32[1,1,12,24,1024]{4,3,2,1,0:T(8,128)S(1)} %copy-done, s32[64,128]{1,0:T(8,128)S(1)} %get-tuple-element.47.conn_ref, f32[12,1024]{1,0:T(8,128)S(1)} %shard_map.70.row_ref, ...), custom_call_target="tpu_custom_call" | custom-call | tf_op jit(solution)/shard_map/pallas_call | solution.py:654
  52.1 0.7 collective-permute-start.16
  52.8 0.8 collective-permute-start.17
  53.6 4.4 %collective-permute-done.16.left_ref = f32[12,128]{1,0:T(8,128)S(1)} collective-permute-done((f32[12,128]{1,0:T(8,128)S(1)}, f32[12,128]{1,0:T(8,128)S(1)}, u32[]{:S(2)}, u32[]{:S(2)}) %collective-permute-start.16) | collective-permute-done | bytes 6176 | tf_op jit(solution)/shard_map/ppermute | solution.py:683
  58.0 0.0 collective-permute-done.17.below_ref
  58.0 0.8 shard_map.75
  58.8 8.0 %all-to-all-start = ((f32[256,1,128]{2,1,0:T(1,128)}), f32[256,1,128]{2,1,0:T(1,128)S(1)}, u32[]{:S(2)}, u32[]{:S(2)}) async-start(f32[256,1,128]{2,1,0:T(1,128)} %bitcast.2), calls=%async_computation | async-start | bytes 262144 | tf_op jit(solution)/shard_map/all_to_all | solution.py:793
  67.4 0.6 shard_map.77.joint_ref
  68.0 0.1 shard_map.76.velocity_ref
  68.1 11.8 %all-to-all-done = f32[256,1,128]{2,1,0:T(1,128)S(1)} async-done(((f32[256,1,128]{2,1,0:T(1,128)}), f32[256,1,128]{2,1,0:T(1,128)S(1)}, u32[]{:S(2)}, u32[]{:S(2)}) %all-to-all-start) | async-done | bytes 131104 | tf_op jit(solution)/shard_map/all_to_all | solution.py:793
  80.0 0.9 %shard_map.78 = (f32[24,128]{1,0:T(8,128)}, f32[96,128]{1,0:T(8,128)}) custom-call(f32[256,128]{1,0:T(8,128)S(1)} %bitcast.7, f32[1]{0:T(128)S(6)} %copy.14.step_ref, f32[48,128]{1,0:T(8,128)S(1)} %shard_map.76.velocity_ref, f32[12,1024]{1,0:T(8,128)S(1)} %get-tuple-element.89.base_ref, f32[12,1024]{1,0:T(8,128)S(1)} %shard_map.77.joint_ref, ...), custom_call_target="tpu_custom_call" | custom-call | tf_op jit(solution)/shard_map/pallas_call | solution.py:654
  (9 shorter events, 0.0 us)
Async XLA Ops:
  0.6 22.4 %copy-start = (f32[1,1,12,24,1024]{4,3,2,1,0:T(8,128)S(1)}, f32[1,1,12,24,1024]{4,3,2,1,0:T(8,128)}, u32[]{:S(2)}) copy-start(f32[1,1,12,24,1024]{4,3,2,1,0:T(8,128)} %blocks_ref.13) | copy-start | bytes 3538948
  0.6 22.4 %copy-start.1 = (f32[1,1,3,1024]{3,1,2,0:T(1,128)S(1)}, f32[1,1,3,1024]{3,1,2,0:T(1,128)}, u32[]{:S(2)}) copy-start(f32[1,1,3,1024]{3,1,2,0:T(1,128)} %param.8) | copy-start | bytes 36868
  0.7 0.9 %copy-start.2 = (s32[1,1,8,1024]{3,2,1,0:T(8,128)S(1)}, s32[1,1,8,1024]{3,2,1,0:T(8,128)}, u32[]{:S(2)}) copy-start(s32[1,1,8,1024]{3,2,1,0:T(8,128)} %ids_at.1) | copy-start | bytes 98308
  1.5 0.7 copy-start.3
  9.5 11.8 %collective-permute-start = (f32[24,128]{1,0:T(8,128)S(1)}, f32[24,128]{1,0:T(8,128)S(1)}, u32[]{:S(2)}, u32[]{:S(2)}) collective-permute-start(f32[24,128]{1,0:T(8,128)S(1)} %get-tuple-element.56), channel_id=1, source_target_pairs={{0,31},{1,2},{2,1},{3,4},{4,3},{5,6},{6,5},{7,8},{8,7},{9,10},{10,... | collective-permute-start | bytes 36872 | tf_op jit(solution)/shard_map/ppermute | solution.py:677
  18.2 3.5 %collective-permute-start.1 = (f32[24,128]{1,0:T(8,128)S(1)}, f32[24,128]{1,0:T(8,128)S(1)}, u32[]{:S(2)}, u32[]{:S(2)}) collective-permute-start(f32[24,128]{1,0:T(8,128)S(1)} %get-tuple-element.57), channel_id=1, source_target_pairs={{0,224},{32,64},{64,32},{96,128},{128,96},{160,192},{192,160},{224... | collective-permute-start | bytes 36872 | tf_op jit(solution)/shard_map/ppermute | solution.py:677
  20.3 2.8 %collective-permute-start.2 = (f32[24,128]{1,0:T(8,128)S(1)}, f32[24,128]{1,0:T(8,128)S(1)}, u32[]{:S(2)}, u32[]{:S(2)}) collective-permute-start(f32[24,128]{1,0:T(8,128)S(1)} %get-tuple-element.58), channel_id=1, source_target_pairs={{0,1},{1,0},{2,3},{3,2},{4,5},{5,4},{6,7},{7,6},{8,9},{9,8},{10,11... | collective-permute-start | bytes 36872 | tf_op jit(solution)/shard_map/ppermute | solution.py:677
  20.3 2.8 %collective-permute-start.3 = (f32[24,128]{1,0:T(8,128)S(1)}, f32[24,128]{1,0:T(8,128)S(1)}, u32[]{:S(2)}, u32[]{:S(2)}) collective-permute-start(f32[24,128]{1,0:T(8,128)S(1)} %get-tuple-element.59), channel_id=1, source_target_pairs={{0,32},{32,0},{64,96},{96,64},{128,160},{160,128},{192,224},{224,1... | collective-permute-start | bytes 36872 | tf_op jit(solution)/shard_map/ppermute | solution.py:677
  26.9 6.0 %collective-permute-start.4 = (f32[18,128]{1,0:T(8,128)S(1)}, f32[18,128]{1,0:T(8,128)S(1)}, u32[]{:S(2)}, u32[]{:S(2)}) collective-permute-start(f32[18,128]{1,0:T(8,128)S(1)} %get-tuple-element.64), channel_id=1, source_target_pairs={{0,31},{1,2},{2,1},{3,4},{4,3},{5,6},{6,5},{7,8},{8,7},{9,10},{10,... | collective-permute-start | bytes 27656 | tf_op jit(solution)/shard_map/ppermute | solution.py:677
  27.9 4.9 %collective-permute-start.5 = (f32[18,128]{1,0:T(8,128)S(1)}, f32[18,128]{1,0:T(8,128)S(1)}, u32[]{:S(2)}, u32[]{:S(2)}) collective-permute-start(f32[18,128]{1,0:T(8,128)S(1)} %get-tuple-element.65), channel_id=1, source_target_pairs={{0,224},{32,64},{64,32},{96,128},{128,96},{160,192},{192,160},{224... | collective-permute-start | bytes 27656 | tf_op jit(solution)/shard_map/ppermute | solution.py:677
  31.2 2.8 %collective-permute-start.6 = (f32[18,128]{1,0:T(8,128)S(1)}, f32[18,128]{1,0:T(8,128)S(1)}, u32[]{:S(2)}, u32[]{:S(2)}) collective-permute-start(f32[18,128]{1,0:T(8,128)S(1)} %get-tuple-element.66), channel_id=1, source_target_pairs={{0,1},{1,0},{2,3},{3,2},{4,5},{5,4},{6,7},{7,6},{8,9},{9,8},{10,11... | collective-permute-start | bytes 27656 | tf_op jit(solution)/shard_map/ppermute | solution.py:677
  31.2 2.8 %collective-permute-start.7 = (f32[18,128]{1,0:T(8,128)S(1)}, f32[18,128]{1,0:T(8,128)S(1)}, u32[]{:S(2)}, u32[]{:S(2)}) collective-permute-start(f32[18,128]{1,0:T(8,128)S(1)} %get-tuple-element.67), channel_id=1, source_target_pairs={{0,32},{32,0},{64,96},{96,64},{128,160},{160,128},{192,224},{224,1... | collective-permute-start | bytes 27656 | tf_op jit(solution)/shard_map/ppermute | solution.py:677
  35.2 5.5 %collective-permute-start.10 = (f32[12,128]{1,0:T(8,128)S(1)}, f32[12,128]{1,0:T(8,128)S(1)}, u32[]{:S(2)}, u32[]{:S(2)}) collective-permute-start(f32[12,128]{1,0:T(8,128)S(1)} %get-tuple-element.74), channel_id=1, source_target_pairs={{0,1},{1,0},{2,3},{3,2},{4,5},{5,4},{6,7},{7,6},{8,9},{9,8},{10,11... | collective-permute-start | bytes 18440 | tf_op jit(solution)/shard_map/ppermute | solution.py:677
  35.4 5.3 %collective-permute-start.11 = (f32[12,128]{1,0:T(8,128)S(1)}, f32[12,128]{1,0:T(8,128)S(1)}, u32[]{:S(2)}, u32[]{:S(2)}) collective-permute-start(f32[12,128]{1,0:T(8,128)S(1)} %get-tuple-element.75), channel_id=1, source_target_pairs={{0,32},{32,0},{64,96},{96,64},{128,160},{160,128},{192,224},{224,1... | collective-permute-start | bytes 18440 | tf_op jit(solution)/shard_map/ppermute | solution.py:677
  37.4 5.8 %collective-permute-start.8 = (f32[12,128]{1,0:T(8,128)S(1)}, f32[12,128]{1,0:T(8,128)S(1)}, u32[]{:S(2)}, u32[]{:S(2)}) collective-permute-start(f32[12,128]{1,0:T(8,128)S(1)} %get-tuple-element.72), channel_id=1, source_target_pairs={{0,31},{1,2},{2,1},{3,4},{4,3},{5,6},{6,5},{7,8},{8,7},{9,10},{10,... | collective-permute-start | bytes 18440 | tf_op jit(solution)/shard_map/ppermute | solution.py:677
  39.8 3.5 %collective-permute-start.9 = (f32[12,128]{1,0:T(8,128)S(1)}, f32[12,128]{1,0:T(8,128)S(1)}, u32[]{:S(2)}, u32[]{:S(2)}) collective-permute-start(f32[12,128]{1,0:T(8,128)S(1)} %get-tuple-element.73), channel_id=1, source_target_pairs={{0,224},{32,64},{64,32},{96,128},{128,96},{160,192},{192,160},{224... | collective-permute-start | bytes 18440 | tf_op jit(solution)/shard_map/ppermute | solution.py:677
  44.4 6.0 %collective-permute-start.12 = (f32[24,128]{1,0:T(8,128)S(1)}, f32[24,128]{1,0:T(8,128)S(1)}, u32[]{:S(2)}, u32[]{:S(2)}) collective-permute-start(f32[24,128]{1,0:T(8,128)S(1)} %get-tuple-element.77), channel_id=1, source_target_pairs={{0,31},{1,2},{2,1},{3,4},{4,3},{5,6},{6,5},{7,8},{8,7},{9,10},{10,... | collective-permute-start | bytes 36872 | tf_op jit(solution)/shard_map/ppermute | solution.py:677
  46.9 3.5 %collective-permute-start.13 = (f32[24,128]{1,0:T(8,128)S(1)}, f32[24,128]{1,0:T(8,128)S(1)}, u32[]{:S(2)}, u32[]{:S(2)}) collective-permute-start(f32[24,128]{1,0:T(8,128)S(1)} %get-tuple-element.78), channel_id=1, source_target_pairs={{0,224},{32,64},{64,32},{96,128},{128,96},{160,192},{192,160},{224... | collective-permute-start | bytes 36872 | tf_op jit(solution)/shard_map/ppermute | solution.py:677
  48.1 2.8 %collective-permute-start.14 = (f32[24,128]{1,0:T(8,128)S(1)}, f32[24,128]{1,0:T(8,128)S(1)}, u32[]{:S(2)}, u32[]{:S(2)}) collective-permute-start(f32[24,128]{1,0:T(8,128)S(1)} %get-tuple-element.79), channel_id=1, source_target_pairs={{0,1},{1,0},{2,3},{3,2},{4,5},{5,4},{6,7},{7,6},{8,9},{9,8},{10,11... | collective-permute-start | bytes 36872 | tf_op jit(solution)/shard_map/ppermute | solution.py:677
  48.1 2.8 %collective-permute-start.15 = (f32[24,128]{1,0:T(8,128)S(1)}, f32[24,128]{1,0:T(8,128)S(1)}, u32[]{:S(2)}, u32[]{:S(2)}) collective-permute-start(f32[24,128]{1,0:T(8,128)S(1)} %get-tuple-element.80), channel_id=1, source_target_pairs={{0,32},{32,0},{64,96},{96,64},{128,160},{160,128},{192,224},{224,1... | collective-permute-start | bytes 36872 | tf_op jit(solution)/shard_map/ppermute | solution.py:677
  52.1 5.9 %collective-permute-start.16 = (f32[12,128]{1,0:T(8,128)S(1)}, f32[12,128]{1,0:T(8,128)S(1)}, u32[]{:S(2)}, u32[]{:S(2)}) collective-permute-start(f32[12,128]{1,0:T(8,128)S(1)} %get-tuple-element.83), channel_id=1, source_target_pairs={{0,1},{1,2},{2,3},{3,4},{4,5},{5,6},{6,7},{7,8},{8,9},{9,10},{10,1... | collective-permute-start | bytes 18440 | tf_op jit(solution)/shard_map/ppermute | solution.py:683
  52.8 5.2 %collective-permute-start.17 = (f32[12,128]{1,0:T(8,128)S(1)}, f32[12,128]{1,0:T(8,128)S(1)}, u32[]{:S(2)}, u32[]{:S(2)}) collective-permute-start(f32[12,128]{1,0:T(8,128)S(1)} %get-tuple-element.84), channel_id=1, source_target_pairs={{0,32},{32,64},{64,96},{96,128},{128,160},{160,192},{192,224},{224... | collective-permute-start | bytes 18440 | tf_op jit(solution)/shard_map/ppermute | solution.py:683
  58.8 21.2 %all-to-all-start = ((f32[256,1,128]{2,1,0:T(1,128)}), f32[256,1,128]{2,1,0:T(1,128)S(1)}, u32[]{:S(2)}, u32[]{:S(2)}) async-start(f32[256,1,128]{2,1,0:T(1,128)} %bitcast.2), calls=%async_computation | async-start | bytes 262144 | tf_op jit(solution)/shard_map/all_to_all | solution.py:793

commit v5 on v4

--- a/solution.py
+++ b/solution.py
@@ -74,14 +74,14 @@
 
 SCAN_STEPS = tuple(1 << step for step in range(10))
 RUNS = 5
+SORT_FIRST = 64
 SORTED_ROWS = 8 * RUNS
 LOOSE_ROWS = tuple(row for row in range(ITEM_ROWS) if row % 8 >= 3)
 
 
-def sort_items(keys):
+def sort_items(keys, size, last):
     sub, lane = tile_iota(0), tile_iota(1)
-    size = 2
-    while size <= 8192:
+    while size <= last:
         half = size // 2
         while half >= 1:
             new = list(keys)
@@ -150,33 +150,47 @@
     return (found[0:rows] * 128.0 + found[rows : 2 * rows]).astype(I32)
 
 
-def relabel(conn_ref, send_ref, conn_out, own_out, pair_out, inverse_out, send_out):
-    for half in range(8):
-        start = (half % 2) * LANES
-        send_out[half : half + 1, :] = send_ref[0, 0, half // 2 : half // 2 + 1, start : start + LANES]
+def relabel_kernel(ids_ref, send_ref, conn_out, inverse_out):
     place = lax.broadcasted_iota(I32, (1, 8 * LANES), 1)
-    inverse_out[...] = inverse_of(one_line(send_out[...]), place, 8)
+    inverse_out[...] = inverse_of(one_line(send_ref[...]), place, 8)
+    for chunk in range(CHUNKS):
+        ids = ids_ref[0, 0, :, chunk * LANES : (chunk + 1) * LANES]
+        (label,) = table_picks([rows_of(inverse_out, 0)], 8, ids & 1023)
+        conn_out[8 * chunk : 8 * chunk + 8, :] = jnp.where(ids < 1024, label, ids)
+
+
+def to_lists(source_ref, channels, send_ref, out_ref):
+    tables = [rows_of(source_ref, NODE_ROWS * channel) for channel in range(channels)]
+    for channel, values in enumerate(table_picks(tables, 8, send_ref[...])):
+        base = NODE_ROWS * channel
+        out_ref[base : base + 8, :] = values
+        out_ref[base + 8 : base + 16, :] = source_ref[base + 8 : base + 16, :]
+
+
+def first_keys(ids_ref, own_out, pair_out):
+    place = lax.broadcasted_iota(I32, (1, 8 * LANES), 1)
+    own_out[...] = inverse_of(ids_ref[0, 0, 0:1, :], place, 8)
+    pair_line = jnp.concatenate(
+        [
+            ids_ref[0, 0, k : k + 1, chunk * LANES : (chunk + 1) * LANES]
+            for chunk in range(CHUNKS)
+            for k in (1, 2)
+        ],
+        axis=1,
+    )
+    pair_out[...] = inverse_of(pair_line, lax.broadcasted_iota(I32, (1, 16 * LANES), 1), NODE_ROWS)
     sub, lane = tile_iota(0), tile_iota(1)
     keys = []
     for chunk in range(CHUNKS):
-        ids = conn_ref[0, 0, :, chunk * LANES : (chunk + 1) * LANES]
-        (label,) = table_picks([rows_of(inverse_out, 0)], 8, ids & 1023)
-        ids = jnp.where(ids < 1024, label, ids)
-        conn_out[8 * chunk : 8 * chunk + 8, :] = ids
+        ids = ids_ref[0, 0, :, chunk * LANES : (chunk + 1) * LANES]
         item = ids * 8192 + (chunk * 1024 + sub * LANES + lane)
         keys.append(jnp.where(sub < 3, 2048 * 8192, item))
-    first_line = jnp.concatenate([conn_out[8 * chunk : 8 * chunk + 1, :] for chunk in range(CHUNKS)], axis=1)
-    own_out[...] = inverse_of(first_line, place, 8)
-    pair_line = jnp.concatenate(
-        [conn_out[8 * chunk + k : 8 * chunk + k + 1, :] for chunk in range(CHUNKS) for k in (1, 2)], axis=1
-    )
-    pair_out[...] = inverse_of(pair_line, lax.broadcasted_iota(I32, (1, 16 * LANES), 1), NODE_ROWS)
     return keys
 
 
 def make_order(keys, key_out, scan_out, end_out, keys_ref):
     sub, lane = tile_iota(0), tile_iota(1)
-    keys = sort_items(keys)
+    keys = sort_items(keys, 2 * SORT_FIRST, 8192)
     for register in range(8):
         keys_ref[8 * register : 8 * register + 8, :] = keys[register]
     group = lane * 8 + sub
@@ -228,21 +242,28 @@
             sorted_ref[base : base + 8, :] = values
     scan = scan_ref[...]
     follows = [(scan & (1 << step)) != 0 for step in range(len(SCAN_STEPS) + 1)]
+    runs = []
     for channel in range(channels):
         base = SORTED_ROWS * channel
-        runs = [sorted_ref[base : base + 8, :]]
+        mine = [sorted_ref[base : base + 8, :]]
         for register in range(1, RUNS):
             same = nodes[register] == nodes[register - 1]
             here = sorted_ref[base + 8 * register : base + 8 * register + 8, :]
-            runs.append(jnp.maximum(here, jnp.where(same, runs[-1], 0.0)))
-        total = runs[-1]
-        for step, distance in enumerate(SCAN_STEPS):
-            total = jnp.maximum(total, jnp.where(follows[step], group_shift(total, distance), 0.0))
-        carry = jnp.where(follows[-1], group_shift(total, 1), 0.0)
+            mine.append(jnp.maximum(here, jnp.where(same, mine[-1], 0.0)))
+        runs.append(mine)
+    totals = [mine[-1] for mine in runs]
+    for step, distance in enumerate(SCAN_STEPS):
+        totals = [
+            jnp.maximum(total, jnp.where(follows[step], group_shift(total, distance), 0.0))
+            for total in totals
+        ]
+    carries = [jnp.where(follows[-1], group_shift(total, 1), 0.0) for total in totals]
+    for channel in range(channels):
+        base = SORTED_ROWS * channel
         for register in range(RUNS):
             open_run = nodes[register] == nodes[0]
             sorted_ref[base + 8 * register : base + 8 * register + 8, :] = jnp.maximum(
-                runs[register], jnp.where(open_run, carry, 0.0)
+                runs[channel][register], jnp.where(open_run, carries[channel], 0.0)
             )
     sorted_tables = [rows_of(sorted_ref, SORTED_ROWS * channel) for channel in range(channels)]
     first_tables = [lambda row, at=at: at(8 * row) for at in tables]
@@ -426,21 +447,13 @@
             ref[3 * cone + start : 3 * cone + start + 1, :] = values[cone : cone + 1, :]
 
 
-def start_kernel(blocks_at, ids_at, send_at, *rest):
-    conn_out, plan, (inverse_out, send_out), rest = rest[0], rest[1:6], rest[6:8], rest[8:]
-    (row_out, part_out), packets, rest = rest[:2], rest[2:6], rest[6:]
-    blocks_ref, ids_ref, send_ref, keys, term, items, peaks, semaphores = rest
-    pairs = ((ids_at, ids_ref), (send_at, send_ref), (blocks_at, blocks_ref))
-    copies = [
-        pltpu.make_async_copy(source, target, semaphores.at[k])
-        for k, (source, target) in enumerate(pairs)
-    ]
-    for copy in copies:
-        copy.start()
-    copies[0].wait()
-    copies[1].wait()
-    first_keys = relabel(ids_ref, send_ref, conn_out, *plan[3:], inverse_out, send_out)
-    copies[2].wait()
+def start_kernel(blocks_at, ids_ref, *rest):
+    plan, (row_out, part_out), rest = rest[:5], rest[5:7], rest[7:]
+    blocks_ref, keys_ref, term, items, peaks, semaphore = rest
+    copy = pltpu.make_async_copy(blocks_at, blocks_ref, semaphore)
+    copy.start()
+    keys = sort_items(first_keys(ids_ref, *plan[3:]), 2, SORT_FIRST)
+    copy.wait()
     below, above = [live.astype(F32) for live in live_sides()]
     for chunk in range(CHUNKS):
         at = slice(chunk * LANES, (chunk + 1) * LANES)
@@ -450,8 +463,15 @@
     row_out[...] = 1.0 / jnp.sqrt(peaks[...])
     column_maxima(blocks_ref, None, term, 0)
     column_maxima(blocks_ref, row_out, term, 3)
-    make_order(first_keys, *plan[:3], keys)
+    make_order(keys, *plan[:3], keys_ref)
     scatter_maxima(term, 6, plan, items, part_out)
+
+
+def pack_kernel(part_ref, lists_ref, send_out, part_out, *packets):
+    for half in range(8):
+        start = (half % 2) * LANES
+        send_out[half : half + 1, :] = lists_ref[0, 0, half // 2 : half // 2 + 1, start : start + LANES]
+    to_lists(part_ref, 6, send_out, part_out)
     pack(part_out, 6, packets)
 
 
@@ -477,7 +497,8 @@
         row_maxima(blocks_ref, [node_picks(merged, 3, conn_ref, chunk)], at, peaks)
     row_out[...] = row_ref[...] / jnp.sqrt(row_ref[...] * peaks[...])
     column_maxima(blocks_ref, row_out, term, 0)
-    scatter_maxima(term, 3, plan, items, part_out)
+    scatter_maxima(term, 3, plan, items, merged)
+    to_lists(merged, 3, send_ref, part_out)
     pack(part_out, 3, packets)
     tables = [rows_of(loads_ref, 8 * c) for c in range(3)]
     for c, values in enumerate(table_picks(tables, 8, send_ref[...])):
@@ -691,29 +712,32 @@
     twice = ((6 * ITEM_ROWS, LANES), F32)
     ids = ((64, LANES), I32)
     few = ((8, LANES), I32)
-    conn, *rest = call(
+    *plan, row, part = call(
         start_kernel,
-        [ids, ((SORTED_ROWS, LANES), I32), few, ((16, LANES), I32), few, ((16, LANES), I32), few, few]
-        + [rows, ((96, LANES), F32)]
-        + [((24, LANES), F32)] * 4,
+        [((SORTED_ROWS, LANES), I32), few, ((16, LANES), I32), few, ((16, LANES), I32)]
+        + [rows, ((96, LANES), F32)],
         [
             ((1, 1, STRAINS, 24, 1024), F32),
-            ((1, 1, 8, 1024), I32),
-            ((1, 1, SIDES, 256), I32),
             ids,
             twice,
             ((6 * SORTED_ROWS, LANES), F32),
             rows,
-            pltpu.SemaphoreType.DMA((3,)),
+            pltpu.SemaphoreType.DMA,
         ],
         blocks,
         connectivity,
-        send_lists,
-        outside=(0, 1, 2),
+        outside=(0,),
         limit=LIMIT,
         work=12_000_000_000,
     )
-    plan, (inverse, send, row, part), packets = rest[:5], rest[5:9], rest[9:]
+    send, part, *packets = call(
+        pack_kernel,
+        [few, ((96, LANES), F32)] + [((24, LANES), F32)] * 4,
+        [],
+        part,
+        send_lists,
+    )
+    conn, inverse = call(relabel_kernel, [ids, few], [], connectivity, send, work=BESIDE)
     row, scale, part, loads, *packets = call(
         sweep_kernel,
         [rows, nodes, nodes, ((24, LANES), F32)] + [((18, LANES), F32)] * 4,

time: 81.2 us -> 79.4 us (0.978)
    pallas_call x11 -> x13, Pallas kernels: 18.2 us -> 17.5 us  [call(): pl.pallas_call(body, out_shape=[jax.ShapeDtypeStruct(shape, kind) for sha...]
  transfers between devices with their start and end apart: 19 -> 19, of which waited for: 9 -> 8; matrix products, arithmetic and copies ran while one was open for 0% -> 0% of each run, Pallas kernels for 3% -> 3%
where the time goes in v5:
time: 79.4 us; the launch traced here: 79.1 us
  starting transfers between devices  35 us (44%)
  waiting for transfers between devices  24.4 us (31%)
  Pallas kernels  17.5 us (22%)
  between operations  1.58 us (2%)
    ppermute x16, starting transfers between devices, exchange(): lax.ppermute(packet, axis, swap_pairs(axis, odd))  25.4 us
    pallas_call x13, Pallas kernels, call(): pl.pallas_call(body, out_shape=[jax.ShapeDtypeStruct(shape, kind) for sha...  17.5 us
    all_to_all x1, waiting for transfers between devices, per_device(): sums = lax.all_to_all(sums, AXES, 0, 0, tiled=True)  11.8 us
    ppermute x16, waiting for transfers between devices, exchange(): lax.ppermute(packet, axis, swap_pairs(axis, odd))  8.11 us
    all_to_all x1, starting transfers between devices, per_device(): sums = lax.all_to_all(sums, AXES, 0, 0, tiled=True)  8.02 us
    ppermute x2, waiting for transfers between devices, shift_up(): lax.ppermute(packet, axis, [(i, (i + 1) % count) for i in range(count)])  4.4 us
  transfers between devices with their start and end apart: 19, of which 8 were waited for; matrix products, arithmetic and copies ran while one was open for 0% of the time, Pallas kernels for 3%

profile of v5, /device:TPU:1, one launch (start us, length us, event | category | flops | bytes accessed | tf_op | source)
XLA Modules:
  0.0 79.1 jit_solution(10077519708908725684)
XLA Ops:
  0.6 0.8 copy-done.3
  1.4 7.2 %shard_map.68 = (s32[40,128]{1,0:T(8,128)S(1)}, s32[8,128]{1,0:T(8,128)S(1)}, s32[16,128]{1,0:T(8,128)S(1)}, s32[8,128]{1,0:T(8,128)S(1)}, s32[16,128]{1,0:T(8,1...) custom-call(f32[1,1,12,24,1024]{4,3,2,1,0:T(8,128)} %blocks_ref.13, s32[1,1,8,1024]{3,2,1,0:T(8,128)S(1)} %copy-done.3), custom_call_target="tpu_custom_call" | custom-call | flops 12000000000 | bytes 46875000 | tf_op jit(solution)/shard_map/pallas_call | solution.py:675
  8.6 0.1 shard_map.69
  8.7 8.7 %collective-permute-start = (f32[24,128]{1,0:T(8,128)S(1)}, f32[24,128]{1,0:T(8,128)S(1)}, u32[]{:S(2)}, u32[]{:S(2)}) collective-permute-start(f32[24,128]{1,0:T(8,128)S(1)} %get-tuple-element.58), channel_id=1, source_target_pairs={{0,31},{1,2},{2,1},{3,4},{4,3},{5,6},{6,5},{7,8},{8,7},{9,10},{10,... | collective-permute-start | bytes 36872 | tf_op jit(solution)/shard_map/ppermute | solution.py:698
  17.4 2.1 %collective-permute-start.1 = (f32[24,128]{1,0:T(8,128)S(1)}, f32[24,128]{1,0:T(8,128)S(1)}, u32[]{:S(2)}, u32[]{:S(2)}) collective-permute-start(f32[24,128]{1,0:T(8,128)S(1)} %get-tuple-element.59), channel_id=1, source_target_pairs={{0,224},{32,64},{64,32},{96,128},{128,96},{160,192},{192,160},{224... | collective-permute-start | bytes 36872 | tf_op jit(solution)/shard_map/ppermute | solution.py:698
  19.6 0.0 collective-permute-start.2
  19.6 1.0 %collective-permute-start.3 = (f32[24,128]{1,0:T(8,128)S(1)}, f32[24,128]{1,0:T(8,128)S(1)}, u32[]{:S(2)}, u32[]{:S(2)}) collective-permute-start(f32[24,128]{1,0:T(8,128)S(1)} %get-tuple-element.61), channel_id=1, source_target_pairs={{0,32},{32,0},{64,96},{96,64},{128,160},{160,128},{192,224},{224,1... | collective-permute-start | bytes 36872 | tf_op jit(solution)/shard_map/ppermute | solution.py:698
  20.6 0.4 shard_map.70
  20.9 0.0 collective-permute-done.rest_5_
  20.9 0.0 collective-permute-done.1.rest_6_
  21.0 1.4 %collective-permute-done.2.rest_7_ = f32[24,128]{1,0:T(8,128)S(1)} collective-permute-done((f32[24,128]{1,0:T(8,128)S(1)}, f32[24,128]{1,0:T(8,128)S(1)}, u32[]{:S(2)}, u32[]{:S(2)}) %collective-permute-start.2) | collective-permute-done | bytes 12320 | tf_op jit(solution)/shard_map/ppermute | solution.py:698
  22.3 0.0 collective-permute-done.3.rest_8_
  22.3 2.6 %shard_map.71 = (f32[12,1024]{1,0:T(8,128)S(1)}, f32[48,128]{1,0:T(8,128)S(1)}, f32[48,128]{1,0:T(8,128)S(1)}, f32[24,128]{1,0:T(8,128)S(1)}, f32[18,128]{1,0:T(...) custom-call(f32[1,1,12,24,1024]{4,3,2,1,0:T(8,128)S(1)} %copy-done, ...), custom_call_target="tpu_custom_call" | custom-call | tf_op jit(solution)/shard_map/pallas_call | solution.py:675
  25.0 1.3 %collective-permute-start.4 = (f32[18,128]{1,0:T(8,128)S(1)}, f32[18,128]{1,0:T(8,128)S(1)}, u32[]{:S(2)}, u32[]{:S(2)}) collective-permute-start(f32[18,128]{1,0:T(8,128)S(1)} %get-tuple-element.66), channel_id=1, source_target_pairs={{0,31},{1,2},{2,1},{3,4},{4,3},{5,6},{6,5},{7,8},{8,7},{9,10},{10,... | collective-permute-start | bytes 27656 | tf_op jit(solution)/shard_map/ppermute | solution.py:698
  26.3 3.1 %collective-permute-start.5 = (f32[18,128]{1,0:T(8,128)S(1)}, f32[18,128]{1,0:T(8,128)S(1)}, u32[]{:S(2)}, u32[]{:S(2)}) collective-permute-start(f32[18,128]{1,0:T(8,128)S(1)} %get-tuple-element.67), channel_id=1, source_target_pairs={{0,224},{32,64},{64,32},{96,128},{128,96},{160,192},{192,160},{224... | collective-permute-start | bytes 27656 | tf_op jit(solution)/shard_map/ppermute | solution.py:698
  29.3 0.0 collective-permute-start.6
  29.3 0.6 shard_map.72.row_ref
  29.9 1.0 %collective-permute-done.4.rest_0_ = f32[18,128]{1,0:T(8,128)S(1)} collective-permute-done((f32[18,128]{1,0:T(8,128)S(1)}, f32[18,128]{1,0:T(8,128)S(1)}, u32[]{:S(2)}, u32[]{:S(2)}) %collective-permute-start.4) | collective-permute-done | bytes 9248 | tf_op jit(solution)/shard_map/ppermute | solution.py:698
  30.9 1.3 %collective-permute-done.6.rest_2_ = f32[18,128]{1,0:T(8,128)S(1)} collective-permute-done((f32[18,128]{1,0:T(8,128)S(1)}, f32[18,128]{1,0:T(8,128)S(1)}, u32[]{:S(2)}, u32[]{:S(2)}) %collective-permute-start.6) | collective-permute-done | bytes 9248 | tf_op jit(solution)/shard_map/ppermute | solution.py:698
  32.2 0.0 collective-permute-done.7.rest_3_
  32.2 1.2 %shard_map.73 = (f32[48,128]{1,0:T(8,128)S(1)}, f32[12,1024]{1,0:T(8,128)S(1)}, f32[48,128]{1,0:T(8,128)S(1)}, f32[12,128]{1,0:T(8,128)S(1)}, f32[12,128]{1,0:T(...) custom-call(f32[1,1,12,24,1024]{4,3,2,1,0:T(8,128)S(1)} %copy-done, s32[64,128]{1,0:T(8,128)S(1)} %get-tuple-element.50.conn_ref, ...), custom_call_target="tpu_custom_call" | custom-call | tf_op jit(solution)/shard_map/pallas_call | solution.py:675
  33.3 0.4 collective-permute-start.10
  33.7 1.8 %collective-permute-start.11 = (f32[12,128]{1,0:T(8,128)S(1)}, f32[12,128]{1,0:T(8,128)S(1)}, u32[]{:S(2)}, u32[]{:S(2)}) collective-permute-start(f32[12,128]{1,0:T(8,128)S(1)} %get-tuple-element.77), channel_id=1, source_target_pairs={{0,32},{32,0},{64,96},{96,64},{128,160},{160,128},{192,224},{224,1... | collective-permute-start | bytes 18440 | tf_op jit(solution)/shard_map/ppermute | solution.py:698
  35.6 2.4 %collective-permute-start.8 = (f32[12,128]{1,0:T(8,128)S(1)}, f32[12,128]{1,0:T(8,128)S(1)}, u32[]{:S(2)}, u32[]{:S(2)}) collective-permute-start(f32[12,128]{1,0:T(8,128)S(1)} %get-tuple-element.74), channel_id=1, source_target_pairs={{0,31},{1,2},{2,1},{3,4},{4,3},{5,6},{6,5},{7,8},{8,7},{9,10},{10,... | collective-permute-start | bytes 18440 | tf_op jit(solution)/shard_map/ppermute | solution.py:698
  37.9 0.1 collective-permute-start.9
  38.0 0.8 %shard_map.74 = (f32[12,1024]{1,0:T(8,128)S(1)}, f32[48,128]{1,0:T(8,128)S(1)}) custom-call(f32[1,1,12,24,1024]{4,3,2,1,0:T(8,128)S(1)} %copy-done, s32[64,128]{1,0:T(8,128)S(1)} %get-tuple-element.50.conn_ref, f32[12,1024]{1,0:T(8,128)S(1)} %shard_map.72.row_ref, f32[48,128]{1,0:T(8,128)S(1)} %get-tuple-element.70.scale_ref, ...), custom_call_target="tpu_custom_call" | custom-call | flops 1000000000 | bytes 3906250 | tf_op jit(solution)/shard_map/pallas_call | solution.py:675
  38.8 0.0 collective-permute-done.10.rest_2_
  38.8 0.0 collective-permute-done.11.rest_3_
  38.8 2.6 %collective-permute-done.8.rest_0_ = f32[12,128]{1,0:T(8,128)S(1)} collective-permute-done((f32[12,128]{1,0:T(8,128)S(1)}, f32[12,128]{1,0:T(8,128)S(1)}, u32[]{:S(2)}, u32[]{:S(2)}) %collective-permute-start.8) | collective-permute-done | bytes 6176 | tf_op jit(solution)/shard_map/ppermute | solution.py:698
  41.4 0.0 collective-permute-done.9.rest_1_
  41.4 1.1 %shard_map.75 = (f32[96,128]{1,0:T(8,128)S(1)}, f32[24,128]{1,0:T(8,128)S(1)}, f32[24,128]{1,0:T(8,128)S(1)}, f32[24,128]{1,0:T(8,128)S(1)}, f32[24,128]{1,0:T(8,128)S(1)}) custom-call(f32[1,1,12,24,1024]{4,3,2,1,0:T(8,128)S(1)} %copy-done, s32[64,128]{1,0:T(8,128)S(1)} %get-tuple-element.50.conn_ref, f32[12,1024]{1,0:T(8,128)S(1)} %shard_map.72.row_ref, ...), custom_call_target="tpu_custom_call" | custom-call | tf_op jit(solution)/shard_map/pallas_call | solution.py:675
  42.5 2.5 %collective-permute-start.12 = (f32[24,128]{1,0:T(8,128)S(1)}, f32[24,128]{1,0:T(8,128)S(1)}, u32[]{:S(2)}, u32[]{:S(2)}) collective-permute-start(f32[24,128]{1,0:T(8,128)S(1)} %get-tuple-element.79), channel_id=1, source_target_pairs={{0,31},{1,2},{2,1},{3,4},{4,3},{5,6},{6,5},{7,8},{8,7},{9,10},{10,... | collective-permute-start | bytes 36872 | tf_op jit(solution)/shard_map/ppermute | solution.py:698
  45.0 1.2 %collective-permute-start.13 = (f32[24,128]{1,0:T(8,128)S(1)}, f32[24,128]{1,0:T(8,128)S(1)}, u32[]{:S(2)}, u32[]{:S(2)}) collective-permute-start(f32[24,128]{1,0:T(8,128)S(1)} %get-tuple-element.80), channel_id=1, source_target_pairs={{0,224},{32,64},{64,32},{96,128},{128,96},{160,192},{192,160},{224... | collective-permute-start | bytes 36872 | tf_op jit(solution)/shard_map/ppermute | solution.py:698
  46.2 0.0 collective-permute-start.14
  46.2 0.9 %collective-permute-start.15 = (f32[24,128]{1,0:T(8,128)S(1)}, f32[24,128]{1,0:T(8,128)S(1)}, u32[]{:S(2)}, u32[]{:S(2)}) collective-permute-start(f32[24,128]{1,0:T(8,128)S(1)} %get-tuple-element.82), channel_id=1, source_target_pairs={{0,32},{32,0},{64,96},{96,64},{128,160},{160,128},{192,224},{224,1... | collective-permute-start | bytes 36872 | tf_op jit(solution)/shard_map/ppermute | solution.py:698
  47.1 1.4 %collective-permute-done.12.rest_0_ = f32[24,128]{1,0:T(8,128)S(1)} collective-permute-done((f32[24,128]{1,0:T(8,128)S(1)}, f32[24,128]{1,0:T(8,128)S(1)}, u32[]{:S(2)}, u32[]{:S(2)}) %collective-permute-start.12) | collective-permute-done | bytes 12320 | tf_op jit(solution)/shard_map/ppermute | solution.py:698
  48.5 0.0 collective-permute-done.13.rest_1_
  48.5 0.5 collective-permute-done.14.rest_2_
  49.1 1.1 %shard_map.76 = (f32[1,128]{1,0:T(1,128)S(1)}, f32[48,128]{1,0:T(8,128)S(1)}, f32[48,128]{1,0:T(8,128)S(1)}, f32[12,128]{1,0:T(8,128)S(1)}, f32[12,128]{1,0:T(8,128)S(1)}) custom-call(f32[1,1,12,24,1024]{4,3,2,1,0:T(8,128)S(1)} %copy-done, s32[64,128]{1,0:T(8,128)S(1)} %get-tuple-element.50.conn_ref, f32[12,1024]{1,0:T(8,128)S(1)} %shard_map.72.row_ref, ...), custom_call_target="tpu_custom_call" | custom-call | tf_op jit(solution)/shard_map/pallas_call | solution.py:675
  50.2 0.7 collective-permute-start.16
  50.9 0.8 collective-permute-start.17
  51.7 4.4 %collective-permute-done.16.left_ref = f32[12,128]{1,0:T(8,128)S(1)} collective-permute-done((f32[12,128]{1,0:T(8,128)S(1)}, f32[12,128]{1,0:T(8,128)S(1)}, u32[]{:S(2)}, u32[]{:S(2)}) %collective-permute-start.16) | collective-permute-done | bytes 6176 | tf_op jit(solution)/shard_map/ppermute | solution.py:704
  56.1 0.8 shard_map.77
  56.9 8.0 %all-to-all-start = ((f32[256,1,128]{2,1,0:T(1,128)}), f32[256,1,128]{2,1,0:T(1,128)S(1)}, u32[]{:S(2)}, u32[]{:S(2)}) async-start(f32[256,1,128]{2,1,0:T(1,128)} %bitcast.2), calls=%async_computation | async-start | bytes 262144 | tf_op jit(solution)/shard_map/all_to_all | solution.py:817
  65.5 0.6 shard_map.79.joint_ref
  66.1 0.1 shard_map.78.velocity_ref
  66.2 11.8 %all-to-all-done = f32[256,1,128]{2,1,0:T(1,128)S(1)} async-done(((f32[256,1,128]{2,1,0:T(1,128)}), f32[256,1,128]{2,1,0:T(1,128)S(1)}, u32[]{:S(2)}, u32[]{:S(2)}) %all-to-all-start) | async-done | bytes 131104 | tf_op jit(solution)/shard_map/all_to_all | solution.py:817
  78.1 0.9 %shard_map.80 = (f32[24,128]{1,0:T(8,128)}, f32[96,128]{1,0:T(8,128)}) custom-call(f32[256,128]{1,0:T(8,128)S(1)} %bitcast.7, f32[1]{0:T(128)S(6)} %copy.14.step_ref, f32[48,128]{1,0:T(8,128)S(1)} %shard_map.78.velocity_ref, f32[12,1024]{1,0:T(8,128)S(1)} %get-tuple-element.91.base_ref, f32[12,1024]{1,0:T(8,128)S(1)} %shard_map.79.joint_ref, ...), custom_call_target="tpu_custom_call" | custom-call | tf_op jit(solution)/shard_map/pallas_call | solution.py:675
  (11 shorter events, 0.0 us)
Async XLA Ops:
  0.6 8.0 %copy-start.2 = (s32[1,1,4,256]{3,2,1,0:T(4,128)S(1)}, s32[1,1,4,256]{3,2,1,0:T(4,128)}, u32[]{:S(2)}) copy-start(s32[1,1,4,256]{3,2,1,0:T(4,128)} %lists_ref.1) | copy-start | bytes 12292
  0.6 0.8 copy-start.3
  8.7 12.2 %collective-permute-start = (f32[24,128]{1,0:T(8,128)S(1)}, f32[24,128]{1,0:T(8,128)S(1)}, u32[]{:S(2)}, u32[]{:S(2)}) collective-permute-start(f32[24,128]{1,0:T(8,128)S(1)} %get-tuple-element.58), channel_id=1, source_target_pairs={{0,31},{1,2},{2,1},{3,4},{4,3},{5,6},{6,5},{7,8},{8,7},{9,10},{10,... | collective-permute-start | bytes 36872 | tf_op jit(solution)/shard_map/ppermute | solution.py:698
  17.4 3.5 %collective-permute-start.1 = (f32[24,128]{1,0:T(8,128)S(1)}, f32[24,128]{1,0:T(8,128)S(1)}, u32[]{:S(2)}, u32[]{:S(2)}) collective-permute-start(f32[24,128]{1,0:T(8,128)S(1)} %get-tuple-element.59), channel_id=1, source_target_pairs={{0,224},{32,64},{64,32},{96,128},{128,96},{160,192},{192,160},{224... | collective-permute-start | bytes 36872 | tf_op jit(solution)/shard_map/ppermute | solution.py:698
  19.6 2.8 %collective-permute-start.2 = (f32[24,128]{1,0:T(8,128)S(1)}, f32[24,128]{1,0:T(8,128)S(1)}, u32[]{:S(2)}, u32[]{:S(2)}) collective-permute-start(f32[24,128]{1,0:T(8,128)S(1)} %get-tuple-element.60), channel_id=1, source_target_pairs={{0,1},{1,0},{2,3},{3,2},{4,5},{5,4},{6,7},{7,6},{8,9},{9,8},{10,11... | collective-permute-start | bytes 36872 | tf_op jit(solution)/shard_map/ppermute | solution.py:698
  19.6 2.8 %collective-permute-start.3 = (f32[24,128]{1,0:T(8,128)S(1)}, f32[24,128]{1,0:T(8,128)S(1)}, u32[]{:S(2)}, u32[]{:S(2)}) collective-permute-start(f32[24,128]{1,0:T(8,128)S(1)} %get-tuple-element.61), channel_id=1, source_target_pairs={{0,32},{32,0},{64,96},{96,64},{128,160},{160,128},{192,224},{224,1... | collective-permute-start | bytes 36872 | tf_op jit(solution)/shard_map/ppermute | solution.py:698
  20.6 1.8 %copy-start = (f32[1,1,12,24,1024]{4,3,2,1,0:T(8,128)S(1)}, f32[1,1,12,24,1024]{4,3,2,1,0:T(8,128)}, u32[]{:S(2)}) copy-start(f32[1,1,12,24,1024]{4,3,2,1,0:T(8,128)} %blocks_ref.13) | copy-start | bytes 3538948
  20.6 1.8 %copy-start.1 = (f32[1,1,3,1024]{3,1,2,0:T(1,128)S(1)}, f32[1,1,3,1024]{3,1,2,0:T(1,128)}, u32[]{:S(2)}) copy-start(f32[1,1,3,1024]{3,1,2,0:T(1,128)} %param.8) | copy-start | bytes 36868
  25.0 6.0 %collective-permute-start.4 = (f32[18,128]{1,0:T(8,128)S(1)}, f32[18,128]{1,0:T(8,128)S(1)}, u32[]{:S(2)}, u32[]{:S(2)}) collective-permute-start(f32[18,128]{1,0:T(8,128)S(1)} %get-tuple-element.66), channel_id=1, source_target_pairs={{0,31},{1,2},{2,1},{3,4},{4,3},{5,6},{6,5},{7,8},{8,7},{9,10},{10,... | collective-permute-start | bytes 27656 | tf_op jit(solution)/shard_map/ppermute | solution.py:698
  26.3 4.6 %collective-permute-start.5 = (f32[18,128]{1,0:T(8,128)S(1)}, f32[18,128]{1,0:T(8,128)S(1)}, u32[]{:S(2)}, u32[]{:S(2)}) collective-permute-start(f32[18,128]{1,0:T(8,128)S(1)} %get-tuple-element.67), channel_id=1, source_target_pairs={{0,224},{32,64},{64,32},{96,128},{128,96},{160,192},{192,160},{224... | collective-permute-start | bytes 27656 | tf_op jit(solution)/shard_map/ppermute | solution.py:698
  29.3 2.8 %collective-permute-start.6 = (f32[18,128]{1,0:T(8,128)S(1)}, f32[18,128]{1,0:T(8,128)S(1)}, u32[]{:S(2)}, u32[]{:S(2)}) collective-permute-start(f32[18,128]{1,0:T(8,128)S(1)} %get-tuple-element.68), channel_id=1, source_target_pairs={{0,1},{1,0},{2,3},{3,2},{4,5},{5,4},{6,7},{7,6},{8,9},{9,8},{10,11... | collective-permute-start | bytes 27656 | tf_op jit(solution)/shard_map/ppermute | solution.py:698
  29.3 2.8 %collective-permute-start.7 = (f32[18,128]{1,0:T(8,128)S(1)}, f32[18,128]{1,0:T(8,128)S(1)}, u32[]{:S(2)}, u32[]{:S(2)}) collective-permute-start(f32[18,128]{1,0:T(8,128)S(1)} %get-tuple-element.69), channel_id=1, source_target_pairs={{0,32},{32,0},{64,96},{96,64},{128,160},{160,128},{192,224},{224,1... | collective-permute-start | bytes 27656 | tf_op jit(solution)/shard_map/ppermute | solution.py:698
  33.3 5.5 %collective-permute-start.10 = (f32[12,128]{1,0:T(8,128)S(1)}, f32[12,128]{1,0:T(8,128)S(1)}, u32[]{:S(2)}, u32[]{:S(2)}) collective-permute-start(f32[12,128]{1,0:T(8,128)S(1)} %get-tuple-element.76), channel_id=1, source_target_pairs={{0,1},{1,0},{2,3},{3,2},{4,5},{5,4},{6,7},{7,6},{8,9},{9,8},{10,11... | collective-permute-start | bytes 18440 | tf_op jit(solution)/shard_map/ppermute | solution.py:698
  33.7 5.1 %collective-permute-start.11 = (f32[12,128]{1,0:T(8,128)S(1)}, f32[12,128]{1,0:T(8,128)S(1)}, u32[]{:S(2)}, u32[]{:S(2)}) collective-permute-start(f32[12,128]{1,0:T(8,128)S(1)} %get-tuple-element.77), channel_id=1, source_target_pairs={{0,32},{32,0},{64,96},{96,64},{128,160},{160,128},{192,224},{224,1... | collective-permute-start | bytes 18440 | tf_op jit(solution)/shard_map/ppermute | solution.py:698
  35.6 5.8 %collective-permute-start.8 = (f32[12,128]{1,0:T(8,128)S(1)}, f32[12,128]{1,0:T(8,128)S(1)}, u32[]{:S(2)}, u32[]{:S(2)}) collective-permute-start(f32[12,128]{1,0:T(8,128)S(1)} %get-tuple-element.74), channel_id=1, source_target_pairs={{0,31},{1,2},{2,1},{3,4},{4,3},{5,6},{6,5},{7,8},{8,7},{9,10},{10,... | collective-permute-start | bytes 18440 | tf_op jit(solution)/shard_map/ppermute | solution.py:698
  37.9 3.5 %collective-permute-start.9 = (f32[12,128]{1,0:T(8,128)S(1)}, f32[12,128]{1,0:T(8,128)S(1)}, u32[]{:S(2)}, u32[]{:S(2)}) collective-permute-start(f32[12,128]{1,0:T(8,128)S(1)} %get-tuple-element.75), channel_id=1, source_target_pairs={{0,224},{32,64},{64,32},{96,128},{128,96},{160,192},{192,160},{224... | collective-permute-start | bytes 18440 | tf_op jit(solution)/shard_map/ppermute | solution.py:698
  42.5 6.0 %collective-permute-start.12 = (f32[24,128]{1,0:T(8,128)S(1)}, f32[24,128]{1,0:T(8,128)S(1)}, u32[]{:S(2)}, u32[]{:S(2)}) collective-permute-start(f32[24,128]{1,0:T(8,128)S(1)} %get-tuple-element.79), channel_id=1, source_target_pairs={{0,31},{1,2},{2,1},{3,4},{4,3},{5,6},{6,5},{7,8},{8,7},{9,10},{10,... | collective-permute-start | bytes 36872 | tf_op jit(solution)/shard_map/ppermute | solution.py:698
  45.0 3.5 %collective-permute-start.13 = (f32[24,128]{1,0:T(8,128)S(1)}, f32[24,128]{1,0:T(8,128)S(1)}, u32[]{:S(2)}, u32[]{:S(2)}) collective-permute-start(f32[24,128]{1,0:T(8,128)S(1)} %get-tuple-element.80), channel_id=1, source_target_pairs={{0,224},{32,64},{64,32},{96,128},{128,96},{160,192},{192,160},{224... | collective-permute-start | bytes 36872 | tf_op jit(solution)/shard_map/ppermute | solution.py:698
  46.2 2.8 %collective-permute-start.14 = (f32[24,128]{1,0:T(8,128)S(1)}, f32[24,128]{1,0:T(8,128)S(1)}, u32[]{:S(2)}, u32[]{:S(2)}) collective-permute-start(f32[24,128]{1,0:T(8,128)S(1)} %get-tuple-element.81), channel_id=1, source_target_pairs={{0,1},{1,0},{2,3},{3,2},{4,5},{5,4},{6,7},{7,6},{8,9},{9,8},{10,11... | collective-permute-start | bytes 36872 | tf_op jit(solution)/shard_map/ppermute | solution.py:698
  46.2 2.8 %collective-permute-start.15 = (f32[24,128]{1,0:T(8,128)S(1)}, f32[24,128]{1,0:T(8,128)S(1)}, u32[]{:S(2)}, u32[]{:S(2)}) collective-permute-start(f32[24,128]{1,0:T(8,128)S(1)} %get-tuple-element.82), channel_id=1, source_target_pairs={{0,32},{32,0},{64,96},{96,64},{128,160},{160,128},{192,224},{224,1... | collective-permute-start | bytes 36872 | tf_op jit(solution)/shard_map/ppermute | solution.py:698
  50.2 5.9 %collective-permute-start.16 = (f32[12,128]{1,0:T(8,128)S(1)}, f32[12,128]{1,0:T(8,128)S(1)}, u32[]{:S(2)}, u32[]{:S(2)}) collective-permute-start(f32[12,128]{1,0:T(8,128)S(1)} %get-tuple-element.85), channel_id=1, source_target_pairs={{0,1},{1,2},{2,3},{3,4},{4,5},{5,6},{6,7},{7,8},{8,9},{9,10},{10,1... | collective-permute-start | bytes 18440 | tf_op jit(solution)/shard_map/ppermute | solution.py:704
  50.9 5.2 %collective-permute-start.17 = (f32[12,128]{1,0:T(8,128)S(1)}, f32[12,128]{1,0:T(8,128)S(1)}, u32[]{:S(2)}, u32[]{:S(2)}) collective-permute-start(f32[12,128]{1,0:T(8,128)S(1)} %get-tuple-element.86), channel_id=1, source_target_pairs={{0,32},{32,64},{64,96},{96,128},{128,160},{160,192},{192,224},{224... | collective-permute-start | bytes 18440 | tf_op jit(solution)/shard_map/ppermute | solution.py:704
  56.9 21.2 %all-to-all-start = ((f32[256,1,128]{2,1,0:T(1,128)}), f32[256,1,128]{2,1,0:T(1,128)S(1)}, u32[]{:S(2)}, u32[]{:S(2)}) async-start(f32[256,1,128]{2,1,0:T(1,128)} %bitcast.2), calls=%async_computation | async-start | bytes 262144 | tf_op jit(solution)/shard_map/all_to_all | solution.py:817

commit v6 on v5

--- a/solution.py
+++ b/solution.py
@@ -74,7 +74,8 @@
 
 SCAN_STEPS = tuple(1 << step for step in range(10))
 RUNS = 5
-SORT_FIRST = 64
+NEAR_STEPS = 2
+SORT_FIRST = 512
 SORTED_ROWS = 8 * RUNS
 LOOSE_ROWS = tuple(row for row in range(ITEM_ROWS) if row % 8 >= 3)
 
@@ -230,7 +231,7 @@
         end_out[8 * half : 8 * half + 8, :] = jnp.where(named, end, 8192)
 
 
-def scatter_maxima(term_ref, channels, plan, sorted_ref, out_ref):
+def scatter_maxima(term_ref, channels, plan, sorted_ref, total_ref, out_ref):
     key_ref, scan_ref, end_ref, own_ref, pair_ref = plan
     tables = [rows_of(term_ref, ITEM_ROWS * channel) for channel in range(channels)]
     nodes = []
@@ -241,6 +242,8 @@
             base = SORTED_ROWS * channel + 8 * register
             sorted_ref[base : base + 8, :] = values
     scan = scan_ref[...]
+    reach = (scan & ((1 << len(SCAN_STEPS)) - (1 << NEAR_STEPS))).astype(F32)
+    far = jnp.max(reach) > 0.0
     follows = [(scan & (1 << step)) != 0 for step in range(len(SCAN_STEPS) + 1)]
     runs = []
     for channel in range(channels):
@@ -251,12 +254,27 @@
             here = sorted_ref[base + 8 * register : base + 8 * register + 8, :]
             mine.append(jnp.maximum(here, jnp.where(same, mine[-1], 0.0)))
         runs.append(mine)
-    totals = [mine[-1] for mine in runs]
-    for step, distance in enumerate(SCAN_STEPS):
-        totals = [
-            jnp.maximum(total, jnp.where(follows[step], group_shift(total, distance), 0.0))
-            for total in totals
-        ]
+
+    def joined(totals, steps):
+        for step in steps:
+            shifted = [group_shift(total, SCAN_STEPS[step]) for total in totals]
+            totals = [
+                jnp.maximum(total, jnp.where(follows[step], other, 0.0))
+                for total, other in zip(totals, shifted)
+            ]
+        return totals
+
+    totals = joined([mine[-1] for mine in runs], range(NEAR_STEPS))
+    for channel, total in enumerate(totals):
+        total_ref[8 * channel : 8 * channel + 8, :] = total
+
+    @pl.when(far)
+    def _():
+        mine = [total_ref[8 * channel : 8 * channel + 8, :] for channel in range(channels)]
+        for channel, total in enumerate(joined(mine, range(NEAR_STEPS, len(SCAN_STEPS)))):
+            total_ref[8 * channel : 8 * channel + 8, :] = total
+
+    totals = [total_ref[8 * channel : 8 * channel + 8, :] for channel in range(channels)]
     carries = [jnp.where(follows[-1], group_shift(total, 1), 0.0) for total in totals]
     for channel in range(channels):
         base = SORTED_ROWS * channel
@@ -449,7 +467,7 @@
 
 def start_kernel(blocks_at, ids_ref, *rest):
     plan, (row_out, part_out), rest = rest[:5], rest[5:7], rest[7:]
-    blocks_ref, keys_ref, term, items, peaks, semaphore = rest
+    blocks_ref, keys_ref, term, items, totals, peaks, semaphore = rest
     copy = pltpu.make_async_copy(blocks_at, blocks_ref, semaphore)
     copy.start()
     keys = sort_items(first_keys(ids_ref, *plan[3:]), 2, SORT_FIRST)
@@ -464,7 +482,7 @@
     column_maxima(blocks_ref, None, term, 0)
     column_maxima(blocks_ref, row_out, term, 3)
     make_order(keys, *plan[:3], keys_ref)
-    scatter_maxima(term, 6, plan, items, part_out)
+    scatter_maxima(term, 6, plan, items, totals, part_out)
 
 
 def pack_kernel(part_ref, lists_ref, send_out, part_out, *packets):
@@ -481,7 +499,7 @@
     plan, rest = rest[:5], rest[5:]
     arrived, rest = by_side(rest[:4]), rest[4:]
     row_out, scale_out, part_out, loads_out, rest = rest[0], rest[1], rest[2], rest[3], rest[4:]
-    packets, (term, items, peaks, merged) = rest[:4], rest[4:]
+    packets, (term, items, totals, peaks, merged) = rest[:4], rest[4:]
     unpack(part_ref, 6, arrived, jnp.maximum, merged)
     row = lax.broadcasted_iota(I32, (NODE_ROWS, LANES), 0)
     below, above = [live.astype(F32) for live in live_sides()]
@@ -497,7 +515,7 @@
         row_maxima(blocks_ref, [node_picks(merged, 3, conn_ref, chunk)], at, peaks)
     row_out[...] = row_ref[...] / jnp.sqrt(row_ref[...] * peaks[...])
     column_maxima(blocks_ref, row_out, term, 0)
-    scatter_maxima(term, 3, plan, items, merged)
+    scatter_maxima(term, 3, plan, items, totals, merged)
     to_lists(merged, 3, send_ref, part_out)
     pack(part_out, 3, packets)
     tables = [rows_of(loads_ref, 8 * c) for c in range(3)]
@@ -721,6 +739,7 @@
             ids,
             twice,
             ((6 * SORTED_ROWS, LANES), F32),
+            nodes,
             rows,
             pltpu.SemaphoreType.DMA,
         ],
@@ -741,7 +760,7 @@
     row, scale, part, loads, *packets = call(
         sweep_kernel,
         [rows, nodes, nodes, ((24, LANES), F32)] + [((18, LANES), F32)] * 4,
-        [items, ((3 * SORTED_ROWS, LANES), F32), rows, ((96, LANES), F32)],
+        [items, ((3 * SORTED_ROWS, LANES), F32), ((24, LANES), F32), rows, ((96, LANES), F32)],
         blocks,
         conn,
         row,

time: 79.4 us -> 78 us (0.982)
  Pallas kernels: 17.5 us -> 16.1 us
    pallas_call x13, Pallas kernels: 17.5 us -> 16.1 us  [call(): pl.pallas_call(body, out_shape=[jax.ShapeDtypeStruct(shape, kind) for sha...]
where the time goes in v6:
time: 78 us; the launch traced here: 77.8 us
  starting transfers between devices  35 us (45%)
  waiting for transfers between devices  24.3 us (31%)
  Pallas kernels  16.1 us (21%)
  between operations  1.58 us (2%)
    ppermute x16, starting transfers between devices, exchange(): lax.ppermute(packet, axis, swap_pairs(axis, odd))  25.4 us
    pallas_call x13, Pallas kernels, call(): pl.pallas_call(body, out_shape=[jax.ShapeDtypeStruct(shape, kind) for sha...  16.1 us
    all_to_all x1, waiting for transfers between devices, per_device(): sums = lax.all_to_all(sums, AXES, 0, 0, tiled=True)  11.8 us
    ppermute x16, waiting for transfers between devices, exchange(): lax.ppermute(packet, axis, swap_pairs(axis, odd))  8.11 us
    all_to_all x1, starting transfers between devices, per_device(): sums = lax.all_to_all(sums, AXES, 0, 0, tiled=True)  8.02 us
    ppermute x2, waiting for transfers between devices, shift_up(): lax.ppermute(packet, axis, [(i, (i + 1) % count) for i in range(count)])  4.4 us
  transfers between devices with their start and end apart: 19, of which 8 were waited for; matrix products, arithmetic and copies ran while one was open for 0% of the time, Pallas kernels for 3%

profile of v6, /device:TPU:1, one launch (start us, length us, event | category | flops | bytes accessed | tf_op | source)
XLA Modules:
  0.0 77.8 jit_solution(9250065757649817528)
XLA Ops:
  0.6 0.8 copy-done.3
  1.4 6.3 %shard_map.68 = (s32[40,128]{1,0:T(8,128)S(1)}, s32[8,128]{1,0:T(8,128)S(1)}, s32[16,128]{1,0:T(8,128)S(1)}, s32[8,128]{1,0:T(8,128)S(1)}, s32[16,128]{1,0:T(8,1...) custom-call(f32[1,1,12,24,1024]{4,3,2,1,0:T(8,128)} %blocks_ref.13, s32[1,1,8,1024]{3,2,1,0:T(8,128)S(1)} %copy-done.3), custom_call_target="tpu_custom_call" | custom-call | flops 12000000000 | bytes 46875000 | tf_op jit(solution)/shard_map/pallas_call | solution.py:693
  7.7 0.1 shard_map.69
  7.9 8.7 %collective-permute-start = (f32[24,128]{1,0:T(8,128)S(1)}, f32[24,128]{1,0:T(8,128)S(1)}, u32[]{:S(2)}, u32[]{:S(2)}) collective-permute-start(f32[24,128]{1,0:T(8,128)S(1)} %get-tuple-element.58), channel_id=1, source_target_pairs={{0,31},{1,2},{2,1},{3,4},{4,3},{5,6},{6,5},{7,8},{8,7},{9,10},{10,... | collective-permute-start | bytes 36872 | tf_op jit(solution)/shard_map/ppermute | solution.py:716
  16.6 2.1 %collective-permute-start.1 = (f32[24,128]{1,0:T(8,128)S(1)}, f32[24,128]{1,0:T(8,128)S(1)}, u32[]{:S(2)}, u32[]{:S(2)}) collective-permute-start(f32[24,128]{1,0:T(8,128)S(1)} %get-tuple-element.59), channel_id=1, source_target_pairs={{0,224},{32,64},{64,32},{96,128},{128,96},{160,192},{192,160},{224... | collective-permute-start | bytes 36872 | tf_op jit(solution)/shard_map/ppermute | solution.py:716
  18.7 0.0 collective-permute-start.2
  18.7 1.0 %collective-permute-start.3 = (f32[24,128]{1,0:T(8,128)S(1)}, f32[24,128]{1,0:T(8,128)S(1)}, u32[]{:S(2)}, u32[]{:S(2)}) collective-permute-start(f32[24,128]{1,0:T(8,128)S(1)} %get-tuple-element.61), channel_id=1, source_target_pairs={{0,32},{32,0},{64,96},{96,64},{128,160},{160,128},{192,224},{224,1... | collective-permute-start | bytes 36872 | tf_op jit(solution)/shard_map/ppermute | solution.py:716
  19.7 0.4 shard_map.70
  20.1 0.0 collective-permute-done.rest_5_
  20.1 0.0 collective-permute-done.1.rest_6_
  20.1 1.4 %collective-permute-done.2.rest_7_ = f32[24,128]{1,0:T(8,128)S(1)} collective-permute-done((f32[24,128]{1,0:T(8,128)S(1)}, f32[24,128]{1,0:T(8,128)S(1)}, u32[]{:S(2)}, u32[]{:S(2)}) %collective-permute-start.2) | collective-permute-done | bytes 12320 | tf_op jit(solution)/shard_map/ppermute | solution.py:716
  21.5 0.0 collective-permute-done.3.rest_8_
  21.5 2.1 %shard_map.71 = (f32[12,1024]{1,0:T(8,128)S(1)}, f32[48,128]{1,0:T(8,128)S(1)}, f32[48,128]{1,0:T(8,128)S(1)}, f32[24,128]{1,0:T(8,128)S(1)}, f32[18,128]{1,0:T(...) custom-call(f32[1,1,12,24,1024]{4,3,2,1,0:T(8,128)S(1)} %copy-done, ...), custom_call_target="tpu_custom_call" | custom-call | tf_op jit(solution)/shard_map/pallas_call | solution.py:693
  23.6 1.3 %collective-permute-start.4 = (f32[18,128]{1,0:T(8,128)S(1)}, f32[18,128]{1,0:T(8,128)S(1)}, u32[]{:S(2)}, u32[]{:S(2)}) collective-permute-start(f32[18,128]{1,0:T(8,128)S(1)} %get-tuple-element.66), channel_id=1, source_target_pairs={{0,31},{1,2},{2,1},{3,4},{4,3},{5,6},{6,5},{7,8},{8,7},{9,10},{10,... | collective-permute-start | bytes 27656 | tf_op jit(solution)/shard_map/ppermute | solution.py:716
  24.9 3.1 %collective-permute-start.5 = (f32[18,128]{1,0:T(8,128)S(1)}, f32[18,128]{1,0:T(8,128)S(1)}, u32[]{:S(2)}, u32[]{:S(2)}) collective-permute-start(f32[18,128]{1,0:T(8,128)S(1)} %get-tuple-element.67), channel_id=1, source_target_pairs={{0,224},{32,64},{64,32},{96,128},{128,96},{160,192},{192,160},{224... | collective-permute-start | bytes 27656 | tf_op jit(solution)/shard_map/ppermute | solution.py:716
  28.0 0.0 collective-permute-start.6
  28.0 0.0 collective-permute-start.7
  28.0 0.6 shard_map.72.row_ref
  28.6 1.0 %collective-permute-done.4.rest_0_ = f32[18,128]{1,0:T(8,128)S(1)} collective-permute-done((f32[18,128]{1,0:T(8,128)S(1)}, f32[18,128]{1,0:T(8,128)S(1)}, u32[]{:S(2)}, u32[]{:S(2)}) %collective-permute-start.4) | collective-permute-done | bytes 9248 | tf_op jit(solution)/shard_map/ppermute | solution.py:716
  29.6 0.0 collective-permute-done.5.rest_1_
  29.6 1.3 %collective-permute-done.6.rest_2_ = f32[18,128]{1,0:T(8,128)S(1)} collective-permute-done((f32[18,128]{1,0:T(8,128)S(1)}, f32[18,128]{1,0:T(8,128)S(1)}, u32[]{:S(2)}, u32[]{:S(2)}) %collective-permute-start.6) | collective-permute-done | bytes 9248 | tf_op jit(solution)/shard_map/ppermute | solution.py:716
  30.8 1.2 %shard_map.73 = (f32[48,128]{1,0:T(8,128)S(1)}, f32[12,1024]{1,0:T(8,128)S(1)}, f32[48,128]{1,0:T(8,128)S(1)}, f32[12,128]{1,0:T(8,128)S(1)}, f32[12,128]{1,0:T(...) custom-call(f32[1,1,12,24,1024]{4,3,2,1,0:T(8,128)S(1)} %copy-done, s32[64,128]{1,0:T(8,128)S(1)} %get-tuple-element.50.conn_ref, ...), custom_call_target="tpu_custom_call" | custom-call | tf_op jit(solution)/shard_map/pallas_call | solution.py:693
  32.0 0.4 collective-permute-start.10
  32.4 1.8 %collective-permute-start.11 = (f32[12,128]{1,0:T(8,128)S(1)}, f32[12,128]{1,0:T(8,128)S(1)}, u32[]{:S(2)}, u32[]{:S(2)}) collective-permute-start(f32[12,128]{1,0:T(8,128)S(1)} %get-tuple-element.77), channel_id=1, source_target_pairs={{0,32},{32,0},{64,96},{96,64},{128,160},{160,128},{192,224},{224,1... | collective-permute-start | bytes 18440 | tf_op jit(solution)/shard_map/ppermute | solution.py:716
  34.2 2.4 %collective-permute-start.8 = (f32[12,128]{1,0:T(8,128)S(1)}, f32[12,128]{1,0:T(8,128)S(1)}, u32[]{:S(2)}, u32[]{:S(2)}) collective-permute-start(f32[12,128]{1,0:T(8,128)S(1)} %get-tuple-element.74), channel_id=1, source_target_pairs={{0,31},{1,2},{2,1},{3,4},{4,3},{5,6},{6,5},{7,8},{8,7},{9,10},{10,... | collective-permute-start | bytes 18440 | tf_op jit(solution)/shard_map/ppermute | solution.py:716
  36.6 0.1 collective-permute-start.9
  36.7 0.8 %shard_map.74 = (f32[12,1024]{1,0:T(8,128)S(1)}, f32[48,128]{1,0:T(8,128)S(1)}) custom-call(f32[1,1,12,24,1024]{4,3,2,1,0:T(8,128)S(1)} %copy-done, s32[64,128]{1,0:T(8,128)S(1)} %get-tuple-element.50.conn_ref, f32[12,1024]{1,0:T(8,128)S(1)} %shard_map.72.row_ref, f32[48,128]{1,0:T(8,128)S(1)} %get-tuple-element.70.scale_ref, ...), custom_call_target="tpu_custom_call" | custom-call | flops 1000000000 | bytes 3906250 | tf_op jit(solution)/shard_map/pallas_call | solution.py:693
  37.5 0.0 collective-permute-done.10.rest_2_
  37.5 2.6 %collective-permute-done.8.rest_0_ = f32[12,128]{1,0:T(8,128)S(1)} collective-permute-done((f32[12,128]{1,0:T(8,128)S(1)}, f32[12,128]{1,0:T(8,128)S(1)}, u32[]{:S(2)}, u32[]{:S(2)}) %collective-permute-start.8) | collective-permute-done | bytes 6176 | tf_op jit(solution)/shard_map/ppermute | solution.py:716
  40.1 1.1 %shard_map.75 = (f32[96,128]{1,0:T(8,128)S(1)}, f32[24,128]{1,0:T(8,128)S(1)}, f32[24,128]{1,0:T(8,128)S(1)}, f32[24,128]{1,0:T(8,128)S(1)}, f32[24,128]{1,0:T(8,128)S(1)}) custom-call(f32[1,1,12,24,1024]{4,3,2,1,0:T(8,128)S(1)} %copy-done, s32[64,128]{1,0:T(8,128)S(1)} %get-tuple-element.50.conn_ref, f32[12,1024]{1,0:T(8,128)S(1)} %shard_map.72.row_ref, ...), custom_call_target="tpu_custom_call" | custom-call | tf_op jit(solution)/shard_map/pallas_call | solution.py:693
  41.2 2.5 %collective-permute-start.12 = (f32[24,128]{1,0:T(8,128)S(1)}, f32[24,128]{1,0:T(8,128)S(1)}, u32[]{:S(2)}, u32[]{:S(2)}) collective-permute-start(f32[24,128]{1,0:T(8,128)S(1)} %get-tuple-element.79), channel_id=1, source_target_pairs={{0,31},{1,2},{2,1},{3,4},{4,3},{5,6},{6,5},{7,8},{8,7},{9,10},{10,... | collective-permute-start | bytes 36872 | tf_op jit(solution)/shard_map/ppermute | solution.py:716
  43.7 1.2 %collective-permute-start.13 = (f32[24,128]{1,0:T(8,128)S(1)}, f32[24,128]{1,0:T(8,128)S(1)}, u32[]{:S(2)}, u32[]{:S(2)}) collective-permute-start(f32[24,128]{1,0:T(8,128)S(1)} %get-tuple-element.80), channel_id=1, source_target_pairs={{0,224},{32,64},{64,32},{96,128},{128,96},{160,192},{192,160},{224... | collective-permute-start | bytes 36872 | tf_op jit(solution)/shard_map/ppermute | solution.py:716
  44.9 0.0 collective-permute-start.14
  44.9 0.9 %collective-permute-start.15 = (f32[24,128]{1,0:T(8,128)S(1)}, f32[24,128]{1,0:T(8,128)S(1)}, u32[]{:S(2)}, u32[]{:S(2)}) collective-permute-start(f32[24,128]{1,0:T(8,128)S(1)} %get-tuple-element.82), channel_id=1, source_target_pairs={{0,32},{32,0},{64,96},{96,64},{128,160},{160,128},{192,224},{224,1... | collective-permute-start | bytes 36872 | tf_op jit(solution)/shard_map/ppermute | solution.py:716
  45.8 1.4 %collective-permute-done.12.rest_0_ = f32[24,128]{1,0:T(8,128)S(1)} collective-permute-done((f32[24,128]{1,0:T(8,128)S(1)}, f32[24,128]{1,0:T(8,128)S(1)}, u32[]{:S(2)}, u32[]{:S(2)}) %collective-permute-start.12) | collective-permute-done | bytes 12320 | tf_op jit(solution)/shard_map/ppermute | solution.py:716
  47.2 0.0 collective-permute-done.13.rest_1_
  47.2 0.5 collective-permute-done.14.rest_2_
  47.7 1.1 %shard_map.76 = (f32[1,128]{1,0:T(1,128)S(1)}, f32[48,128]{1,0:T(8,128)S(1)}, f32[48,128]{1,0:T(8,128)S(1)}, f32[12,128]{1,0:T(8,128)S(1)}, f32[12,128]{1,0:T(8,128)S(1)}) custom-call(f32[1,1,12,24,1024]{4,3,2,1,0:T(8,128)S(1)} %copy-done, s32[64,128]{1,0:T(8,128)S(1)} %get-tuple-element.50.conn_ref, f32[12,1024]{1,0:T(8,128)S(1)} %shard_map.72.row_ref, ...), custom_call_target="tpu_custom_call" | custom-call | tf_op jit(solution)/shard_map/pallas_call | solution.py:693
  48.9 0.7 collective-permute-start.16
  49.6 0.8 collective-permute-start.17
  50.4 4.4 %collective-permute-done.16.left_ref = f32[12,128]{1,0:T(8,128)S(1)} collective-permute-done((f32[12,128]{1,0:T(8,128)S(1)}, f32[12,128]{1,0:T(8,128)S(1)}, u32[]{:S(2)}, u32[]{:S(2)}) %collective-permute-start.16) | collective-permute-done | bytes 6176 | tf_op jit(solution)/shard_map/ppermute | solution.py:722
  54.8 0.0 collective-permute-done.17.below_ref
  54.8 0.8 shard_map.77
  55.5 8.0 %all-to-all-start = ((f32[256,1,128]{2,1,0:T(1,128)}), f32[256,1,128]{2,1,0:T(1,128)S(1)}, u32[]{:S(2)}, u32[]{:S(2)}) async-start(f32[256,1,128]{2,1,0:T(1,128)} %bitcast.2), calls=%async_computation | async-start | bytes 262144 | tf_op jit(solution)/shard_map/all_to_all | solution.py:836
  64.2 0.6 shard_map.79.joint_ref
  64.7 0.1 shard_map.78.velocity_ref
  64.9 11.8 %all-to-all-done = f32[256,1,128]{2,1,0:T(1,128)S(1)} async-done(((f32[256,1,128]{2,1,0:T(1,128)}), f32[256,1,128]{2,1,0:T(1,128)S(1)}, u32[]{:S(2)}, u32[]{:S(2)}) %all-to-all-start) | async-done | bytes 131104 | tf_op jit(solution)/shard_map/all_to_all | solution.py:836
  76.7 0.9 %shard_map.80 = (f32[24,128]{1,0:T(8,128)}, f32[96,128]{1,0:T(8,128)}) custom-call(f32[256,128]{1,0:T(8,128)S(1)} %bitcast.7, f32[1]{0:T(128)S(6)} %copy.14.step_ref, f32[48,128]{1,0:T(8,128)S(1)} %shard_map.78.velocity_ref, f32[12,1024]{1,0:T(8,128)S(1)} %get-tuple-element.91.base_ref, f32[12,1024]{1,0:T(8,128)S(1)} %shard_map.79.joint_ref, ...), custom_call_target="tpu_custom_call" | custom-call | tf_op jit(solution)/shard_map/pallas_call | solution.py:693
  (11 shorter events, 0.0 us)
Async XLA Ops:
  0.6 7.1 %copy-start.2 = (s32[1,1,4,256]{3,2,1,0:T(4,128)S(1)}, s32[1,1,4,256]{3,2,1,0:T(4,128)}, u32[]{:S(2)}) copy-start(s32[1,1,4,256]{3,2,1,0:T(4,128)} %lists_ref.1) | copy-start | bytes 12292
  0.6 0.8 copy-start.3
  7.9 12.2 %collective-permute-start = (f32[24,128]{1,0:T(8,128)S(1)}, f32[24,128]{1,0:T(8,128)S(1)}, u32[]{:S(2)}, u32[]{:S(2)}) collective-permute-start(f32[24,128]{1,0:T(8,128)S(1)} %get-tuple-element.58), channel_id=1, source_target_pairs={{0,31},{1,2},{2,1},{3,4},{4,3},{5,6},{6,5},{7,8},{8,7},{9,10},{10,... | collective-permute-start | bytes 36872 | tf_op jit(solution)/shard_map/ppermute | solution.py:716
  16.6 3.5 %collective-permute-start.1 = (f32[24,128]{1,0:T(8,128)S(1)}, f32[24,128]{1,0:T(8,128)S(1)}, u32[]{:S(2)}, u32[]{:S(2)}) collective-permute-start(f32[24,128]{1,0:T(8,128)S(1)} %get-tuple-element.59), channel_id=1, source_target_pairs={{0,224},{32,64},{64,32},{96,128},{128,96},{160,192},{192,160},{224... | collective-permute-start | bytes 36872 | tf_op jit(solution)/shard_map/ppermute | solution.py:716
  18.7 2.8 %collective-permute-start.2 = (f32[24,128]{1,0:T(8,128)S(1)}, f32[24,128]{1,0:T(8,128)S(1)}, u32[]{:S(2)}, u32[]{:S(2)}) collective-permute-start(f32[24,128]{1,0:T(8,128)S(1)} %get-tuple-element.60), channel_id=1, source_target_pairs={{0,1},{1,0},{2,3},{3,2},{4,5},{5,4},{6,7},{7,6},{8,9},{9,8},{10,11... | collective-permute-start | bytes 36872 | tf_op jit(solution)/shard_map/ppermute | solution.py:716
  18.7 2.8 %collective-permute-start.3 = (f32[24,128]{1,0:T(8,128)S(1)}, f32[24,128]{1,0:T(8,128)S(1)}, u32[]{:S(2)}, u32[]{:S(2)}) collective-permute-start(f32[24,128]{1,0:T(8,128)S(1)} %get-tuple-element.61), channel_id=1, source_target_pairs={{0,32},{32,0},{64,96},{96,64},{128,160},{160,128},{192,224},{224,1... | collective-permute-start | bytes 36872 | tf_op jit(solution)/shard_map/ppermute | solution.py:716
  19.7 1.8 %copy-start = (f32[1,1,12,24,1024]{4,3,2,1,0:T(8,128)S(1)}, f32[1,1,12,24,1024]{4,3,2,1,0:T(8,128)}, u32[]{:S(2)}) copy-start(f32[1,1,12,24,1024]{4,3,2,1,0:T(8,128)} %blocks_ref.13) | copy-start | bytes 3538948
  19.7 1.8 %copy-start.1 = (f32[1,1,3,1024]{3,1,2,0:T(1,128)S(1)}, f32[1,1,3,1024]{3,1,2,0:T(1,128)}, u32[]{:S(2)}) copy-start(f32[1,1,3,1024]{3,1,2,0:T(1,128)} %param.8) | copy-start | bytes 36868
  23.6 6.0 %collective-permute-start.4 = (f32[18,128]{1,0:T(8,128)S(1)}, f32[18,128]{1,0:T(8,128)S(1)}, u32[]{:S(2)}, u32[]{:S(2)}) collective-permute-start(f32[18,128]{1,0:T(8,128)S(1)} %get-tuple-element.66), channel_id=1, source_target_pairs={{0,31},{1,2},{2,1},{3,4},{4,3},{5,6},{6,5},{7,8},{8,7},{9,10},{10,... | collective-permute-start | bytes 27656 | tf_op jit(solution)/shard_map/ppermute | solution.py:716
  24.9 4.6 %collective-permute-start.5 = (f32[18,128]{1,0:T(8,128)S(1)}, f32[18,128]{1,0:T(8,128)S(1)}, u32[]{:S(2)}, u32[]{:S(2)}) collective-permute-start(f32[18,128]{1,0:T(8,128)S(1)} %get-tuple-element.67), channel_id=1, source_target_pairs={{0,224},{32,64},{64,32},{96,128},{128,96},{160,192},{192,160},{224... | collective-permute-start | bytes 27656 | tf_op jit(solution)/shard_map/ppermute | solution.py:716
  28.0 2.8 %collective-permute-start.6 = (f32[18,128]{1,0:T(8,128)S(1)}, f32[18,128]{1,0:T(8,128)S(1)}, u32[]{:S(2)}, u32[]{:S(2)}) collective-permute-start(f32[18,128]{1,0:T(8,128)S(1)} %get-tuple-element.68), channel_id=1, source_target_pairs={{0,1},{1,0},{2,3},{3,2},{4,5},{5,4},{6,7},{7,6},{8,9},{9,8},{10,11... | collective-permute-start | bytes 27656 | tf_op jit(solution)/shard_map/ppermute | solution.py:716
  28.0 2.8 %collective-permute-start.7 = (f32[18,128]{1,0:T(8,128)S(1)}, f32[18,128]{1,0:T(8,128)S(1)}, u32[]{:S(2)}, u32[]{:S(2)}) collective-permute-start(f32[18,128]{1,0:T(8,128)S(1)} %get-tuple-element.69), channel_id=1, source_target_pairs={{0,32},{32,0},{64,96},{96,64},{128,160},{160,128},{192,224},{224,1... | collective-permute-start | bytes 27656 | tf_op jit(solution)/shard_map/ppermute | solution.py:716
  32.0 5.5 %collective-permute-start.10 = (f32[12,128]{1,0:T(8,128)S(1)}, f32[12,128]{1,0:T(8,128)S(1)}, u32[]{:S(2)}, u32[]{:S(2)}) collective-permute-start(f32[12,128]{1,0:T(8,128)S(1)} %get-tuple-element.76), channel_id=1, source_target_pairs={{0,1},{1,0},{2,3},{3,2},{4,5},{5,4},{6,7},{7,6},{8,9},{9,8},{10,11... | collective-permute-start | bytes 18440 | tf_op jit(solution)/shard_map/ppermute | solution.py:716
  32.4 5.1 %collective-permute-start.11 = (f32[12,128]{1,0:T(8,128)S(1)}, f32[12,128]{1,0:T(8,128)S(1)}, u32[]{:S(2)}, u32[]{:S(2)}) collective-permute-start(f32[12,128]{1,0:T(8,128)S(1)} %get-tuple-element.77), channel_id=1, source_target_pairs={{0,32},{32,0},{64,96},{96,64},{128,160},{160,128},{192,224},{224,1... | collective-permute-start | bytes 18440 | tf_op jit(solution)/shard_map/ppermute | solution.py:716
  34.2 5.8 %collective-permute-start.8 = (f32[12,128]{1,0:T(8,128)S(1)}, f32[12,128]{1,0:T(8,128)S(1)}, u32[]{:S(2)}, u32[]{:S(2)}) collective-permute-start(f32[12,128]{1,0:T(8,128)S(1)} %get-tuple-element.74), channel_id=1, source_target_pairs={{0,31},{1,2},{2,1},{3,4},{4,3},{5,6},{6,5},{7,8},{8,7},{9,10},{10,... | collective-permute-start | bytes 18440 | tf_op jit(solution)/shard_map/ppermute | solution.py:716
  36.6 3.5 %collective-permute-start.9 = (f32[12,128]{1,0:T(8,128)S(1)}, f32[12,128]{1,0:T(8,128)S(1)}, u32[]{:S(2)}, u32[]{:S(2)}) collective-permute-start(f32[12,128]{1,0:T(8,128)S(1)} %get-tuple-element.75), channel_id=1, source_target_pairs={{0,224},{32,64},{64,32},{96,128},{128,96},{160,192},{192,160},{224... | collective-permute-start | bytes 18440 | tf_op jit(solution)/shard_map/ppermute | solution.py:716
  41.2 6.0 %collective-permute-start.12 = (f32[24,128]{1,0:T(8,128)S(1)}, f32[24,128]{1,0:T(8,128)S(1)}, u32[]{:S(2)}, u32[]{:S(2)}) collective-permute-start(f32[24,128]{1,0:T(8,128)S(1)} %get-tuple-element.79), channel_id=1, source_target_pairs={{0,31},{1,2},{2,1},{3,4},{4,3},{5,6},{6,5},{7,8},{8,7},{9,10},{10,... | collective-permute-start | bytes 36872 | tf_op jit(solution)/shard_map/ppermute | solution.py:716
  43.7 3.5 %collective-permute-start.13 = (f32[24,128]{1,0:T(8,128)S(1)}, f32[24,128]{1,0:T(8,128)S(1)}, u32[]{:S(2)}, u32[]{:S(2)}) collective-permute-start(f32[24,128]{1,0:T(8,128)S(1)} %get-tuple-element.80), channel_id=1, source_target_pairs={{0,224},{32,64},{64,32},{96,128},{128,96},{160,192},{192,160},{224... | collective-permute-start | bytes 36872 | tf_op jit(solution)/shard_map/ppermute | solution.py:716
  44.9 2.8 %collective-permute-start.14 = (f32[24,128]{1,0:T(8,128)S(1)}, f32[24,128]{1,0:T(8,128)S(1)}, u32[]{:S(2)}, u32[]{:S(2)}) collective-permute-start(f32[24,128]{1,0:T(8,128)S(1)} %get-tuple-element.81), channel_id=1, source_target_pairs={{0,1},{1,0},{2,3},{3,2},{4,5},{5,4},{6,7},{7,6},{8,9},{9,8},{10,11... | collective-permute-start | bytes 36872 | tf_op jit(solution)/shard_map/ppermute | solution.py:716
  44.9 2.8 %collective-permute-start.15 = (f32[24,128]{1,0:T(8,128)S(1)}, f32[24,128]{1,0:T(8,128)S(1)}, u32[]{:S(2)}, u32[]{:S(2)}) collective-permute-start(f32[24,128]{1,0:T(8,128)S(1)} %get-tuple-element.82), channel_id=1, source_target_pairs={{0,32},{32,0},{64,96},{96,64},{128,160},{160,128},{192,224},{224,1... | collective-permute-start | bytes 36872 | tf_op jit(solution)/shard_map/ppermute | solution.py:716
  48.9 5.9 %collective-permute-start.16 = (f32[12,128]{1,0:T(8,128)S(1)}, f32[12,128]{1,0:T(8,128)S(1)}, u32[]{:S(2)}, u32[]{:S(2)}) collective-permute-start(f32[12,128]{1,0:T(8,128)S(1)} %get-tuple-element.85), channel_id=1, source_target_pairs={{0,1},{1,2},{2,3},{3,4},{4,5},{5,6},{6,7},{7,8},{8,9},{9,10},{10,1... | collective-permute-start | bytes 18440 | tf_op jit(solution)/shard_map/ppermute | solution.py:722
  49.6 5.2 %collective-permute-start.17 = (f32[12,128]{1,0:T(8,128)S(1)}, f32[12,128]{1,0:T(8,128)S(1)}, u32[]{:S(2)}, u32[]{:S(2)}) collective-permute-start(f32[12,128]{1,0:T(8,128)S(1)} %get-tuple-element.86), channel_id=1, source_target_pairs={{0,32},{32,64},{64,96},{96,128},{128,160},{160,192},{192,224},{224... | collective-permute-start | bytes 18440 | tf_op jit(solution)/shard_map/ppermute | solution.py:722
  55.5 21.2 %all-to-all-start = ((f32[256,1,128]{2,1,0:T(1,128)}), f32[256,1,128]{2,1,0:T(1,128)S(1)}, u32[]{:S(2)}, u32[]{:S(2)}) async-start(f32[256,1,128]{2,1,0:T(1,128)} %bitcast.2), calls=%async_computation | async-start | bytes 262144 | tf_op jit(solution)/shard_map/all_to_all | solution.py:836

commit v7 on v6

--- a/solution.py
+++ b/solution.py
@@ -341,14 +341,30 @@
         out_ref[NODE_ROWS * channel : NODE_ROWS * (channel + 1), :] = out
 
 
-def row_maxima(blocks_ref, picked, at, max_ref):
+def fold_rows(rows, merge, ref, first, at):
+    sub = tile_iota(0)
+
+    def fold(low, high, step):
+        here = (sub & step) == 0
+        return merge(
+            jnp.where(here, low, high), pick(jnp.where(here, high, low), sub ^ step, 0)
+        )
+
+    pairs = [fold(rows[r], rows[r + 4], 4) for r in (0, 2, 1, 3)]
+    fours = [fold(pairs[0], pairs[1], 2), fold(pairs[2], pairs[3], 2)]
+    ref[first : first + 8, at] = fold(fours[0], fours[1], 1)
+    rest = fold(fold(rows[8], rows[9], 4), fold(rows[10], rows[11], 4), 2)
+    rest = merge(rest, pick(rest, sub ^ 1, 0))
+    for r, place in enumerate((0, 4, 2, 6)):
+        ref[first + 8 + r : first + 9 + r, at] = rest[place : place + 1, :]
+
+
+def row_maxima(blocks_ref, scales, at, max_ref):
+    whole = []
     for r in range(STRAINS):
-        sized = [jnp.abs(blocks_ref[0, 0, r, 8 * c : 8 * c + 8, at]) for c in range(3)]
-        for k, scales in enumerate(picked):
-            whole = sized[0] * scales[0]
-            for c in range(1, 3):
-                whole = jnp.maximum(whole, sized[c] * scales[c])
-            max_ref[STRAINS * k + r : STRAINS * k + r + 1, at] = jnp.max(whole, axis=0, keepdims=True)
+        sized = [jnp.abs(blocks_ref[0, 0, r, 8 * c : 8 * c + 8, at]) * scales[c] for c in range(3)]
+        whole.append(jnp.maximum(jnp.maximum(sized[0], sized[1]), sized[2]))
+    fold_rows(whole, jnp.maximum, max_ref, 0, at)
 
 
 def column_maxima(blocks_ref, row_ref, term_ref, first_channel):
@@ -365,18 +381,15 @@
             term_ref[base : base + 8, :] = best[c]
 
 
-def apply_blocks(blocks_ref, table_ref, sets, conn_ref, strain_ref):
+def apply_blocks(blocks_ref, table_ref, conn_ref, strain_ref):
     for chunk in range(CHUNKS):
-        values = node_picks(table_ref, 3 * sets, conn_ref, chunk)
+        values = node_picks(table_ref, 3, conn_ref, chunk)
         at = slice(chunk * LANES, (chunk + 1) * LANES)
+        totals = []
         for r in range(STRAINS):
-            parts = [blocks_ref[0, 0, r, 8 * c : 8 * c + 8, at] for c in range(3)]
-            for k in range(sets):
-                mine = values[3 * k : 3 * k + 3]
-                total = parts[0] * mine[0] + parts[1] * mine[1] + parts[2] * mine[2]
-                strain_ref[STRAINS * k + r : STRAINS * k + r + 1, at] = jnp.sum(
-                    total, axis=0, keepdims=True
-                )
+            parts = [blocks_ref[0, 0, r, 8 * c : 8 * c + 8, at] * values[c] for c in range(3)]
+            totals.append(parts[0] + parts[1] + parts[2])
+        fold_rows(totals, jnp.add, strain_ref, 0, at)
 
 
 def apply_transpose(blocks_ref, strain_ref, sets, term_ref):
@@ -477,7 +490,7 @@
         at = slice(chunk * LANES, (chunk + 1) * LANES)
         ids = ids_ref[0, 0, :, at]
         scale = jnp.where(ids < 1536, 1.0, jnp.where(ids < 1792, below, above))
-        row_maxima(blocks_ref, [[scale] * 3], at, peaks)
+        row_maxima(blocks_ref, [scale] * 3, at, peaks)
     row_out[...] = 1.0 / jnp.sqrt(peaks[...])
     column_maxima(blocks_ref, None, term, 0)
     column_maxima(blocks_ref, row_out, term, 3)
@@ -512,7 +525,7 @@
         scale_out[NODE_ROWS * c : NODE_ROWS * (c + 1), :] = second
     for chunk in range(CHUNKS):
         at = slice(chunk * LANES, (chunk + 1) * LANES)
-        row_maxima(blocks_ref, [node_picks(merged, 3, conn_ref, chunk)], at, peaks)
+        row_maxima(blocks_ref, node_picks(merged, 3, conn_ref, chunk), at, peaks)
     row_out[...] = row_ref[...] / jnp.sqrt(row_ref[...] * peaks[...])
     column_maxima(blocks_ref, row_out, term, 0)
     scatter_maxima(term, 3, plan, items, totals, merged)
@@ -536,7 +549,7 @@
 def row_kernel(blocks_ref, conn_ref, row_ref, scale_ref, row_out, peaks):
     for chunk in range(CHUNKS):
         at = slice(chunk * LANES, (chunk + 1) * LANES)
-        row_maxima(blocks_ref, [node_picks(scale_ref, 3, conn_ref, chunk)], at, peaks)
+        row_maxima(blocks_ref, node_picks(scale_ref, 3, conn_ref, chunk), at, peaks)
     row_out[...] = row_ref[...] / jnp.sqrt(row_ref[...] * peaks[...])
 
 
@@ -553,7 +566,7 @@
             base = NODE_ROWS * c + 8 + 2 * side
             table[base : base + 2, :] = arrived[side][12 + 2 * c : 14 + 2 * c]
     table[...] = scale * (scale * table[...])
-    apply_blocks(blocks_ref, table, 1, conn_ref, strain)
+    apply_blocks(blocks_ref, table, conn_ref, strain)
     row = row_ref[...]
     image = row * strain[...]
     image_out[...] = image
@@ -580,7 +593,7 @@
     unpack(part_ref, 3, arrived, jnp.add, table)
     scale = scale_ref[...]
     table[...] = scale * table[...]
-    apply_blocks(blocks_ref, table, 1, conn_ref, strain)
+    apply_blocks(blocks_ref, table, conn_ref, strain)
     row = row_ref[...]
     strain[...] = row * (row * strain[...])
     apply_transpose(blocks_ref, strain, 1, term)
@@ -592,7 +605,7 @@
 
 def joint_kernel(blocks_ref, conn_ref, row_ref, scale_ref, joint_ref, line_ref, image_out, table, strain):
     table[...] = scale_ref[...] * joint_ref[...]
-    apply_blocks(blocks_ref, table, 1, conn_ref, strain)
+    apply_blocks(blocks_ref, table, conn_ref, strain)
     image_out[...] = row_ref[...] * strain[...]
 
 
@@ -614,7 +627,7 @@
     joint_out[...] = table[48:96, :]
     scale = scale_ref[...]
     table[0:48, :] = scale * table[0:48, :]
-    apply_blocks(blocks_ref, table, 1, conn_ref, strain)
+    apply_blocks(blocks_ref, table, conn_ref, strain)
     row = row_ref[...]
     strain[...] = row * (row * strain[...])
     apply_transpose(blocks_ref, strain, 1, term)

time: 78 us -> 77.9 us (level)
  no operation moved by 1% of the time
where the time goes in v7:
time: 77.9 us; the launch traced here: 77.7 us
  starting transfers between devices  35 us (45%)
  waiting for transfers between devices  24.4 us (31%)
  Pallas kernels  16 us (21%)
  between operations  1.58 us (2%)
    ppermute x16, starting transfers between devices, exchange(): lax.ppermute(packet, axis, swap_pairs(axis, odd))  25.4 us
    pallas_call x13, Pallas kernels, call(): pl.pallas_call(body, out_shape=[jax.ShapeDtypeStruct(shape, kind) for sha...  16 us
    all_to_all x1, waiting for transfers between devices, per_device(): sums = lax.all_to_all(sums, AXES, 0, 0, tiled=True)  11.9 us
    ppermute x16, waiting for transfers between devices, exchange(): lax.ppermute(packet, axis, swap_pairs(axis, odd))  8.13 us
    all_to_all x1, starting transfers between devices, per_device(): sums = lax.all_to_all(sums, AXES, 0, 0, tiled=True)  8.02 us
    ppermute x2, waiting for transfers between devices, shift_up(): lax.ppermute(packet, axis, [(i, (i + 1) % count) for i in range(count)])  4.4 us
  transfers between devices with their start and end apart: 19, of which 8 were waited for; matrix products, arithmetic and copies ran while one was open for 0% of the time, Pallas kernels for 3%

profile of v7, /device:TPU:1, one launch (start us, length us, event | category | flops | bytes accessed | tf_op | source)
XLA Modules:
  0.0 77.7 jit_solution(7087641034914944103)
XLA Ops:
  0.6 0.8 copy-done.3
  1.4 6.3 %shard_map.68 = (s32[40,128]{1,0:T(8,128)S(1)}, s32[8,128]{1,0:T(8,128)S(1)}, s32[16,128]{1,0:T(8,128)S(1)}, s32[8,128]{1,0:T(8,128)S(1)}, s32[16,128]{1,0:T(8,1...) custom-call(f32[1,1,12,24,1024]{4,3,2,1,0:T(8,128)} %blocks_ref.13, s32[1,1,8,1024]{3,2,1,0:T(8,128)S(1)} %copy-done.3), custom_call_target="tpu_custom_call" | custom-call | flops 12000000000 | bytes 46875000 | tf_op jit(solution)/shard_map/pallas_call | solution.py:706
  7.7 0.1 shard_map.69
  7.9 8.7 %collective-permute-start = (f32[24,128]{1,0:T(8,128)S(1)}, f32[24,128]{1,0:T(8,128)S(1)}, u32[]{:S(2)}, u32[]{:S(2)}) collective-permute-start(f32[24,128]{1,0:T(8,128)S(1)} %get-tuple-element.58), channel_id=1, source_target_pairs={{0,31},{1,2},{2,1},{3,4},{4,3},{5,6},{6,5},{7,8},{8,7},{9,10},{10,... | collective-permute-start | bytes 36872 | tf_op jit(solution)/shard_map/ppermute | solution.py:729
  16.5 2.1 %collective-permute-start.1 = (f32[24,128]{1,0:T(8,128)S(1)}, f32[24,128]{1,0:T(8,128)S(1)}, u32[]{:S(2)}, u32[]{:S(2)}) collective-permute-start(f32[24,128]{1,0:T(8,128)S(1)} %get-tuple-element.59), channel_id=1, source_target_pairs={{0,224},{32,64},{64,32},{96,128},{128,96},{160,192},{192,160},{224... | collective-permute-start | bytes 36872 | tf_op jit(solution)/shard_map/ppermute | solution.py:729
  18.7 0.0 collective-permute-start.2
  18.7 1.0 %collective-permute-start.3 = (f32[24,128]{1,0:T(8,128)S(1)}, f32[24,128]{1,0:T(8,128)S(1)}, u32[]{:S(2)}, u32[]{:S(2)}) collective-permute-start(f32[24,128]{1,0:T(8,128)S(1)} %get-tuple-element.61), channel_id=1, source_target_pairs={{0,32},{32,0},{64,96},{96,64},{128,160},{160,128},{192,224},{224,1... | collective-permute-start | bytes 36872 | tf_op jit(solution)/shard_map/ppermute | solution.py:729
  19.7 0.4 shard_map.70
  20.1 0.0 collective-permute-done.rest_5_
  20.1 0.0 collective-permute-done.1.rest_6_
  20.1 1.4 %collective-permute-done.2.rest_7_ = f32[24,128]{1,0:T(8,128)S(1)} collective-permute-done((f32[24,128]{1,0:T(8,128)S(1)}, f32[24,128]{1,0:T(8,128)S(1)}, u32[]{:S(2)}, u32[]{:S(2)}) %collective-permute-start.2) | collective-permute-done | bytes 12320 | tf_op jit(solution)/shard_map/ppermute | solution.py:729
  21.4 0.0 collective-permute-done.3.rest_8_
  21.4 2.1 %shard_map.71 = (f32[12,1024]{1,0:T(8,128)S(1)}, f32[48,128]{1,0:T(8,128)S(1)}, f32[48,128]{1,0:T(8,128)S(1)}, f32[24,128]{1,0:T(8,128)S(1)}, f32[18,128]{1,0:T(...) custom-call(f32[1,1,12,24,1024]{4,3,2,1,0:T(8,128)S(1)} %copy-done, ...), custom_call_target="tpu_custom_call" | custom-call | tf_op jit(solution)/shard_map/pallas_call | solution.py:706
  23.6 1.3 %collective-permute-start.4 = (f32[18,128]{1,0:T(8,128)S(1)}, f32[18,128]{1,0:T(8,128)S(1)}, u32[]{:S(2)}, u32[]{:S(2)}) collective-permute-start(f32[18,128]{1,0:T(8,128)S(1)} %get-tuple-element.66), channel_id=1, source_target_pairs={{0,31},{1,2},{2,1},{3,4},{4,3},{5,6},{6,5},{7,8},{8,7},{9,10},{10,... | collective-permute-start | bytes 27656 | tf_op jit(solution)/shard_map/ppermute | solution.py:729
  24.9 3.1 %collective-permute-start.5 = (f32[18,128]{1,0:T(8,128)S(1)}, f32[18,128]{1,0:T(8,128)S(1)}, u32[]{:S(2)}, u32[]{:S(2)}) collective-permute-start(f32[18,128]{1,0:T(8,128)S(1)} %get-tuple-element.67), channel_id=1, source_target_pairs={{0,224},{32,64},{64,32},{96,128},{128,96},{160,192},{192,160},{224... | collective-permute-start | bytes 27656 | tf_op jit(solution)/shard_map/ppermute | solution.py:729
  27.9 0.0 collective-permute-start.6
  27.9 0.0 collective-permute-start.7
  27.9 0.6 shard_map.72.row_ref
  28.5 1.0 %collective-permute-done.4.rest_0_ = f32[18,128]{1,0:T(8,128)S(1)} collective-permute-done((f32[18,128]{1,0:T(8,128)S(1)}, f32[18,128]{1,0:T(8,128)S(1)}, u32[]{:S(2)}, u32[]{:S(2)}) %collective-permute-start.4) | collective-permute-done | bytes 9248 | tf_op jit(solution)/shard_map/ppermute | solution.py:729
  29.5 0.0 collective-permute-done.5.rest_1_
  29.5 1.3 %collective-permute-done.6.rest_2_ = f32[18,128]{1,0:T(8,128)S(1)} collective-permute-done((f32[18,128]{1,0:T(8,128)S(1)}, f32[18,128]{1,0:T(8,128)S(1)}, u32[]{:S(2)}, u32[]{:S(2)}) %collective-permute-start.6) | collective-permute-done | bytes 9248 | tf_op jit(solution)/shard_map/ppermute | solution.py:729
  30.8 0.0 collective-permute-done.7.rest_3_
  30.8 1.1 %shard_map.73 = (f32[48,128]{1,0:T(8,128)S(1)}, f32[12,1024]{1,0:T(8,128)S(1)}, f32[48,128]{1,0:T(8,128)S(1)}, f32[12,128]{1,0:T(8,128)S(1)}, f32[12,128]{1,0:T(...) custom-call(f32[1,1,12,24,1024]{4,3,2,1,0:T(8,128)S(1)} %copy-done, s32[64,128]{1,0:T(8,128)S(1)} %get-tuple-element.50.conn_ref, ...), custom_call_target="tpu_custom_call" | custom-call | tf_op jit(solution)/shard_map/pallas_call | solution.py:706
  31.9 0.4 collective-permute-start.10
  32.3 1.8 %collective-permute-start.11 = (f32[12,128]{1,0:T(8,128)S(1)}, f32[12,128]{1,0:T(8,128)S(1)}, u32[]{:S(2)}, u32[]{:S(2)}) collective-permute-start(f32[12,128]{1,0:T(8,128)S(1)} %get-tuple-element.77), channel_id=1, source_target_pairs={{0,32},{32,0},{64,96},{96,64},{128,160},{160,128},{192,224},{224,1... | collective-permute-start | bytes 18440 | tf_op jit(solution)/shard_map/ppermute | solution.py:729
  34.1 2.4 %collective-permute-start.8 = (f32[12,128]{1,0:T(8,128)S(1)}, f32[12,128]{1,0:T(8,128)S(1)}, u32[]{:S(2)}, u32[]{:S(2)}) collective-permute-start(f32[12,128]{1,0:T(8,128)S(1)} %get-tuple-element.74), channel_id=1, source_target_pairs={{0,31},{1,2},{2,1},{3,4},{4,3},{5,6},{6,5},{7,8},{8,7},{9,10},{10,... | collective-permute-start | bytes 18440 | tf_op jit(solution)/shard_map/ppermute | solution.py:729
  36.5 0.1 collective-permute-start.9
  36.6 0.8 %shard_map.74 = (f32[12,1024]{1,0:T(8,128)S(1)}, f32[48,128]{1,0:T(8,128)S(1)}) custom-call(f32[1,1,12,24,1024]{4,3,2,1,0:T(8,128)S(1)} %copy-done, s32[64,128]{1,0:T(8,128)S(1)} %get-tuple-element.50.conn_ref, f32[12,1024]{1,0:T(8,128)S(1)} %shard_map.72.row_ref, f32[48,128]{1,0:T(8,128)S(1)} %get-tuple-element.70.scale_ref, ...), custom_call_target="tpu_custom_call" | custom-call | flops 1000000000 | bytes 3906250 | tf_op jit(solution)/shard_map/pallas_call | solution.py:706
  37.4 0.0 collective-permute-done.11.rest_3_
  37.4 2.6 %collective-permute-done.8.rest_0_ = f32[12,128]{1,0:T(8,128)S(1)} collective-permute-done((f32[12,128]{1,0:T(8,128)S(1)}, f32[12,128]{1,0:T(8,128)S(1)}, u32[]{:S(2)}, u32[]{:S(2)}) %collective-permute-start.8) | collective-permute-done | bytes 6176 | tf_op jit(solution)/shard_map/ppermute | solution.py:729
  40.0 0.0 collective-permute-done.9.rest_1_
  40.0 1.1 %shard_map.75 = (f32[96,128]{1,0:T(8,128)S(1)}, f32[24,128]{1,0:T(8,128)S(1)}, f32[24,128]{1,0:T(8,128)S(1)}, f32[24,128]{1,0:T(8,128)S(1)}, f32[24,128]{1,0:T(8,128)S(1)}) custom-call(f32[1,1,12,24,1024]{4,3,2,1,0:T(8,128)S(1)} %copy-done, s32[64,128]{1,0:T(8,128)S(1)} %get-tuple-element.50.conn_ref, f32[12,1024]{1,0:T(8,128)S(1)} %shard_map.72.row_ref, ...), custom_call_target="tpu_custom_call" | custom-call | tf_op jit(solution)/shard_map/pallas_call | solution.py:706
  41.1 2.5 %collective-permute-start.12 = (f32[24,128]{1,0:T(8,128)S(1)}, f32[24,128]{1,0:T(8,128)S(1)}, u32[]{:S(2)}, u32[]{:S(2)}) collective-permute-start(f32[24,128]{1,0:T(8,128)S(1)} %get-tuple-element.79), channel_id=1, source_target_pairs={{0,31},{1,2},{2,1},{3,4},{4,3},{5,6},{6,5},{7,8},{8,7},{9,10},{10,... | collective-permute-start | bytes 36872 | tf_op jit(solution)/shard_map/ppermute | solution.py:729
  43.5 1.2 %collective-permute-start.13 = (f32[24,128]{1,0:T(8,128)S(1)}, f32[24,128]{1,0:T(8,128)S(1)}, u32[]{:S(2)}, u32[]{:S(2)}) collective-permute-start(f32[24,128]{1,0:T(8,128)S(1)} %get-tuple-element.80), channel_id=1, source_target_pairs={{0,224},{32,64},{64,32},{96,128},{128,96},{160,192},{192,160},{224... | collective-permute-start | bytes 36872 | tf_op jit(solution)/shard_map/ppermute | solution.py:729
  44.8 0.9 %collective-permute-start.15 = (f32[24,128]{1,0:T(8,128)S(1)}, f32[24,128]{1,0:T(8,128)S(1)}, u32[]{:S(2)}, u32[]{:S(2)}) collective-permute-start(f32[24,128]{1,0:T(8,128)S(1)} %get-tuple-element.82), channel_id=1, source_target_pairs={{0,32},{32,0},{64,96},{96,64},{128,160},{160,128},{192,224},{224,1... | collective-permute-start | bytes 36872 | tf_op jit(solution)/shard_map/ppermute | solution.py:729
  45.7 1.4 %collective-permute-done.12.rest_0_ = f32[24,128]{1,0:T(8,128)S(1)} collective-permute-done((f32[24,128]{1,0:T(8,128)S(1)}, f32[24,128]{1,0:T(8,128)S(1)}, u32[]{:S(2)}, u32[]{:S(2)}) %collective-permute-start.12) | collective-permute-done | bytes 12320 | tf_op jit(solution)/shard_map/ppermute | solution.py:729
  47.0 0.5 collective-permute-done.14.rest_2_
  47.6 0.0 collective-permute-done.15.rest_3_
  47.6 1.1 %shard_map.76 = (f32[1,128]{1,0:T(1,128)S(1)}, f32[48,128]{1,0:T(8,128)S(1)}, f32[48,128]{1,0:T(8,128)S(1)}, f32[12,128]{1,0:T(8,128)S(1)}, f32[12,128]{1,0:T(8,128)S(1)}) custom-call(f32[1,1,12,24,1024]{4,3,2,1,0:T(8,128)S(1)} %copy-done, s32[64,128]{1,0:T(8,128)S(1)} %get-tuple-element.50.conn_ref, f32[12,1024]{1,0:T(8,128)S(1)} %shard_map.72.row_ref, ...), custom_call_target="tpu_custom_call" | custom-call | tf_op jit(solution)/shard_map/pallas_call | solution.py:706
  48.7 0.7 collective-permute-start.16
  49.5 0.8 collective-permute-start.17
  50.2 4.4 %collective-permute-done.16.left_ref = f32[12,128]{1,0:T(8,128)S(1)} collective-permute-done((f32[12,128]{1,0:T(8,128)S(1)}, f32[12,128]{1,0:T(8,128)S(1)}, u32[]{:S(2)}, u32[]{:S(2)}) %collective-permute-start.16) | collective-permute-done | bytes 6176 | tf_op jit(solution)/shard_map/ppermute | solution.py:735
  54.6 0.8 shard_map.77
  55.4 8.0 %all-to-all-start = ((f32[256,1,128]{2,1,0:T(1,128)}), f32[256,1,128]{2,1,0:T(1,128)S(1)}, u32[]{:S(2)}, u32[]{:S(2)}) async-start(f32[256,1,128]{2,1,0:T(1,128)} %bitcast.2), calls=%async_computation | async-start | bytes 262144 | tf_op jit(solution)/shard_map/all_to_all | solution.py:849
  64.1 0.5 shard_map.79.joint_ref
  64.6 0.1 shard_map.78.velocity_ref
  64.7 11.9 %all-to-all-done = f32[256,1,128]{2,1,0:T(1,128)S(1)} async-done(((f32[256,1,128]{2,1,0:T(1,128)}), f32[256,1,128]{2,1,0:T(1,128)S(1)}, u32[]{:S(2)}, u32[]{:S(2)}) %all-to-all-start) | async-done | bytes 131104 | tf_op jit(solution)/shard_map/all_to_all | solution.py:849
  76.6 0.9 %shard_map.80 = (f32[24,128]{1,0:T(8,128)}, f32[96,128]{1,0:T(8,128)}) custom-call(f32[256,128]{1,0:T(8,128)S(1)} %bitcast.7, f32[1]{0:T(128)S(6)} %copy.14.step_ref, f32[48,128]{1,0:T(8,128)S(1)} %shard_map.78.velocity_ref, f32[12,1024]{1,0:T(8,128)S(1)} %get-tuple-element.91.base_ref, f32[12,1024]{1,0:T(8,128)S(1)} %shard_map.79.joint_ref, ...), custom_call_target="tpu_custom_call" | custom-call | tf_op jit(solution)/shard_map/pallas_call | solution.py:706
  (11 shorter events, 0.0 us)
Async XLA Ops:
  0.6 7.1 %copy-start.2 = (s32[1,1,4,256]{3,2,1,0:T(4,128)S(1)}, s32[1,1,4,256]{3,2,1,0:T(4,128)}, u32[]{:S(2)}) copy-start(s32[1,1,4,256]{3,2,1,0:T(4,128)} %lists_ref.1) | copy-start | bytes 12292
  0.6 0.8 copy-start.3
  7.9 12.2 %collective-permute-start = (f32[24,128]{1,0:T(8,128)S(1)}, f32[24,128]{1,0:T(8,128)S(1)}, u32[]{:S(2)}, u32[]{:S(2)}) collective-permute-start(f32[24,128]{1,0:T(8,128)S(1)} %get-tuple-element.58), channel_id=1, source_target_pairs={{0,31},{1,2},{2,1},{3,4},{4,3},{5,6},{6,5},{7,8},{8,7},{9,10},{10,... | collective-permute-start | bytes 36872 | tf_op jit(solution)/shard_map/ppermute | solution.py:729
  16.5 3.5 %collective-permute-start.1 = (f32[24,128]{1,0:T(8,128)S(1)}, f32[24,128]{1,0:T(8,128)S(1)}, u32[]{:S(2)}, u32[]{:S(2)}) collective-permute-start(f32[24,128]{1,0:T(8,128)S(1)} %get-tuple-element.59), channel_id=1, source_target_pairs={{0,224},{32,64},{64,32},{96,128},{128,96},{160,192},{192,160},{224... | collective-permute-start | bytes 36872 | tf_op jit(solution)/shard_map/ppermute | solution.py:729
  18.7 2.8 %collective-permute-start.2 = (f32[24,128]{1,0:T(8,128)S(1)}, f32[24,128]{1,0:T(8,128)S(1)}, u32[]{:S(2)}, u32[]{:S(2)}) collective-permute-start(f32[24,128]{1,0:T(8,128)S(1)} %get-tuple-element.60), channel_id=1, source_target_pairs={{0,1},{1,0},{2,3},{3,2},{4,5},{5,4},{6,7},{7,6},{8,9},{9,8},{10,11... | collective-permute-start | bytes 36872 | tf_op jit(solution)/shard_map/ppermute | solution.py:729
  18.7 2.8 %collective-permute-start.3 = (f32[24,128]{1,0:T(8,128)S(1)}, f32[24,128]{1,0:T(8,128)S(1)}, u32[]{:S(2)}, u32[]{:S(2)}) collective-permute-start(f32[24,128]{1,0:T(8,128)S(1)} %get-tuple-element.61), channel_id=1, source_target_pairs={{0,32},{32,0},{64,96},{96,64},{128,160},{160,128},{192,224},{224,1... | collective-permute-start | bytes 36872 | tf_op jit(solution)/shard_map/ppermute | solution.py:729
  19.7 1.8 %copy-start = (f32[1,1,12,24,1024]{4,3,2,1,0:T(8,128)S(1)}, f32[1,1,12,24,1024]{4,3,2,1,0:T(8,128)}, u32[]{:S(2)}) copy-start(f32[1,1,12,24,1024]{4,3,2,1,0:T(8,128)} %blocks_ref.13) | copy-start | bytes 3538948
  19.7 1.8 %copy-start.1 = (f32[1,1,3,1024]{3,1,2,0:T(1,128)S(1)}, f32[1,1,3,1024]{3,1,2,0:T(1,128)}, u32[]{:S(2)}) copy-start(f32[1,1,3,1024]{3,1,2,0:T(1,128)} %param.8) | copy-start | bytes 36868
  23.6 6.0 %collective-permute-start.4 = (f32[18,128]{1,0:T(8,128)S(1)}, f32[18,128]{1,0:T(8,128)S(1)}, u32[]{:S(2)}, u32[]{:S(2)}) collective-permute-start(f32[18,128]{1,0:T(8,128)S(1)} %get-tuple-element.66), channel_id=1, source_target_pairs={{0,31},{1,2},{2,1},{3,4},{4,3},{5,6},{6,5},{7,8},{8,7},{9,10},{10,... | collective-permute-start | bytes 27656 | tf_op jit(solution)/shard_map/ppermute | solution.py:729
  24.9 4.6 %collective-permute-start.5 = (f32[18,128]{1,0:T(8,128)S(1)}, f32[18,128]{1,0:T(8,128)S(1)}, u32[]{:S(2)}, u32[]{:S(2)}) collective-permute-start(f32[18,128]{1,0:T(8,128)S(1)} %get-tuple-element.67), channel_id=1, source_target_pairs={{0,224},{32,64},{64,32},{96,128},{128,96},{160,192},{192,160},{224... | collective-permute-start | bytes 27656 | tf_op jit(solution)/shard_map/ppermute | solution.py:729
  27.9 2.8 %collective-permute-start.6 = (f32[18,128]{1,0:T(8,128)S(1)}, f32[18,128]{1,0:T(8,128)S(1)}, u32[]{:S(2)}, u32[]{:S(2)}) collective-permute-start(f32[18,128]{1,0:T(8,128)S(1)} %get-tuple-element.68), channel_id=1, source_target_pairs={{0,1},{1,0},{2,3},{3,2},{4,5},{5,4},{6,7},{7,6},{8,9},{9,8},{10,11... | collective-permute-start | bytes 27656 | tf_op jit(solution)/shard_map/ppermute | solution.py:729
  27.9 2.8 %collective-permute-start.7 = (f32[18,128]{1,0:T(8,128)S(1)}, f32[18,128]{1,0:T(8,128)S(1)}, u32[]{:S(2)}, u32[]{:S(2)}) collective-permute-start(f32[18,128]{1,0:T(8,128)S(1)} %get-tuple-element.69), channel_id=1, source_target_pairs={{0,32},{32,0},{64,96},{96,64},{128,160},{160,128},{192,224},{224,1... | collective-permute-start | bytes 27656 | tf_op jit(solution)/shard_map/ppermute | solution.py:729
  31.9 5.5 %collective-permute-start.10 = (f32[12,128]{1,0:T(8,128)S(1)}, f32[12,128]{1,0:T(8,128)S(1)}, u32[]{:S(2)}, u32[]{:S(2)}) collective-permute-start(f32[12,128]{1,0:T(8,128)S(1)} %get-tuple-element.76), channel_id=1, source_target_pairs={{0,1},{1,0},{2,3},{3,2},{4,5},{5,4},{6,7},{7,6},{8,9},{9,8},{10,11... | collective-permute-start | bytes 18440 | tf_op jit(solution)/shard_map/ppermute | solution.py:729
  32.3 5.1 %collective-permute-start.11 = (f32[12,128]{1,0:T(8,128)S(1)}, f32[12,128]{1,0:T(8,128)S(1)}, u32[]{:S(2)}, u32[]{:S(2)}) collective-permute-start(f32[12,128]{1,0:T(8,128)S(1)} %get-tuple-element.77), channel_id=1, source_target_pairs={{0,32},{32,0},{64,96},{96,64},{128,160},{160,128},{192,224},{224,1... | collective-permute-start | bytes 18440 | tf_op jit(solution)/shard_map/ppermute | solution.py:729
  34.1 5.8 %collective-permute-start.8 = (f32[12,128]{1,0:T(8,128)S(1)}, f32[12,128]{1,0:T(8,128)S(1)}, u32[]{:S(2)}, u32[]{:S(2)}) collective-permute-start(f32[12,128]{1,0:T(8,128)S(1)} %get-tuple-element.74), channel_id=1, source_target_pairs={{0,31},{1,2},{2,1},{3,4},{4,3},{5,6},{6,5},{7,8},{8,7},{9,10},{10,... | collective-permute-start | bytes 18440 | tf_op jit(solution)/shard_map/ppermute | solution.py:729
  36.5 3.5 %collective-permute-start.9 = (f32[12,128]{1,0:T(8,128)S(1)}, f32[12,128]{1,0:T(8,128)S(1)}, u32[]{:S(2)}, u32[]{:S(2)}) collective-permute-start(f32[12,128]{1,0:T(8,128)S(1)} %get-tuple-element.75), channel_id=1, source_target_pairs={{0,224},{32,64},{64,32},{96,128},{128,96},{160,192},{192,160},{224... | collective-permute-start | bytes 18440 | tf_op jit(solution)/shard_map/ppermute | solution.py:729
  41.1 6.0 %collective-permute-start.12 = (f32[24,128]{1,0:T(8,128)S(1)}, f32[24,128]{1,0:T(8,128)S(1)}, u32[]{:S(2)}, u32[]{:S(2)}) collective-permute-start(f32[24,128]{1,0:T(8,128)S(1)} %get-tuple-element.79), channel_id=1, source_target_pairs={{0,31},{1,2},{2,1},{3,4},{4,3},{5,6},{6,5},{7,8},{8,7},{9,10},{10,... | collective-permute-start | bytes 36872 | tf_op jit(solution)/shard_map/ppermute | solution.py:729
  43.5 3.5 %collective-permute-start.13 = (f32[24,128]{1,0:T(8,128)S(1)}, f32[24,128]{1,0:T(8,128)S(1)}, u32[]{:S(2)}, u32[]{:S(2)}) collective-permute-start(f32[24,128]{1,0:T(8,128)S(1)} %get-tuple-element.80), channel_id=1, source_target_pairs={{0,224},{32,64},{64,32},{96,128},{128,96},{160,192},{192,160},{224... | collective-permute-start | bytes 36872 | tf_op jit(solution)/shard_map/ppermute | solution.py:729
  44.8 2.8 %collective-permute-start.14 = (f32[24,128]{1,0:T(8,128)S(1)}, f32[24,128]{1,0:T(8,128)S(1)}, u32[]{:S(2)}, u32[]{:S(2)}) collective-permute-start(f32[24,128]{1,0:T(8,128)S(1)} %get-tuple-element.81), channel_id=1, source_target_pairs={{0,1},{1,0},{2,3},{3,2},{4,5},{5,4},{6,7},{7,6},{8,9},{9,8},{10,11... | collective-permute-start | bytes 36872 | tf_op jit(solution)/shard_map/ppermute | solution.py:729
  44.8 2.8 %collective-permute-start.15 = (f32[24,128]{1,0:T(8,128)S(1)}, f32[24,128]{1,0:T(8,128)S(1)}, u32[]{:S(2)}, u32[]{:S(2)}) collective-permute-start(f32[24,128]{1,0:T(8,128)S(1)} %get-tuple-element.82), channel_id=1, source_target_pairs={{0,32},{32,0},{64,96},{96,64},{128,160},{160,128},{192,224},{224,1... | collective-permute-start | bytes 36872 | tf_op jit(solution)/shard_map/ppermute | solution.py:729
  48.7 5.9 %collective-permute-start.16 = (f32[12,128]{1,0:T(8,128)S(1)}, f32[12,128]{1,0:T(8,128)S(1)}, u32[]{:S(2)}, u32[]{:S(2)}) collective-permute-start(f32[12,128]{1,0:T(8,128)S(1)} %get-tuple-element.85), channel_id=1, source_target_pairs={{0,1},{1,2},{2,3},{3,4},{4,5},{5,6},{6,7},{7,8},{8,9},{9,10},{10,1... | collective-permute-start | bytes 18440 | tf_op jit(solution)/shard_map/ppermute | solution.py:735
  49.5 5.2 %collective-permute-start.17 = (f32[12,128]{1,0:T(8,128)S(1)}, f32[12,128]{1,0:T(8,128)S(1)}, u32[]{:S(2)}, u32[]{:S(2)}) collective-permute-start(f32[12,128]{1,0:T(8,128)S(1)} %get-tuple-element.86), channel_id=1, source_target_pairs={{0,32},{32,64},{64,96},{96,128},{128,160},{160,192},{192,224},{224... | collective-permute-start | bytes 18440 | tf_op jit(solution)/shard_map/ppermute | solution.py:735
  55.4 21.2 %all-to-all-start = ((f32[256,1,128]{2,1,0:T(1,128)}), f32[256,1,128]{2,1,0:T(1,128)S(1)}, u32[]{:S(2)}, u32[]{:S(2)}) async-start(f32[256,1,128]{2,1,0:T(1,128)} %bitcast.2), calls=%async_computation | async-start | bytes 262144 | tf_op jit(solution)/shard_map/all_to_all | solution.py:849
